TPU v7x, 32 devices: a whole 2x2x4 slice. The times are simulated.
32 devices in a mesh: tc: 16 (over z, y, x), pr: 2 (over core).
Axes of the slice: x: 2, y: 2, z: 4, core: 2. Of those that a mesh axis runs over, the one named last changes fastest.
Arguments:
- pivot_rhs: float32 [16, 1536, 64], P('tc', None, 'pr'), may hold values from -6 to 6
- pivot_inverse: bfloat16 [16, 1536, 1536], P('tc'), as said below
- pivot_owner: int32 [3], replicated, may hold values from 0 to 15, as said below
- coupling_left: bfloat16 [16, 2, 1536, 200], P('tc'), may hold values from -0.15625 to 0.15625
- coupling_right: bfloat16 [16, 2, 1536, 200], P('tc'), may hold values from -0.4375 to 0.4375
- coupling_ranks: int32 [16, 2], P('tc'), may hold values from 100 to 200, as said below
- future_left: bfloat16 [32, 3, 200, 1536], P('tc', None, None, 'pr'), may hold values from -0.15625 to 0.15625
- future_right: bfloat16 [32, 3, 200, 1536], P('tc', None, None, 'pr'), may hold values from -0.4375 to 0.4375
- future_ranks: int32 [32, 3], P('tc'), may hold values from 100 to 200, as said below
- future_rhs: float32 [32, 64, 1536], P('tc', None, 'pr'), may hold values from -6 to 6
Outputs:
- solved: bfloat16 [3, 1536, 64], P(None, None, 'pr')
- future_out: float32 [32, 64, 1536], P('tc', None, 'pr')
Inputs may be any that keep to these rules, and one draw needn't show every extreme that they name: `pivot_owner`: the 3 entries are distinct; entry p names the slot, and so the index of tc, that holds pivot p's tiles. `coupling_ranks`: entry [s, j] is the rank of the tile from the pivot in slot s to the pivot j + 1 places later. In every draw a tile that the window uses has rank exactly 200. `future_ranks`: in every draw one of these tiles has rank exactly 200. `pivot_inverse`: each tile is lower triangular.
All inputs are finite; a program needn't handle non-finite values.
Results may differ from a plain program's by a relative error of at most 0.007.
Values may be sent and summed in bfloat16 or wider, within the bound.
No kernel may reach another device: no remote copies, remote signals or barrier semaphores. Data moves between devices by JAX's collectives and lax.ppermute only.
A program may use at most 64 MiB of HBM per device.

v0:
```python
import jax
import jax.numpy as jnp
from jax import lax
from jax.sharding import PartitionSpec as P


def apply_weights(products, right_part, ranks_part):
    rank_ids = lax.broadcasted_iota(jnp.int32, products.shape, 3)
    weights = jnp.where(rank_ids < ranks_part[:, :, None, None], products, 0.0).astype(jnp.bfloat16)
    return jnp.einsum("fsqr,fsrb->fqb", weights, right_part, preferred_element_type=jnp.float32)


def local(
    pivot_rhs,
    pivot_inverse,
    pivot_owner,
    coupling_left,
    coupling_right,
    coupling_ranks,
    future_left,
    future_right,
    future_ranks,
    future_rhs,
):
    tile_count = pivot_owner.shape[0]
    rank_width = coupling_left.shape[3]
    device_index = lax.axis_index("tc")
    owned_flags = pivot_owner == device_index
    holds_pivot = jnp.any(owned_flags)
    own_pivot = jnp.sum(jnp.where(owned_flags, jnp.arange(tile_count, dtype=jnp.int32), 0))
    pending = pivot_rhs[0]
    inverse_tile = pivot_inverse[0]
    rank_ids = lax.broadcasted_iota(jnp.int32, (rank_width, 1), 0)
    solved = [None] * tile_count
    future_acc = future_rhs
    for current in reversed(range(tile_count)):
        pivot_in = pending.astype(jnp.bfloat16)
        local_solution = lax.dot_general(
            inverse_tile, pivot_in, (((0,), (0,)), ((), ())), preferred_element_type=jnp.float32
        ).astype(jnp.bfloat16)
        is_root = device_index == pivot_owner[current]
        masked_block = jnp.where(is_root, local_solution.astype(jnp.float32), 0.0)
        solved_block = lax.psum(masked_block, "tc").astype(jnp.bfloat16)
        solved[current] = solved_block
        if current > 0:
            distance = current - own_pivot - 1
            active = jnp.logical_and(holds_pivot, distance >= 0)
            slot_entry = jnp.clip(distance, 0, tile_count - 2)
            left_tile = lax.dynamic_index_in_dim(coupling_left[0], slot_entry, 0, keepdims=False)
            right_tile = lax.dynamic_index_in_dim(coupling_right[0], slot_entry, 0, keepdims=False)
            rank_limit = lax.dynamic_index_in_dim(coupling_ranks[0], slot_entry, 0, keepdims=False)
            factor = lax.dot_general(
                left_tile,
                solved_block,
                (((0,), (0,)), ((), ())),
                preferred_element_type=jnp.float32,
            )
            factor = jnp.where(rank_ids < rank_limit, factor, 0.0).astype(jnp.bfloat16)
            change = jnp.dot(right_tile, factor, preferred_element_type=jnp.float32)
            pending = pending - jnp.where(active, change, 0.0)
    stacked = jnp.stack(solved)
    columns = lax.all_to_all(stacked, "pr", split_axis=1, concat_axis=2, tiled=True)
    products = jnp.einsum(
        "sbq,fsrb->fsqr", columns, future_left, preferred_element_type=jnp.float32
    )
    products = lax.psum(products, "pr")
    future_acc = future_acc - apply_weights(products, future_right, future_ranks)
    return (stacked, future_acc)


def solution(mesh):
    return jax.shard_map(
        local,
        mesh=mesh,
        in_specs=(
            P("tc", None, "pr"),
            P("tc", None, None),
            P(),
            P("tc", None, None, None),
            P("tc", None, None, None),
            P("tc", None),
            P("tc", None, None, "pr"),
            P("tc", None, None, "pr"),
            P("tc", None),
            P("tc", None, "pr"),
        ),
        out_specs=(P(None, None, "pr"), P("tc", None, "pr")),
        check_vma=False,
    )
```

profile of v0, /device:TPU:0, one launch (start us, length us, event | category | flops | bytes accessed | tf_op | source)
XLA Modules:
  0.0 280.0 jit_solution(10352152036557066567)
XLA Ops:
  0.6 0.0 copy-start
  0.6 1.4 fusion.74
  3.4 1.3 compare_reduce_fusion
  4.7 1.4 fusion.78
  7.2 1.3 constant_dynamic-slice_fusion.1
  8.6 0.6 iota_compare_fusion.1
  9.1 0.6 iota_compare_fusion.2
  11.8 0.0 copy-start.1
  11.8 3.4 %fusion.15 = f32[1536,32]{0,1:T(8,128)S(1)} fusion(bf16[1,1536,1536]{2,1,0:T(8,128)(2,1)} %param.11, f32[1,1536,32]{1,2,0:T(8,128)} %param.10, pred[]{:T(512)S(6)} %eq.18), kind=kOutput, calls=%fused_computation.13 | convolution fusion | flops 151191552 | bytes 5111809 | tf_op jit(solution)/shard_map/dot_general | solution.py:38
  15.2 80.4 %all-reduce.4 = bf16[1536,32]{0,1:T(8,128)(2,1)S(1)} all-reduce(f32[1536,32]{0,1:T(8,128)S(1)} %fusion.15), channel_id=1, replica_groups=mesh['tc'=16,'pr'=2] {'tc'}, use_global_device_ids=true, to_apply=%region_2.3 | all-reduce | flops 49152 | bytes 294912 | tf_op jit(solution)/shard_map/psum | solution.py:43
  95.6 0.0 copy-done.1
  95.6 1.8 fusion.6
  97.4 3.9 %fusion.27 = f32[1536,32]{0,1:T(8,128)} fusion(bf16[1,1536,1536]{2,1,0:T(8,128)(2,1)} %param.11, f32[1536,32]{0,1:T(8,128)S(1)} %fusion.6, pred[]{:T(512)S(6)} %eq.19), kind=kOutput, calls=%fused_computation.17 | convolution fusion | flops 151191552 | bytes 5111809 | tf_op jit(solution)/shard_map/dot_general | solution.py:38
  101.3 73.9 %all-reduce.5 = bf16[1536,32]{0,1:T(8,128)(2,1)S(1)} all-reduce(f32[1536,32]{0,1:T(8,128)} %fusion.27), channel_id=1, replica_groups=mesh['tc'=16,'pr'=2] {'tc'}, use_global_device_ids=true, to_apply=%region_3.4 | all-reduce | flops 49152 | bytes 294912 | tf_op jit(solution)/shard_map/psum | solution.py:43
  175.2 2.4 fusion.8
  177.6 3.3 %fusion.39 = f32[1536,32]{0,1:T(8,128)S(1)} fusion(bf16[1536,32]{0,1:T(8,128)(2,1)} %fusion.8, bf16[1,1536,1536]{2,1,0:T(8,128)(2,1)} %param.11, pred[]{:T(512)S(6)} %eq.15), kind=kOutput, calls=%fused_computation.21 | convolution fusion | flops 151142400 | bytes 5013505 | tf_op jit(solution)/shard_map/dot_general | solution.py:38
  180.9 75.3 %all-reduce.6 = bf16[1536,32]{0,1:T(8,128)(2,1)S(1)} all-reduce(f32[1536,32]{0,1:T(8,128)S(1)} %fusion.39), channel_id=1, replica_groups=mesh['tc'=16,'pr'=2] {'tc'}, use_global_device_ids=true, to_apply=%region_4.5 | all-reduce | flops 49152 | bytes 294912 | tf_op jit(solution)/shard_map/psum | solution.py:43
  256.2 0.7 pad_maximum_fusion
  256.9 2.4 copy.14
  259.4 1.8 reshape.30
  261.2 5.8 %all_to_all.18 = bf16[2,2,36864]{2,1,0:T(2,128)(2,1)} all-to-all(bf16[2,2,36864]{2,1,0:T(2,128)(2,1)} %reshape.30), channel_id=1, replica_groups=mesh['tc'=16,'pr'=2] {'pr'}, dimensions={0} | all-to-all | bytes 589824 | tf_op jit(solution)/shard_map/all_to_all | solution.py:62
  267.0 2.0 reshape.31
  269.0 1.8 copy.18
  270.9 0.0 copy-start.2
  270.9 0.0 copy-start.3
  270.9 1.0 copy.16
  271.9 2.2 convolution_bitcast_fusion.1
  274.1 4.5 %all-reduce.7 = bf16[2,3,64,200]{3,2,1,0:T(8,128)(2,1)S(1)} all-reduce(f32[2,3,64,200]{3,2,1,0:T(8,128)S(1)} %convolution_bitcast_fusion.1), channel_id=1, replica_groups=mesh['tc'=16,'pr'=2] {'pr'}, use_global_device_ids=true, to_apply=%region_5.6 | all-reduce | flops 76800 | bytes 460800 | tf_op jit(solution)/shard_map/psum | solution.py:66
  278.6 0.0 copy-done
  278.6 0.0 copy-done.2
  278.6 0.0 copy-done.3
  278.6 1.3 fusion.42
Async XLA Ops:
  0.6 278.0 %copy-start = (bf16[2,3,200,768]{3,2,1,0:T(8,128)(2,1)S(1)}, bf16[2,3,200,768]{3,2,1,0:T(8,128)(2,1)}, u32[]{:S(2)}) copy-start(bf16[2,3,200,768]{3,2,1,0:T(8,128)(2,1)} %param.17) | copy-start | bytes 5529604
  11.8 83.8 %copy-start.1 = (bf16[1,2,1536,200]{2,3,1,0:T(8,128)(2,1)S(1)}, bf16[1,2,1536,200]{2,3,1,0:T(8,128)(2,1)}, u32[]{:S(2)}) copy-start(bf16[1,2,1536,200]{2,3,1,0:T(8,128)(2,1)} %param.13) | copy-start | bytes 3686404
  270.9 7.8 %copy-start.2 = (f32[2,64,768]{2,1,0:T(8,128)S(1)}, f32[2,64,768]{2,1,0:T(8,128)}, u32[]{:S(2)}) copy-start(f32[2,64,768]{2,1,0:T(8,128)} %param.19) | copy-start | bytes 1179652
  270.9 7.8 %copy-start.3 = (s32[2,3]{1,0:T(2,128)S(1)}, s32[2,3]{1,0:T(2,128)}, u32[]{:S(2)}) copy-start(s32[2,3]{1,0:T(2,128)} %param.18) | copy-start | bytes 76
where the time goes:
time: 281 us; the launch traced here: 280 us
  blocking collectives  240 us (85%)
  matrix products  18.3 us (7%)
  local copies, waits for them, and re-layouts  12 us (4%)
  between operations  5.19 us (2%)
  other arithmetic  4.67 us (2%)
    psum x3, blocking collectives, local(): solved_block = lax.psum(masked_block, 'tc').astype(jnp.bfloat16)  230 us
    dot_general x3, matrix products, local(): lax.dot_general(inverse_tile, pivot_in, (((0,), (0,)), ((), ())), preferr...  10.6 us
    all_to_all x1, blocking collectives, local(): lax.all_to_all(stacked, 'pr', split_axis=1, concat_axis=2, tiled=True)  5.8 us

commit v1 on v0

--- a/solution.py
+++ b/solution.py
@@ -1,7 +1,35 @@
+import functools
+
 import jax
 import jax.numpy as jnp
 from jax import lax
 from jax.sharding import PartitionSpec as P
+
+
+def doubling_orders(count, cores):
+    bits = [1 << place for place in range(count.bit_length() - 1)]
+    orders = []
+    for core in range(cores):
+        order = list(bits)
+        if core % 2:
+            for place in range(0, len(order) - 1, 2):
+                order[place], order[place + 1] = order[place + 1], order[place]
+        orders.append(order)
+    return orders
+
+
+def spread(block, slots, cores):
+    if slots & (slots - 1):
+        return lax.psum(block, "tc")
+    orders = doubling_orders(slots, cores)
+    for step in range(len(orders[0])):
+        pairs = [
+            (slot * cores + core, (slot ^ orders[core][step]) * cores + core)
+            for slot in range(slots)
+            for core in range(cores)
+        ]
+        block = block + lax.ppermute(block, ("tc", "pr"), pairs)
+    return block
 
 
 def apply_weights(products, right_part, ranks_part):
@@ -11,6 +39,8 @@
 
 
 def local(
+    slots,
+    cores,
     pivot_rhs,
     pivot_inverse,
     pivot_owner,
@@ -39,8 +69,8 @@
             inverse_tile, pivot_in, (((0,), (0,)), ((), ())), preferred_element_type=jnp.float32
         ).astype(jnp.bfloat16)
         is_root = device_index == pivot_owner[current]
-        masked_block = jnp.where(is_root, local_solution.astype(jnp.float32), 0.0)
-        solved_block = lax.psum(masked_block, "tc").astype(jnp.bfloat16)
+        masked_block = jnp.where(is_root, local_solution, jnp.zeros_like(local_solution))
+        solved_block = spread(masked_block, slots, cores)
         solved[current] = solved_block
         if current > 0:
             distance = current - own_pivot - 1
@@ -70,7 +100,7 @@
 
 def solution(mesh):
     return jax.shard_map(
-        local,
+        functools.partial(local, mesh.shape["tc"], mesh.shape["pr"]),
         mesh=mesh,
         in_specs=(
             P("tc", None, "pr"),

time: 281 us -> 104 us (0.37)
  blocking collectives: 240 us -> 10.3 us
  starting transfers between devices: 0 us -> 28.3 us
  waiting for transfers between devices: 0 us -> 24.9 us
    psum x3 -> x0, blocking collectives: 230 us -> none  [local(): solved_block = lax.psum(masked_block, 'tc').astype(jnp.bfloat16)]
    ppermute x0 -> x12, starting transfers between devices: none -> 28.3 us  [spread(): block = block + lax.ppermute(block, ('tc', 'pr'), pairs)]
    ppermute x0 -> x12, waiting for transfers between devices: none -> 24.9 us  [spread(): block = block + lax.ppermute(block, ('tc', 'pr'), pairs)]
  transfers between devices with their start and end apart: 0 -> 12, of which waited for: 0 -> 11; matrix products, arithmetic and copies ran while one was open for 0% -> 4% of each run, Pallas kernels for 0% -> 0%
where the time goes in v1:
time: 104 us; the launch traced here: 103 us
  starting transfers between devices  28.3 us (27%)
  waiting for transfers between devices  24.9 us (24%)
  matrix products  17.6 us (17%)
  local copies, waits for them, and re-layouts  11.2 us (11%)
  blocking collectives  10.3 us (10%)
  between operations  5.38 us (5%)
  other arithmetic  5.37 us (5%)
    ppermute x12, starting transfers between devices, spread(): block = block + lax.ppermute(block, ('tc', 'pr'), pairs)  28.3 us
    ppermute x12, waiting for transfers between devices, spread(): block = block + lax.ppermute(block, ('tc', 'pr'), pairs)  24.9 us
    dot_general x3, matrix products, local(): lax.dot_general(inverse_tile, pivot_in, (((0,), (0,)), ((), ())), preferr...  9.97 us
    all_to_all x1, blocking collectives, local(): lax.all_to_all(stacked, 'pr', split_axis=1, concat_axis=2, tiled=True)  5.82 us
    psum x1, blocking collectives, local(): products = lax.psum(products, 'pr')  4.5 us
    dot_general x2, matrix products, local(): change = jnp.dot(right_tile, factor, preferred_element_type=jnp.float32)  4.14 us
    unnamed x20, local copies, waits for them, and re-layouts  3.9 us
    all_to_all x2, local copies, waits for them, and re-layouts, local(): lax.all_to_all(stacked, 'pr', split_axis=1, concat_axis=2, tiled=True)  2.88 us
  transfers between devices with their start and end apart: 12, of which 11 were waited for; matrix products, arithmetic and copies ran while one was open for 4% of the time, Pallas kernels for 0%

profile of v1, /device:TPU:0, one launch (start us, length us, event | category | flops | bytes accessed | tf_op | source)
XLA Modules:
  0.0 103.2 jit_solution(2179977455496386081)
XLA Ops:
  0.6 0.0 copy-start
  0.6 1.4 %fusion.69 = (s32[1]{0:T(128)}, s32[1]{0:T(128)}, s32[1]{0:T(128)}) fusion(s32[3]{0:T(128)} %param.12), kind=kLoop, calls=%fused_computation.63 | loop fusion | bytes 24 | tf_op jit(solution)/shard_map/slice | solution.py:71
  2.7 3.4 %fusion.30 = bf16[1536,32]{0,1:T(8,128)(2,1)S(1)} fusion(bf16[1,1536,1536]{2,1,0:T(8,128)(2,1)} %param.11, f32[1,1536,32]{1,2,0:T(8,128)} %param.10, pred[]{:T(512)S(6)} %eq.18), kind=kOutput, calls=%fused_computation.18 | convolution fusion | flops 151142400 | bytes 5013505 | tf_op jit(solution)/shard_map/dot_general | solution.py:68
  6.2 3.0 %collective-permute-start = (bf16[1536,32]{0,1:T(8,128)(2,1)S(1)}, bf16[1536,32]{0,1:T(8,128)(2,1)S(1)}, u32[]{:S(2)}, u32[]{:S(2)}) collective-permute-start(bf16[1536,32]{0,1:T(8,128)(2,1)S(1)} %fusion.30), channel_id=1, source_target_pairs={{0,2},{1,5},{2,0},{3,7},{4,6},{5,1},{6,4},{7,3},{8,10},{9,13},{10,... | collective-permute-start | bytes 294920 | tf_op jit(solution)/shard_map/ppermute | solution.py:31
  9.2 2.6 %collective-permute-done = bf16[1536,32]{0,1:T(8,128)(2,1)S(1)} collective-permute-done((bf16[1536,32]{0,1:T(8,128)(2,1)S(1)}, bf16[1536,32]{0,1:T(8,128)(2,1)S(1)}, u32[]{:S(2)}, u32[]{:S(2)}) %collective-permute-start) | collective-permute-done | bytes 98336 | tf_op jit(solution)/shard_map/ppermute | solution.py:31
  11.8 2.1 %collective-permute-start.1 = (bf16[1536,32]{0,1:T(8,128)(2,1)S(1)}, bf16[1536,32]{0,1:T(8,128)(2,1)S(1)}, u32[]{:S(2)}, u32[]{:S(2)}) collective-permute-start(bf16[1536,32]{0,1:T(8,128)(2,1)S(1)} %add.50), channel_id=1, source_target_pairs={{0,4},{1,3},{2,6},{3,1},{4,0},{5,7},{6,2},{7,5},{8,12},{9,11},{10,... | collective-permute-start | bytes 294920 | tf_op jit(solution)/shard_map/ppermute | solution.py:31
  13.9 0.6 fusion.65
  16.6 2.1 %collective-permute-start.2 = (bf16[1536,32]{0,1:T(8,128)(2,1)S(1)}, bf16[1536,32]{0,1:T(8,128)(2,1)S(1)}, u32[]{:S(2)}, u32[]{:S(2)}) collective-permute-start(bf16[1536,32]{0,1:T(8,128)(2,1)S(1)} %add.51), channel_id=1, source_target_pairs={{0,8},{1,17},{2,10},{3,19},{4,12},{5,21},{6,14},{7,23},{8,0},{9,25... | collective-permute-start | bytes 294920 | tf_op jit(solution)/shard_map/ppermute | solution.py:31
  18.7 0.7 compare_reduce_fusion
  20.0 0.6 constant_dynamic-slice_fusion.1
  20.6 0.7 collective-permute-done.2
  21.3 3.1 %collective-permute-start.3 = (bf16[1536,32]{0,1:T(8,128)(2,1)S(1)}, bf16[1536,32]{0,1:T(8,128)(2,1)S(1)}, u32[]{:S(2)}, u32[]{:S(2)}) collective-permute-start(bf16[1536,32]{0,1:T(8,128)(2,1)S(1)} %add.52), channel_id=1, source_target_pairs={{0,16},{1,9},{2,18},{3,11},{4,20},{5,13},{6,22},{7,15},{8,24},{9,1... | collective-permute-start | bytes 294920 | tf_op jit(solution)/shard_map/ppermute | solution.py:31
  24.4 0.6 iota_compare_fusion.2
  25.1 1.9 %collective-permute-done.3 = bf16[1536,32]{0,1:T(8,128)(2,1)S(1)} collective-permute-done((bf16[1536,32]{0,1:T(8,128)(2,1)S(1)}, bf16[1536,32]{0,1:T(8,128)(2,1)S(1)}, u32[]{:S(2)}, u32[]{:S(2)}) %collective-permute-start.3) | collective-permute-done | bytes 98336 | tf_op jit(solution)/shard_map/ppermute | solution.py:31
  27.0 1.8 %fusion.6 = f32[1536,32]{0,1:T(8,128)S(1)} fusion(bf16[1,2,1536,200]{2,3,1,0:T(8,128)(2,1)S(1)} %copy-done.1, s32[]{:T(128)S(6)} %min.7, bf16[1,2,1536,200]{2,3,1,0:T(8,128)(2,1)} %param.14, f32[1,1536,32]{1,2,0:T(8,128)} %param.10, pred[]{:T(512)S(6)} %and.7, bf16[1536,32]{0,1:T(8,128)(2,1)S(1)} %add.52, bf16[1536,32]{0,1:T(8,128)(2,1)S(1)} %collective-permute-done.3, ...), kind=kOutput, calls=%fused_computation.8 | convolution fusion | flops 39481856 | bytes 1820672 | tf_op jit(solution)/shard_map/dot_general | solution.py:89
  28.8 3.2 %fusion.27 = bf16[1536,32]{0,1:T(8,128)(2,1)S(1)} fusion(bf16[1,1536,1536]{2,1,0:T(8,128)(2,1)} %param.11, f32[1536,32]{0,1:T(8,128)S(1)} %fusion.6, pred[]{:T(512)S(6)} %eq.19), kind=kOutput, calls=%fused_computation.17 | convolution fusion | flops 151142400 | bytes 5013505 | tf_op jit(solution)/shard_map/dot_general | solution.py:68
  32.0 0.0 copy-done.3
  32.1 1.9 %collective-permute-start.4 = (bf16[1536,32]{0,1:T(8,128)(2,1)S(1)}, bf16[1536,32]{0,1:T(8,128)(2,1)S(1)}, u32[]{:S(2)}, u32[]{:S(2)}) collective-permute-start(bf16[1536,32]{0,1:T(8,128)(2,1)S(1)} %fusion.27), channel_id=1, source_target_pairs={{0,2},{1,5},{2,0},{3,7},{4,6},{5,1},{6,4},{7,3},{8,10},{9,13},{10,... | collective-permute-start | bytes 294920 | tf_op jit(solution)/shard_map/ppermute | solution.py:31
  34.0 2.8 %collective-permute-done.4 = bf16[1536,32]{0,1:T(8,128)(2,1)S(1)} collective-permute-done((bf16[1536,32]{0,1:T(8,128)(2,1)S(1)}, bf16[1536,32]{0,1:T(8,128)(2,1)S(1)}, u32[]{:S(2)}, u32[]{:S(2)}) %collective-permute-start.4) | collective-permute-done | bytes 98336 | tf_op jit(solution)/shard_map/ppermute | solution.py:31
  36.8 1.9 %collective-permute-start.5 = (bf16[1536,32]{0,1:T(8,128)(2,1)S(1)}, bf16[1536,32]{0,1:T(8,128)(2,1)S(1)}, u32[]{:S(2)}, u32[]{:S(2)}) collective-permute-start(bf16[1536,32]{0,1:T(8,128)(2,1)S(1)} %add.54), channel_id=1, source_target_pairs={{0,4},{1,3},{2,6},{3,1},{4,0},{5,7},{6,2},{7,5},{8,12},{9,11},{10,... | collective-permute-start | bytes 294920 | tf_op jit(solution)/shard_map/ppermute | solution.py:31
  38.7 2.8 %collective-permute-done.5 = bf16[1536,32]{0,1:T(8,128)(2,1)S(1)} collective-permute-done((bf16[1536,32]{0,1:T(8,128)(2,1)S(1)}, bf16[1536,32]{0,1:T(8,128)(2,1)S(1)}, u32[]{:S(2)}, u32[]{:S(2)}) %collective-permute-start.5) | collective-permute-done | bytes 98336 | tf_op jit(solution)/shard_map/ppermute | solution.py:31
  41.5 2.1 %collective-permute-start.6 = (bf16[1536,32]{0,1:T(8,128)(2,1)S(1)}, bf16[1536,32]{0,1:T(8,128)(2,1)}, u32[]{:S(2)}, u32[]{:S(2)}) collective-permute-start(bf16[1536,32]{0,1:T(8,128)(2,1)S(1)} %add.55), channel_id=1, source_target_pairs={{0,8},{1,17},{2,10},{3,19},{4,12},{5,21},{6,14},{7,23},{8,0},{9,25... | collective-permute-start | bytes 294920 | tf_op jit(solution)/shard_map/ppermute | solution.py:31
  44.9 1.6 %collective-permute-done.6 = bf16[1536,32]{0,1:T(8,128)(2,1)} collective-permute-done((bf16[1536,32]{0,1:T(8,128)(2,1)S(1)}, bf16[1536,32]{0,1:T(8,128)(2,1)}, u32[]{:S(2)}, u32[]{:S(2)}) %collective-permute-start.6) | collective-permute-done | bytes 98336 | tf_op jit(solution)/shard_map/ppermute | solution.py:31
  46.5 1.0 add.56
  47.4 3.3 %collective-permute-start.7 = (bf16[1536,32]{0,1:T(8,128)(2,1)S(1)}, bf16[1536,32]{0,1:T(8,128)(2,1)}, u32[]{:S(2)}, u32[]{:S(2)}) collective-permute-start(bf16[1536,32]{0,1:T(8,128)(2,1)S(1)} %add.56), channel_id=1, source_target_pairs={{0,16},{1,9},{2,18},{3,11},{4,20},{5,13},{6,22},{7,15},{8,24},{9,1... | collective-permute-start | bytes 294920 | tf_op jit(solution)/shard_map/ppermute | solution.py:31
  50.7 0.6 iota_compare_fusion.1
  51.3 2.1 %collective-permute-done.7 = bf16[1536,32]{0,1:T(8,128)(2,1)} collective-permute-done((bf16[1536,32]{0,1:T(8,128)(2,1)S(1)}, bf16[1536,32]{0,1:T(8,128)(2,1)}, u32[]{:S(2)}, u32[]{:S(2)}) %collective-permute-start.7) | collective-permute-done | bytes 98336 | tf_op jit(solution)/shard_map/ppermute | solution.py:31
  53.4 2.4 %fusion.8 = bf16[1536,32]{0,1:T(8,128)(2,1)} fusion(f32[1536,32]{0,1:T(8,128)S(1)} %fusion.6, bf16[1,2,1536,200]{2,3,1,0:T(8,128)(2,1)S(1)} %copy-done.1, s32[]{:T(128)S(6)} %min.8, bf16[1,2,1536,200]{2,3,1,0:T(8,128)(2,1)} %param.14, pred[]{:T(512)S(6)} %and.8, bf16[1536,32]{0,1:T(8,128)(2,1)S(1)} %add.56, bf16[1536,32]{0,1:T(8,128)(2,1)} %collective-permute-done.7, ...), kind=kOutput, calls=%fused_computation.10 | convolution fusion | flops 39531008 | bytes 1722368 | tf_op jit(solution)/shard_map/dot_general | solution.py:89
  55.8 3.3 %fusion.21 = bf16[1536,32]{0,1:T(8,128)(2,1)S(1)} fusion(bf16[1536,32]{0,1:T(8,128)(2,1)} %fusion.8, bf16[1,1536,1536]{2,1,0:T(8,128)(2,1)} %param.11, pred[]{:T(512)S(6)} %eq.15), kind=kOutput, calls=%fused_computation.15 | convolution fusion | flops 151093248 | bytes 4915201 | tf_op jit(solution)/shard_map/dot_general | solution.py:68
  59.1 1.6 %collective-permute-start.8 = (bf16[1536,32]{0,1:T(8,128)(2,1)S(1)}, bf16[1536,32]{0,1:T(8,128)(2,1)S(1)}, u32[]{:S(2)}, u32[]{:S(2)}) collective-permute-start(bf16[1536,32]{0,1:T(8,128)(2,1)S(1)} %fusion.21), channel_id=1, source_target_pairs={{0,2},{1,5},{2,0},{3,7},{4,6},{5,1},{6,4},{7,3},{8,10},{9,13},{10,... | collective-permute-start | bytes 294920 | tf_op jit(solution)/shard_map/ppermute | solution.py:31
  60.7 3.1 %collective-permute-done.8 = bf16[1536,32]{0,1:T(8,128)(2,1)S(1)} collective-permute-done((bf16[1536,32]{0,1:T(8,128)(2,1)S(1)}, bf16[1536,32]{0,1:T(8,128)(2,1)S(1)}, u32[]{:S(2)}, u32[]{:S(2)}) %collective-permute-start.8) | collective-permute-done | bytes 98336 | tf_op jit(solution)/shard_map/ppermute | solution.py:31
  63.9 1.6 %collective-permute-start.9 = (bf16[1536,32]{0,1:T(8,128)(2,1)S(1)}, bf16[1536,32]{0,1:T(8,128)(2,1)S(1)}, u32[]{:S(2)}, u32[]{:S(2)}) collective-permute-start(bf16[1536,32]{0,1:T(8,128)(2,1)S(1)} %add.58), channel_id=1, source_target_pairs={{0,4},{1,3},{2,6},{3,1},{4,0},{5,7},{6,2},{7,5},{8,12},{9,11},{10,... | collective-permute-start | bytes 294920 | tf_op jit(solution)/shard_map/ppermute | solution.py:31
  65.4 3.1 %collective-permute-done.9 = bf16[1536,32]{0,1:T(8,128)(2,1)S(1)} collective-permute-done((bf16[1536,32]{0,1:T(8,128)(2,1)S(1)}, bf16[1536,32]{0,1:T(8,128)(2,1)S(1)}, u32[]{:S(2)}, u32[]{:S(2)}) %collective-permute-start.9) | collective-permute-done | bytes 98336 | tf_op jit(solution)/shard_map/ppermute | solution.py:31
  68.6 2.1 %collective-permute-start.10 = (bf16[1536,32]{0,1:T(8,128)(2,1)S(1)}, bf16[1536,32]{0,1:T(8,128)(2,1)S(1)}, u32[]{:S(2)}, u32[]{:S(2)}) collective-permute-start(bf16[1536,32]{0,1:T(8,128)(2,1)S(1)} %add.59), channel_id=1, source_target_pairs={{0,8},{1,17},{2,10},{3,19},{4,12},{5,21},{6,14},{7,23},{8,0},{9,25... | collective-permute-start | bytes 294920 | tf_op jit(solution)/shard_map/ppermute | solution.py:31
  70.7 2.6 %collective-permute-done.10 = bf16[1536,32]{0,1:T(8,128)(2,1)S(1)} collective-permute-done((bf16[1536,32]{0,1:T(8,128)(2,1)S(1)}, bf16[1536,32]{0,1:T(8,128)(2,1)S(1)}, u32[]{:S(2)}, u32[]{:S(2)}) %collective-permute-start.10) | collective-permute-done | bytes 98336 | tf_op jit(solution)/shard_map/ppermute | solution.py:31
  73.3 3.5 %collective-permute-start.11 = (bf16[1536,32]{0,1:T(8,128)(2,1)S(1)}, bf16[1536,32]{0,1:T(8,128)(2,1)S(1)}, u32[]{:S(2)}, u32[]{:S(2)}) collective-permute-start(bf16[1536,32]{0,1:T(8,128)(2,1)S(1)} %add.60), channel_id=1, source_target_pairs={{0,16},{1,9},{2,18},{3,11},{4,20},{5,13},{6,22},{7,15},{8,24},{9,1... | collective-permute-start | bytes 294920 | tf_op jit(solution)/shard_map/ppermute | solution.py:31
  76.8 0.9 add_bitcast_fusion.1
  77.7 1.7 %collective-permute-done.11 = bf16[1536,32]{0,1:T(8,128)(2,1)S(1)} collective-permute-done((bf16[1536,32]{0,1:T(8,128)(2,1)S(1)}, bf16[1536,32]{0,1:T(8,128)(2,1)S(1)}, u32[]{:S(2)}, u32[]{:S(2)}) %collective-permute-start.11) | collective-permute-done | bytes 98336 | tf_op jit(solution)/shard_map/ppermute | solution.py:31
  79.4 0.7 pad_maximum_fusion
  80.1 2.4 %copy.14 = bf16[3,1536,32]{2,0,1:T(4,128)(2,1)S(1)} copy(bf16[3,1536,32]{1,2,0:T(8,128)(2,1)} %pad_maximum_fusion) | data formatting | bytes 589824 | tf_op jit(solution)/shard_map/stack | solution.py:91
  82.6 1.8 %reshape.30 = bf16[2,2,36864]{2,1,0:T(2,128)(2,1)} reshape(bf16[1536,3,32]{2,1,0:T(4,128)(2,1)S(1)} %bitcast.76) | data formatting | bytes 589824
  84.4 5.8 %all_to_all.18 = bf16[2,2,36864]{2,1,0:T(2,128)(2,1)} all-to-all(bf16[2,2,36864]{2,1,0:T(2,128)(2,1)} %reshape.30), channel_id=1, replica_groups=mesh['tc'=16,'pr'=2] {'pr'}, dimensions={0} | all-to-all | bytes 589824 | tf_op jit(solution)/shard_map/all_to_all | solution.py:92
  90.2 2.0 %reshape.31 = bf16[1536,3,32]{2,1,0:T(4,128)(2,1)S(1)} reshape(bf16[2,2,36864]{2,1,0:T(2,128)(2,1)} %all_to_all.18) | data formatting | bytes 589824
  92.2 1.8 %copy.18 = bf16[3,2,768,32]{2,1,3,0:T(2,128)(2,1)} copy(bf16[3,2,768,32]{3,0,2,1:T(4,128)(2,1)S(1)} %bitcast.75) | data formatting | bytes 589824 | tf_op jit(solution)/shard_map/all_to_all | solution.py:92
  94.1 1.0 %copy.16 = bf16[3,768,2,32]{1,3,2,0:T(8,128)(2,1)S(1)} copy(bf16[3,768,2,32]{1,2,3,0:T(2,128)(2,1)} %bitcast.78) | data formatting | bytes 589824 | tf_op jit(solution)/shard_map/all_to_all | solution.py:92
  95.1 2.2 %convolution_bitcast_fusion.1 = f32[2,3,64,200]{3,2,1,0:T(8,128)S(1)} fusion(bf16[3,768,64,1]{1,2,0,3:T(8,128)(2,1)S(1)} %bitcast.77, bf16[2,3,200,768]{3,2,1,0:T(8,128)(2,1)} %param.16), kind=kOutput, calls=%fused_computation.20 | convolution fusion | flops 117964800 | bytes 2445312 | tf_op jit(solution)/shard_map/sbq,fsrb->fsqr/dot_general | solution.py:93
  97.3 4.5 %all-reduce.1 = bf16[2,3,64,200]{3,2,1,0:T(8,128)(2,1)S(1)} all-reduce(f32[2,3,64,200]{3,2,1,0:T(8,128)S(1)} %convolution_bitcast_fusion.1), channel_id=1, replica_groups=mesh['tc'=16,'pr'=2] {'pr'}, use_global_device_ids=true, to_apply=%region_2.3 | all-reduce | flops 76800 | bytes 460800 | tf_op jit(solution)/shard_map/psum | solution.py:96
  101.8 1.3 %fusion.33 = f32[2,64,768]{2,1,0:T(8,128)} fusion(f32[2,64,768]{2,1,0:T(8,128)S(1)} %copy-done.2, bf16[2,3,200,768]{3,2,1,0:T(8,128)(2,1)S(1)} %copy-done, bf16[2,3,64,200]{3,2,1,0:T(8,128)(2,1)S(1)} %all-reduce.1, s32[2,3]{1,0:T(2,128)S(1)} %copy-done.7), kind=kOutput, calls=%fused_computation.21 | convolution fusion | flops 118216704 | bytes 2783256 | tf_op jit(solution)/shard_map/fsqr,fsrb->fqb/dot_general | solution.py:38
  (27 shorter events, 0.3 us)
Async XLA Ops:
  0.6 101.2 %copy-start = (bf16[2,3,200,768]{3,2,1,0:T(8,128)(2,1)S(1)}, bf16[2,3,200,768]{3,2,1,0:T(8,128)(2,1)}, u32[]{:S(2)}) copy-start(bf16[2,3,200,768]{3,2,1,0:T(8,128)(2,1)} %param.17) | copy-start | bytes 5529604
  2.7 11.2 %copy-start.6 = (s32[3]{0:T(128)S(1)}, s32[3]{0:T(128)}, u32[]{:S(2)}) copy-start(s32[3]{0:T(128)} %param.12) | copy-start | bytes 40
  2.7 17.3 %copy-start.8 = (s32[1,2]{1,0:T(1,128)S(1)}, s32[1,2]{1,0:T(1,128)}, u32[]{:S(2)}) copy-start(s32[1,2]{1,0:T(1,128)} %param.15) | copy-start | bytes 28
  2.7 24.3 %copy-start.1 = (bf16[1,2,1536,200]{2,3,1,0:T(8,128)(2,1)S(1)}, bf16[1,2,1536,200]{2,3,1,0:T(8,128)(2,1)}, u32[]{:S(2)}) copy-start(bf16[1,2,1536,200]{2,3,1,0:T(8,128)(2,1)} %param.13) | copy-start | bytes 3686404
  6.2 5.6 %collective-permute-start = (bf16[1536,32]{0,1:T(8,128)(2,1)S(1)}, bf16[1536,32]{0,1:T(8,128)(2,1)S(1)}, u32[]{:S(2)}, u32[]{:S(2)}) collective-permute-start(bf16[1536,32]{0,1:T(8,128)(2,1)S(1)} %fusion.30), channel_id=1, source_target_pairs={{0,2},{1,5},{2,0},{3,7},{4,6},{5,1},{6,4},{7,3},{8,10},{9,13},{10,... | collective-permute-start | bytes 294920 | tf_op jit(solution)/shard_map/ppermute | solution.py:31
  11.8 4.7 %collective-permute-start.1 = (bf16[1536,32]{0,1:T(8,128)(2,1)S(1)}, bf16[1536,32]{0,1:T(8,128)(2,1)S(1)}, u32[]{:S(2)}, u32[]{:S(2)}) collective-permute-start(bf16[1536,32]{0,1:T(8,128)(2,1)S(1)} %add.50), channel_id=1, source_target_pairs={{0,4},{1,3},{2,6},{3,1},{4,0},{5,7},{6,2},{7,5},{8,12},{9,11},{10,... | collective-permute-start | bytes 294920 | tf_op jit(solution)/shard_map/ppermute | solution.py:31
  16.6 4.7 %collective-permute-start.2 = (bf16[1536,32]{0,1:T(8,128)(2,1)S(1)}, bf16[1536,32]{0,1:T(8,128)(2,1)S(1)}, u32[]{:S(2)}, u32[]{:S(2)}) collective-permute-start(bf16[1536,32]{0,1:T(8,128)(2,1)S(1)} %add.51), channel_id=1, source_target_pairs={{0,8},{1,17},{2,10},{3,19},{4,12},{5,21},{6,14},{7,23},{8,0},{9,25... | collective-permute-start | bytes 294920 | tf_op jit(solution)/shard_map/ppermute | solution.py:31
  21.3 5.7 %collective-permute-start.3 = (bf16[1536,32]{0,1:T(8,128)(2,1)S(1)}, bf16[1536,32]{0,1:T(8,128)(2,1)S(1)}, u32[]{:S(2)}, u32[]{:S(2)}) collective-permute-start(bf16[1536,32]{0,1:T(8,128)(2,1)S(1)} %add.52), channel_id=1, source_target_pairs={{0,16},{1,9},{2,18},{3,11},{4,20},{5,13},{6,22},{7,15},{8,24},{9,1... | collective-permute-start | bytes 294920 | tf_op jit(solution)/shard_map/ppermute | solution.py:31
  27.0 5.0 %copy-start.3 = (bf16[1536,32]{0,1:T(8,128)(2,1)}, bf16[1536,32]{0,1:T(8,128)(2,1)S(1)}, u32[]{:S(2)}) copy-start(bf16[1536,32]{0,1:T(8,128)(2,1)S(1)} %collective-permute-done.3) | copy-start | bytes 294916
  32.1 4.7 %collective-permute-start.4 = (bf16[1536,32]{0,1:T(8,128)(2,1)S(1)}, bf16[1536,32]{0,1:T(8,128)(2,1)S(1)}, u32[]{:S(2)}, u32[]{:S(2)}) collective-permute-start(bf16[1536,32]{0,1:T(8,128)(2,1)S(1)} %fusion.27), channel_id=1, source_target_pairs={{0,2},{1,5},{2,0},{3,7},{4,6},{5,1},{6,4},{7,3},{8,10},{9,13},{10,... | collective-permute-start | bytes 294920 | tf_op jit(solution)/shard_map/ppermute | solution.py:31
  36.8 4.7 %collective-permute-start.5 = (bf16[1536,32]{0,1:T(8,128)(2,1)S(1)}, bf16[1536,32]{0,1:T(8,128)(2,1)S(1)}, u32[]{:S(2)}, u32[]{:S(2)}) collective-permute-start(bf16[1536,32]{0,1:T(8,128)(2,1)S(1)} %add.54), channel_id=1, source_target_pairs={{0,4},{1,3},{2,6},{3,1},{4,0},{5,7},{6,2},{7,5},{8,12},{9,11},{10,... | collective-permute-start | bytes 294920 | tf_op jit(solution)/shard_map/ppermute | solution.py:31
  41.5 3.4 %copy-start.5 = (bf16[1536,32]{0,1:T(8,128)(2,1)}, bf16[1536,32]{0,1:T(8,128)(2,1)S(1)}, u32[]{:S(2)}) copy-start(bf16[1536,32]{0,1:T(8,128)(2,1)S(1)} %add.55) | copy-start | bytes 294916
  41.5 4.9 %collective-permute-start.6 = (bf16[1536,32]{0,1:T(8,128)(2,1)S(1)}, bf16[1536,32]{0,1:T(8,128)(2,1)}, u32[]{:S(2)}, u32[]{:S(2)}) collective-permute-start(bf16[1536,32]{0,1:T(8,128)(2,1)S(1)} %add.55), channel_id=1, source_target_pairs={{0,8},{1,17},{2,10},{3,19},{4,12},{5,21},{6,14},{7,23},{8,0},{9,25... | collective-permute-start | bytes 294920 | tf_op jit(solution)/shard_map/ppermute | solution.py:31
  47.4 6.0 %collective-permute-start.7 = (bf16[1536,32]{0,1:T(8,128)(2,1)S(1)}, bf16[1536,32]{0,1:T(8,128)(2,1)}, u32[]{:S(2)}, u32[]{:S(2)}) collective-permute-start(bf16[1536,32]{0,1:T(8,128)(2,1)S(1)} %add.56), channel_id=1, source_target_pairs={{0,16},{1,9},{2,18},{3,11},{4,20},{5,13},{6,22},{7,15},{8,24},{9,1... | collective-permute-start | bytes 294920 | tf_op jit(solution)/shard_map/ppermute | solution.py:31
  55.8 14.9 %copy-start.4 = (bf16[1536,32]{0,1:T(8,128)(2,1)S(1)}, bf16[1536,32]{0,1:T(8,128)(2,1)}, u32[]{:S(2)}) copy-start(bf16[1536,32]{0,1:T(8,128)(2,1)} %copy-done.3) | copy-start | bytes 294916
  59.1 4.7 %collective-permute-start.8 = (bf16[1536,32]{0,1:T(8,128)(2,1)S(1)}, bf16[1536,32]{0,1:T(8,128)(2,1)S(1)}, u32[]{:S(2)}, u32[]{:S(2)}) collective-permute-start(bf16[1536,32]{0,1:T(8,128)(2,1)S(1)} %fusion.21), channel_id=1, source_target_pairs={{0,2},{1,5},{2,0},{3,7},{4,6},{5,1},{6,4},{7,3},{8,10},{9,13},{10,... | collective-permute-start | bytes 294920 | tf_op jit(solution)/shard_map/ppermute | solution.py:31
  63.9 4.7 %collective-permute-start.9 = (bf16[1536,32]{0,1:T(8,128)(2,1)S(1)}, bf16[1536,32]{0,1:T(8,128)(2,1)S(1)}, u32[]{:S(2)}, u32[]{:S(2)}) collective-permute-start(bf16[1536,32]{0,1:T(8,128)(2,1)S(1)} %add.58), channel_id=1, source_target_pairs={{0,4},{1,3},{2,6},{3,1},{4,0},{5,7},{6,2},{7,5},{8,12},{9,11},{10,... | collective-permute-start | bytes 294920 | tf_op jit(solution)/shard_map/ppermute | solution.py:31
  68.6 4.7 %collective-permute-start.10 = (bf16[1536,32]{0,1:T(8,128)(2,1)S(1)}, bf16[1536,32]{0,1:T(8,128)(2,1)S(1)}, u32[]{:S(2)}, u32[]{:S(2)}) collective-permute-start(bf16[1536,32]{0,1:T(8,128)(2,1)S(1)} %add.59), channel_id=1, source_target_pairs={{0,8},{1,17},{2,10},{3,19},{4,12},{5,21},{6,14},{7,23},{8,0},{9,25... | collective-permute-start | bytes 294920 | tf_op jit(solution)/shard_map/ppermute | solution.py:31
  73.3 6.1 %collective-permute-start.11 = (bf16[1536,32]{0,1:T(8,128)(2,1)S(1)}, bf16[1536,32]{0,1:T(8,128)(2,1)S(1)}, u32[]{:S(2)}, u32[]{:S(2)}) collective-permute-start(bf16[1536,32]{0,1:T(8,128)(2,1)S(1)} %add.60), channel_id=1, source_target_pairs={{0,16},{1,9},{2,18},{3,11},{4,20},{5,13},{6,22},{7,15},{8,24},{9,1... | collective-permute-start | bytes 294920 | tf_op jit(solution)/shard_map/ppermute | solution.py:31
  94.1 7.8 %copy-start.2 = (f32[2,64,768]{2,1,0:T(8,128)S(1)}, f32[2,64,768]{2,1,0:T(8,128)}, u32[]{:S(2)}) copy-start(f32[2,64,768]{2,1,0:T(8,128)} %param.19) | copy-start | bytes 1179652
  94.1 7.8 %copy-start.7 = (s32[2,3]{1,0:T(2,128)S(1)}, s32[2,3]{1,0:T(2,128)}, u32[]{:S(2)}) copy-start(s32[2,3]{1,0:T(2,128)} %param.18) | copy-start | bytes 76

commit v2 on v1

v2 whole, which is shorter than its diff:
```python
import functools

import jax
import jax.numpy as jnp
from jax import lax
from jax.experimental import pallas as pl
from jax.experimental.pallas import tpu as pltpu
from jax.sharding import PartitionSpec as P

SMEM = pl.BlockSpec(memory_space=pltpu.SMEM)
VMEM = pl.BlockSpec(memory_space=pltpu.VMEM)
ANY = pl.BlockSpec(memory_space=pl.ANY)
MIB = 1 << 20


def doubling_orders(count, cores):
    bits = [1 << place for place in range(count.bit_length() - 1)]
    orders = []
    for core in range(cores):
        order = list(bits)
        if core % 2:
            for place in range(0, len(order) - 1, 2):
                order[place], order[place + 1] = order[place + 1], order[place]
        orders.append(order)
    return orders


def spread(block, slots, cores):
    if slots & (slots - 1):
        return lax.psum(block, "tc")
    orders = doubling_orders(slots, cores)
    for step in range(len(orders[0])):
        pairs = [
            (slot * cores + core, (slot ^ orders[core][step]) * cores + core)
            for slot in range(slots)
            for core in range(cores)
        ]
        block = block + lax.ppermute(block, ("tc", "pr"), pairs)
    return block


def swap(block, cores):
    return lax.ppermute(block, "pr", [(core, cores - 1 - core) for core in range(cores)])


def block_width(size):
    return 256 if size % 256 == 0 else size


def start_triangle(inverse_ref, buffer, sems):
    size = inverse_ref.shape[0]
    width = block_width(size)
    copies = []
    for place in range(size // width):
        first = place * width
        part = (pl.ds(first, size - first), pl.ds(first, width))
        copies.append(pltpu.make_async_copy(inverse_ref.at[part], buffer.at[part], sems.at[place]))
    for copy in copies:
        copy.start()
    return copies, width


def first_kernel(owner_ref, rhs_ref, inverse_ref, raw_ref, block_ref, buffer, sems):
    copies, width = start_triangle(inverse_ref, buffer, sems)
    is_root = owner_ref[owner_ref.shape[0] - 1] == lax.axis_index("tc")
    pivot_in = rhs_ref[...].astype(jnp.bfloat16)
    for place, copy in enumerate(copies):
        first = place * width
        copy.wait()
        raw = jnp.dot(
            pivot_in[:, first:], buffer[first:, first : first + width], preferred_element_type=jnp.float32
        )
        raw_ref[:, first : first + width] = raw
        block_ref[:, first : first + width] = jnp.where(is_root, raw, 0.0).astype(jnp.bfloat16)


def ahead_kernel(right_ref, inverse_ref, ahead_ref, buffer, sems):
    copies, width = start_triangle(inverse_ref, buffer, sems)
    for place, copy in enumerate(copies):
        first = place * width
        copy.wait()
        for entry in range(right_ref.shape[0]):
            ahead_ref[entry, :, first : first + width] = jnp.dot(
                right_ref[entry, :, first:],
                buffer[first:, first : first + width],
                preferred_element_type=jnp.float32,
            ).astype(jnp.bfloat16)


def step_kernel(current, owner_ref, ranks_ref, solved_ref, left_ref, ahead_ref, raw_ref, new_raw_ref, block_ref):
    me = lax.axis_index("tc")
    own = jnp.int32(current)
    for place in range(owner_ref.shape[0]):
        own = jnp.where(owner_ref[place] == me, jnp.int32(place), own)
    active = own < current
    entry = jnp.clip(current - own - 1, 0, left_ref.shape[0] - 1)
    limit = jnp.where(active, ranks_ref[0, entry], 0)
    factor = lax.dot_general(
        solved_ref[...], left_ref[entry], (((1,), (1,)), ((), ())), preferred_element_type=jnp.float32
    )
    rank_ids = lax.broadcasted_iota(jnp.int32, factor.shape, 1)
    factor = jnp.where(rank_ids < limit, factor, 0.0).astype(jnp.bfloat16)
    raw = raw_ref[...] - jnp.dot(factor, ahead_ref[entry], preferred_element_type=jnp.float32)
    new_raw_ref[...] = raw
    is_root = owner_ref[current - 1] == me
    block_ref[...] = jnp.where(is_root, raw, 0.0).astype(jnp.bfloat16)


def weights_kernel(pivots, ranks_ref, *refs):
    solved_refs, (own_ref, other_ref, weights_ref) = refs[: len(pivots)], refs[len(pivots) :]
    core = lax.axis_index("pr")
    half = own_ref.shape[3]
    own_rows = pl.ds(pl.multiple_of(core * half, half), half)
    other_rows = pl.ds(pl.multiple_of((1 - core) * half, half), half)
    dims = (((1,), (1,)), ((), ()))
    for place, pivot in enumerate(pivots):
        own_part, other_part = solved_refs[place][:, own_rows], solved_refs[place][:, other_rows]
        for row in range(own_ref.shape[0]):
            products = lax.dot_general(
                own_part, own_ref[row, pivot], dims, preferred_element_type=jnp.float32
            ) + lax.dot_general(other_part, other_ref[row, pivot], dims, preferred_element_type=jnp.float32)
            rank_ids = lax.broadcasted_iota(jnp.int32, products.shape, 1)
            weights_ref[row, place] = jnp.where(rank_ids < ranks_ref[row, pivot], products, 0.0).astype(
                jnp.bfloat16
            )


def update_kernel(pivots, own_ref, other_ref, right_ref, rhs_ref, out_ref):
    core = lax.axis_index("pr")
    probes = own_ref.shape[2]
    for row in range(rhs_ref.shape[0]):
        for ref, slot in ((own_ref, core), (other_ref, 1 - core)):
            rows = pl.ds(pl.multiple_of(slot * probes, probes), probes)
            total = rhs_ref[row, rows, :]
            for place, pivot in enumerate(pivots):
                total = total - jnp.dot(
                    ref[row, place], right_ref[row, pivot], preferred_element_type=jnp.float32
                )
            out_ref[row, rows, :] = total


def call(kernel, shapes, specs, scratch=(), flops=0, read=0, limit=16):
    return pl.pallas_call(
        kernel,
        out_shape=shapes,
        in_specs=specs,
        out_specs=[VMEM] * len(shapes),
        scratch_shapes=list(scratch),
        compiler_params=pltpu.CompilerParams(vmem_limit_bytes=limit * MIB),
        cost_estimate=pl.CostEstimate(flops=flops, bytes_accessed=read, transcendentals=0),
    )


def local(
    slots,
    cores,
    pivot_rhs,
    pivot_inverse,
    pivot_owner,
    coupling_left,
    coupling_right,
    coupling_ranks,
    future_left,
    future_right,
    future_ranks,
    future_rhs,
):
    count = pivot_owner.shape[0]
    size, probes = pivot_rhs.shape[1:]
    rank = coupling_left.shape[3]
    entries = coupling_left.shape[1]
    rows = future_left.shape[0]
    blocks = size // block_width(size)
    inverse = pivot_inverse[0]
    rhs = jnp.swapaxes(pivot_rhs[0], 0, 1)
    left = jnp.swapaxes(coupling_left[0], 1, 2)
    right = jnp.swapaxes(coupling_right[0], 1, 2)
    triangle = [pltpu.VMEM((size, size), jnp.bfloat16), pltpu.SemaphoreType.DMA((blocks,))]
    wide = jax.ShapeDtypeStruct((probes, size), jnp.float32)
    narrow = jax.ShapeDtypeStruct((probes, size), jnp.bfloat16)

    raw, block = call(
        first_kernel, [wide, narrow], [SMEM, VMEM, ANY], triangle, probes * size * size, size * size
    )(pivot_owner, rhs, inverse)
    (ahead,) = call(
        ahead_kernel,
        [jax.ShapeDtypeStruct((entries, rank, size), jnp.bfloat16)],
        [VMEM, ANY],
        triangle,
        entries * rank * size * size,
        size * size + 4 * entries * rank * size,
    )(right, inverse)
    other_left = swap(future_left, cores)

    solved = [None] * count
    for current in reversed(range(count)):
        solved[current] = spread(block, slots, cores)
        if current > 0:
            raw, block = call(
                functools.partial(step_kernel, current),
                [wide, narrow],
                [SMEM, SMEM] + [VMEM] * 4,
                (),
                4 * probes * rank * size,
                4 * rank * size,
            )(pivot_owner, coupling_ranks, solved[current], left, ahead, raw)

    total = future_rhs
    for pivots in (tuple(range(count - 1, 0, -1)), (0,)):
        (weights,) = call(
            functools.partial(weights_kernel, pivots),
            [jax.ShapeDtypeStruct((rows, len(pivots), probes, rank), jnp.bfloat16)],
            [SMEM] + [VMEM] * (len(pivots) + 2),
            (),
            2 * rows * len(pivots) * probes * rank * size,
            2 * rows * len(pivots) * rank * size,
        )(future_ranks, *[solved[pivot] for pivot in pivots], future_left, other_left)
        (total,) = call(
            functools.partial(update_kernel, pivots),
            [jax.ShapeDtypeStruct(total.shape, jnp.float32)],
            [VMEM] * 4,
            (),
            2 * rows * len(pivots) * probes * rank * size,
            rows * len(pivots) * rank * size + 2 * 4 * total.size,
        )(weights, swap(weights, cores), future_right, total)
    return jnp.swapaxes(jnp.stack(solved), 1, 2), total


def solution(mesh):
    return jax.shard_map(
        functools.partial(local, mesh.shape["tc"], mesh.shape["pr"]),
        mesh=mesh,
        in_specs=(
            P("tc", None, "pr"),
            P("tc", None, None),
            P(),
            P("tc", None, None, None),
            P("tc", None, None, None),
            P("tc", None),
            P("tc", None, None, "pr"),
            P("tc", None, None, "pr"),
            P("tc", None),
            P("tc", None, "pr"),
        ),
        out_specs=(P(None, None, "pr"), P("tc", None, "pr")),
        check_vma=False,
    )
```

time: 104 us -> 80.6 us (0.77)
  matrix products: 17.6 us -> 0 us
  waiting for transfers between devices: 24.9 us -> 41.3 us
  Pallas kernels: 0 us -> 11.8 us
  blocking collectives: 10.3 us -> 0 us
  starting transfers between devices: 28.3 us -> 20.1 us
  local copies, waits for them, and re-layouts: 11.2 us -> 5.25 us
  between operations: 5.38 us -> 0.86 us
  other arithmetic: 5.37 us -> 1.06 us
    dot_general x7 -> x0, matrix products: 17.6 us -> none  [the longest x3 9.97 us: local(): lax.dot_general(inverse_tile, pivot_in, (((0,), (0,)), ((), ())), preferr...]
    ppermute x12, waiting for transfers between devices: 24.9 us -> 41.1 us  [spread(): block = block + lax.ppermute(block, ('tc', 'pr'), pairs)]
    pallas_call x0 -> x8, Pallas kernels: none -> 11.8 us  [the longest x2 3.09 us: local(): call(functools.partial(step_kernel, current), [wide, narrow], [SMEM, SMEM...]
    ppermute x12, starting transfers between devices: 28.3 us -> 18.9 us  [spread(): block = block + lax.ppermute(block, ('tc', 'pr'), pairs)]
    all_to_all x1 -> x0, blocking collectives: 5.82 us -> none  [local(): lax.all_to_all(stacked, 'pr', split_axis=1, concat_axis=2, tiled=True)]
    psum x1 -> x0, blocking collectives: 4.5 us -> none  [local(): products = lax.psum(products, 'pr')]
    all_to_all x2 -> x0, local copies, waits for them, and re-layouts: 2.88 us -> none  [local(): lax.all_to_all(stacked, 'pr', split_axis=1, concat_axis=2, tiled=True)]
    another operation x1 -> x0, local copies, waits for them, and re-layouts: 2.43 us -> none  [local(): stacked = jnp.stack(solved)]
  transfers between devices with their start and end apart: 12 -> 15, of which waited for: 11 -> 12; matrix products, arithmetic and copies ran while one was open for 4% -> 1% of each run, Pallas kernels for 0% -> 12%
where the time goes in v2:
time: 80.6 us; the launch traced here: 80.4 us
  waiting for transfers between devices  41.3 us (51%)
  starting transfers between devices  20.1 us (25%)
  Pallas kernels  11.8 us (15%)
  local copies, waits for them, and re-layouts  5.25 us (7%)
  other arithmetic  1.06 us (1%)
  between operations  0.86 us (1%)
    ppermute x12, waiting for transfers between devices, spread(): block = block + lax.ppermute(block, ('tc', 'pr'), pairs)  41.1 us
    ppermute x12, starting transfers between devices, spread(): block = block + lax.ppermute(block, ('tc', 'pr'), pairs)  18.9 us
    unnamed x24, local copies, waits for them, and re-layouts  5.25 us
    pallas_call x2, Pallas kernels, local(): call(functools.partial(step_kernel, current), [wide, narrow], [SMEM, SMEM...  3.09 us
    pallas_call x2, Pallas kernels, local(): call(functools.partial(weights_kernel, pivots), [jax.ShapeDtypeStruct((ro...  2.43 us
    pallas_call x1, Pallas kernels, local(): call(ahead_kernel, [jax.ShapeDtypeStruct((entries, rank, size), jnp.bfloa...  2.43 us
    pallas_call x1, Pallas kernels, local(): call(first_kernel, [wide, narrow], [SMEM, VMEM, ANY], triangle, probes *...  2.23 us
    pallas_call x2, Pallas kernels, local(): call(functools.partial(update_kernel, pivots), [jax.ShapeDtypeStruct(tota...  1.65 us
  transfers between devices with their start and end apart: 15, of which 12 were waited for; matrix products, arithmetic and copies ran while one was open for 1% of the time, Pallas kernels for 12%

profile of v2, /device:TPU:0, one launch (start us, length us, event | category | flops | bytes accessed | tf_op | source)
XLA Modules:
  0.0 80.4 jit_solution(2491425461280274382)
XLA Ops:
  0.6 0.5 collective-permute-start.12
  1.1 2.3 %copy-done = bf16[1,1536,1536]{2,1,0:T(8,128)(2,1)S(1)} copy-done((bf16[1,1536,1536]{2,1,0:T(8,128)(2,1)S(1)}, bf16[1,1536,1536]{2,1,0:T(8,128)(2,1)}, u32[]{:S(2)}) %copy-start) | copy-done | bytes 4718616
  3.5 0.9 %copy-done.7 = f32[1,1536,32]{1,2,0:T(8,128)S(1)} copy-done((f32[1,1536,32]{1,2,0:T(8,128)S(1)}, f32[1,1536,32]{1,2,0:T(8,128)}, u32[]{:S(2)}) %copy-start.7) | copy-done | bytes 196632
  4.4 0.7 copy-done.8
  5.1 2.2 %shard_map.113 = (f32[32,1536]{1,0:T(8,128)S(1)}, bf16[32,1536]{1,0:T(8,128)(2,1)S(1)}) custom-call(s32[3]{0:T(128)S(1)} %copy-done.8, f32[32,1536]{1,0:T(8,128)S(1)} %bitcast.23, bf16[1536,1536]{1,0:T(8,128)(2,1)S(1)} %bitcast.15), custom_call_target="tpu_custom_call" | custom-call | flops 75497472 | bytes 2359296 | tf_op jit(solution)/shard_map/pallas_call | solution.py:182
  7.3 2.6 %collective-permute-start = (bf16[32,1536]{1,0:T(8,128)(2,1)S(1)}, bf16[32,1536]{1,0:T(8,128)(2,1)S(1)}, u32[]{:S(2)}, u32[]{:S(2)}) collective-permute-start(bf16[32,1536]{1,0:T(8,128)(2,1)S(1)} %get-tuple-element.7), channel_id=1, source_target_pairs={{0,2},{1,5},{2,0},{3,7},{4,6},{5,1},{6,4},{7,3},{8,10},{9,13},{10,... | collective-permute-start | bytes 294920 | tf_op jit(solution)/shard_map/ppermute | solution.py:38
  9.9 2.6 %collective-permute-done = bf16[32,1536]{1,0:T(8,128)(2,1)S(1)} collective-permute-done((bf16[32,1536]{1,0:T(8,128)(2,1)S(1)}, bf16[32,1536]{1,0:T(8,128)(2,1)S(1)}, u32[]{:S(2)}, u32[]{:S(2)}) %collective-permute-start) | collective-permute-done | bytes 98336 | tf_op jit(solution)/shard_map/ppermute | solution.py:38
  12.5 2.1 %collective-permute-start.1 = (bf16[32,1536]{1,0:T(8,128)(2,1)S(1)}, bf16[32,1536]{1,0:T(8,128)(2,1)S(1)}, u32[]{:S(2)}, u32[]{:S(2)}) collective-permute-start(bf16[32,1536]{1,0:T(8,128)(2,1)S(1)} %add.36), channel_id=1, source_target_pairs={{0,4},{1,3},{2,6},{3,1},{4,0},{5,7},{6,2},{7,5},{8,12},{9,11},{10,... | collective-permute-start | bytes 294920 | tf_op jit(solution)/shard_map/ppermute | solution.py:38
  14.6 2.6 %collective-permute-done.1 = bf16[32,1536]{1,0:T(8,128)(2,1)S(1)} collective-permute-done((bf16[32,1536]{1,0:T(8,128)(2,1)S(1)}, bf16[32,1536]{1,0:T(8,128)(2,1)S(1)}, u32[]{:S(2)}, u32[]{:S(2)}) %collective-permute-start.1) | collective-permute-done | bytes 98336 | tf_op jit(solution)/shard_map/ppermute | solution.py:38
  17.2 2.1 %collective-permute-start.2 = (bf16[32,1536]{1,0:T(8,128)(2,1)S(1)}, bf16[32,1536]{1,0:T(8,128)(2,1)S(1)}, u32[]{:S(2)}, u32[]{:S(2)}) collective-permute-start(bf16[32,1536]{1,0:T(8,128)(2,1)S(1)} %add.37), channel_id=1, source_target_pairs={{0,8},{1,17},{2,10},{3,19},{4,12},{5,21},{6,14},{7,23},{8,0},{9,25... | collective-permute-start | bytes 294920 | tf_op jit(solution)/shard_map/ppermute | solution.py:38
  19.4 2.6 %collective-permute-done.2 = bf16[32,1536]{1,0:T(8,128)(2,1)S(1)} collective-permute-done((bf16[32,1536]{1,0:T(8,128)(2,1)S(1)}, bf16[32,1536]{1,0:T(8,128)(2,1)S(1)}, u32[]{:S(2)}, u32[]{:S(2)}) %collective-permute-start.2) | collective-permute-done | bytes 98336 | tf_op jit(solution)/shard_map/ppermute | solution.py:38
  22.0 3.1 %collective-permute-start.3 = (bf16[32,1536]{1,0:T(8,128)(2,1)S(1)}, bf16[32,1536]{1,0:T(8,128)(2,1)S(1)}, u32[]{:S(2)}, u32[]{:S(2)}) collective-permute-start(bf16[32,1536]{1,0:T(8,128)(2,1)S(1)} %add.38), channel_id=1, source_target_pairs={{0,16},{1,9},{2,18},{3,11},{4,20},{5,13},{6,22},{7,15},{8,24},{9,1... | collective-permute-start | bytes 294920 | tf_op jit(solution)/shard_map/ppermute | solution.py:38
  25.1 1.3 %copy-done.5 = bf16[1,2,1536,200]{2,3,1,0:T(8,128)(2,1)S(1)} copy-done((bf16[1,2,1536,200]{2,3,1,0:T(8,128)(2,1)S(1)}, bf16[1,2,1536,200]{2,3,1,0:T(8,128)(2,1)}, u32[]{:S(2)}) %copy-start.5) | copy-done | bytes 1228824
  26.4 2.4 %shard_map.114.ahead_ref = bf16[2,200,1536]{2,1,0:T(8,128)(2,1)S(1)} custom-call(bf16[2,200,1536]{2,1,0:T(8,128)(2,1)S(1)} %bitcast.21, bf16[1536,1536]{1,0:T(8,128)(2,1)S(1)} %bitcast.16), custom_call_target="tpu_custom_call" | custom-call | flops 943718400 | bytes 4816896 | tf_op jit(solution)/shard_map/pallas_call | solution.py:185
  28.8 0.0 collective-permute-done.3
  28.9 0.0 copy-done.4
  28.9 1.2 %shard_map.115 = (f32[32,1536]{1,0:T(8,128)S(1)}, bf16[32,1536]{1,0:T(8,128)(2,1)S(1)}) custom-call(s32[3]{0:T(128)S(1)} %copy-done.9, s32[1,2]{1,0:T(1,128)S(1)} %copy-done.11, bf16[32,1536]{1,0:T(8,128)(2,1)S(1)} %add.39.solved_ref.refs_0_, bf16[2,200,1536]{2,1,0:T(8,128)(2,1)S(1)} %bitcast.17, bf16[2,200,1536]{2,1,0:T(8,128)(2,1)S(1)} %shard_map.114.ahead_ref, ...), custom_call_target="tpu_custom_call" | custom-call | flops 39321600 | bytes 1228800 | tf_op jit(solution)/shard_map/pallas_call | solution.py:199
  30.1 1.6 %collective-permute-start.4 = (bf16[32,1536]{1,0:T(8,128)(2,1)S(1)}, bf16[32,1536]{1,0:T(8,128)(2,1)S(1)}, u32[]{:S(2)}, u32[]{:S(2)}) collective-permute-start(bf16[32,1536]{1,0:T(8,128)(2,1)S(1)} %get-tuple-element.9), channel_id=1, source_target_pairs={{0,2},{1,5},{2,0},{3,7},{4,6},{5,1},{6,4},{7,3},{8,10},{9,13},{10,... | collective-permute-start | bytes 294920 | tf_op jit(solution)/shard_map/ppermute | solution.py:38
  31.7 4.2 %collective-permute-done.4 = bf16[32,1536]{1,0:T(8,128)(2,1)S(1)} collective-permute-done((bf16[32,1536]{1,0:T(8,128)(2,1)S(1)}, bf16[32,1536]{1,0:T(8,128)(2,1)S(1)}, u32[]{:S(2)}, u32[]{:S(2)}) %collective-permute-start.4) | collective-permute-done | bytes 98336 | tf_op jit(solution)/shard_map/ppermute | solution.py:38
  35.9 1.6 %collective-permute-start.5 = (bf16[32,1536]{1,0:T(8,128)(2,1)S(1)}, bf16[32,1536]{1,0:T(8,128)(2,1)S(1)}, u32[]{:S(2)}, u32[]{:S(2)}) collective-permute-start(bf16[32,1536]{1,0:T(8,128)(2,1)S(1)} %add.40), channel_id=1, source_target_pairs={{0,4},{1,3},{2,6},{3,1},{4,0},{5,7},{6,2},{7,5},{8,12},{9,11},{10,... | collective-permute-start | bytes 294920 | tf_op jit(solution)/shard_map/ppermute | solution.py:38
  37.5 3.1 %collective-permute-done.5 = bf16[32,1536]{1,0:T(8,128)(2,1)S(1)} collective-permute-done((bf16[32,1536]{1,0:T(8,128)(2,1)S(1)}, bf16[32,1536]{1,0:T(8,128)(2,1)S(1)}, u32[]{:S(2)}, u32[]{:S(2)}) %collective-permute-start.5) | collective-permute-done | bytes 98336 | tf_op jit(solution)/shard_map/ppermute | solution.py:38
  40.6 1.2 %collective-permute-start.6 = (bf16[32,1536]{1,0:T(8,128)(2,1)S(1)}, bf16[32,1536]{1,0:T(8,128)(2,1)S(1)}, u32[]{:S(2)}, u32[]{:S(2)}) collective-permute-start(bf16[32,1536]{1,0:T(8,128)(2,1)S(1)} %add.41), channel_id=1, source_target_pairs={{0,8},{1,17},{2,10},{3,19},{4,12},{5,21},{6,14},{7,23},{8,0},{9,25... | collective-permute-start | bytes 294920 | tf_op jit(solution)/shard_map/ppermute | solution.py:38
  41.8 4.2 %collective-permute-done.6 = bf16[32,1536]{1,0:T(8,128)(2,1)S(1)} collective-permute-done((bf16[32,1536]{1,0:T(8,128)(2,1)S(1)}, bf16[32,1536]{1,0:T(8,128)(2,1)S(1)}, u32[]{:S(2)}, u32[]{:S(2)}) %collective-permute-start.6) | collective-permute-done | bytes 98336 | tf_op jit(solution)/shard_map/ppermute | solution.py:38
  46.0 1.2 %collective-permute-start.7 = (bf16[32,1536]{1,0:T(8,128)(2,1)S(1)}, bf16[32,1536]{1,0:T(8,128)(2,1)S(1)}, u32[]{:S(2)}, u32[]{:S(2)}) collective-permute-start(bf16[32,1536]{1,0:T(8,128)(2,1)S(1)} %add.42), channel_id=1, source_target_pairs={{0,16},{1,9},{2,18},{3,11},{4,20},{5,13},{6,22},{7,15},{8,24},{9,1... | collective-permute-start | bytes 294920 | tf_op jit(solution)/shard_map/ppermute | solution.py:38
  47.2 5.3 %collective-permute-done.7 = bf16[32,1536]{1,0:T(8,128)(2,1)S(1)} collective-permute-done((bf16[32,1536]{1,0:T(8,128)(2,1)S(1)}, bf16[32,1536]{1,0:T(8,128)(2,1)S(1)}, u32[]{:S(2)}, u32[]{:S(2)}) %collective-permute-start.7) | collective-permute-done | bytes 98336 | tf_op jit(solution)/shard_map/ppermute | solution.py:38
  52.5 0.0 copy-start.2
  52.6 0.0 copy-start.10
  52.6 1.9 %shard_map.116 = (f32[32,1536]{1,0:T(8,128)}, bf16[32,1536]{1,0:T(8,128)(2,1)S(1)}) custom-call(s32[3]{0:T(128)S(1)} %copy-done.9, s32[1,2]{1,0:T(1,128)S(1)} %copy-done.11, bf16[32,1536]{1,0:T(8,128)(2,1)S(1)} %add.43.solved_ref.refs_1_, bf16[2,200,1536]{2,1,0:T(8,128)(2,1)S(1)} %bitcast.18, bf16[2,200,1536]{2,1,0:T(8,128)(2,1)S(1)} %shard_map.114.ahead_ref, ...), custom_call_target="tpu_custom_call" | custom-call | flops 39321600 | bytes 1228800 | tf_op jit(solution)/shard_map/pallas_call | solution.py:199
  54.4 1.3 %collective-permute-start.8 = (bf16[32,1536]{1,0:T(8,128)(2,1)S(1)}, bf16[32,1536]{1,0:T(8,128)(2,1)S(1)}, u32[]{:S(2)}, u32[]{:S(2)}) collective-permute-start(bf16[32,1536]{1,0:T(8,128)(2,1)S(1)} %get-tuple-element.11), channel_id=1, source_target_pairs={{0,2},{1,5},{2,0},{3,7},{4,6},{5,1},{6,4},{7,3},{8,10},{9,13},{10,... | collective-permute-start | bytes 294920 | tf_op jit(solution)/shard_map/ppermute | solution.py:38
  55.7 3.3 %collective-permute-done.8 = bf16[32,1536]{1,0:T(8,128)(2,1)S(1)} collective-permute-done((bf16[32,1536]{1,0:T(8,128)(2,1)S(1)}, bf16[32,1536]{1,0:T(8,128)(2,1)S(1)}, u32[]{:S(2)}, u32[]{:S(2)}) %collective-permute-start.8) | collective-permute-done | bytes 98336 | tf_op jit(solution)/shard_map/ppermute | solution.py:38
  59.1 1.4 %collective-permute-start.9 = (bf16[32,1536]{1,0:T(8,128)(2,1)S(1)}, bf16[32,1536]{1,0:T(8,128)(2,1)S(1)}, u32[]{:S(2)}, u32[]{:S(2)}) collective-permute-start(bf16[32,1536]{1,0:T(8,128)(2,1)S(1)} %add.44), channel_id=1, source_target_pairs={{0,4},{1,3},{2,6},{3,1},{4,0},{5,7},{6,2},{7,5},{8,12},{9,11},{10,... | collective-permute-start | bytes 294920 | tf_op jit(solution)/shard_map/ppermute | solution.py:38
  60.5 3.3 %collective-permute-done.9 = bf16[32,1536]{1,0:T(8,128)(2,1)S(1)} collective-permute-done((bf16[32,1536]{1,0:T(8,128)(2,1)S(1)}, bf16[32,1536]{1,0:T(8,128)(2,1)S(1)}, u32[]{:S(2)}, u32[]{:S(2)}) %collective-permute-start.9) | collective-permute-done | bytes 98336 | tf_op jit(solution)/shard_map/ppermute | solution.py:38
  63.8 0.1 collective-permute-start.10
  63.9 4.6 %collective-permute-done.10 = bf16[32,1536]{1,0:T(8,128)(2,1)S(1)} collective-permute-done((bf16[32,1536]{1,0:T(8,128)(2,1)S(1)}, bf16[32,1536]{1,0:T(8,128)(2,1)S(1)}, u32[]{:S(2)}, u32[]{:S(2)}) %collective-permute-start.10) | collective-permute-done | bytes 98336 | tf_op jit(solution)/shard_map/ppermute | solution.py:38
  68.5 0.8 collective-permute-start.11
  69.3 5.3 %collective-permute-done.11 = bf16[32,1536]{1,0:T(8,128)(2,1)S(1)} collective-permute-done((bf16[32,1536]{1,0:T(8,128)(2,1)S(1)}, bf16[32,1536]{1,0:T(8,128)(2,1)S(1)}, u32[]{:S(2)}, u32[]{:S(2)}) %collective-permute-start.11) | collective-permute-done | bytes 98336 | tf_op jit(solution)/shard_map/ppermute | solution.py:38
  74.6 0.0 collective-permute-done.12.refs_2_.refs_3_
  74.7 1.0 %shard_map.117.own_ref = bf16[2,1,32,200]{3,2,1,0:T(8,128)(2,1)S(1)} custom-call(s32[2,3]{1,0:T(2,128)S(1)} %copy-done.10, bf16[32,1536]{1,0:T(8,128)(2,1)S(1)} %add.47.refs_0_, bf16[2,3,200,768]{3,2,1,0:T(8,128)(2,1)S(1)} %copy-done.2, bf16[2,3,200,768]{3,2,1,0:T(8,128)(2,1)S(1)} %collective-permute-done.12.refs_2_.refs_3_), custom_call_target="tpu_custom_call" | custom-call | flops 39321600 | bytes 1228800 | tf_op jit(solution)/shard_map/pallas_call | solution.py:210
  75.7 0.0 copy-start.3
  75.7 0.0 copy-start.6
  75.7 0.1 collective-permute-start.13
  75.8 1.4 %shard_map.118.own_ref = bf16[2,2,32,200]{3,2,1,0:T(8,128)(2,1)S(1)} custom-call(s32[2,3]{1,0:T(2,128)S(1)} %copy-done.10, bf16[32,1536]{1,0:T(8,128)(2,1)S(1)} %add.39.solved_ref.refs_0_, bf16[32,1536]{1,0:T(8,128)(2,1)S(1)} %add.43.solved_ref.refs_1_, bf16[2,3,200,768]{3,2,1,0:T(8,128)(2,1)S(1)} %copy-done.2, ...), custom_call_target="tpu_custom_call" | custom-call | flops 78643200 | bytes 2457600 | tf_op jit(solution)/shard_map/pallas_call | solution.py:210
  77.2 0.6 collective-permute-start.14
  77.8 0.7 maximum_bitcast_fusion
  78.5 0.2 collective-permute-done.14.other_ref
  78.7 0.6 shard_map.119.rhs_ref
  79.3 0.0 collective-permute-done.13.other_ref
  79.3 1.1 %shard_map.120 = f32[2,64,768]{2,1,0:T(8,128)} custom-call(bf16[2,1,32,200]{3,2,1,0:T(8,128)(2,1)S(1)} %shard_map.117.own_ref, bf16[2,1,32,200]{3,2,1,0:T(8,128)(2,1)S(1)} %collective-permute-done.13.other_ref, bf16[2,3,200,768]{3,2,1,0:T(8,128)(2,1)S(1)} %copy-done.3, f32[2,64,768]{2,1,0:T(8,128)S(1)} %shard_map.119.rhs_ref), custom_call_target="tpu_custom_call" | custom-call | flops 39321600 | bytes 1400832 | tf_op jit(solution)/shard_map/pallas_call | solution.py:218
  (27 shorter events, 0.3 us)
Async XLA Ops:
  0.6 74.0 %collective-permute-start.12 = (bf16[2,3,200,768]{3,2,1,0:T(8,128)(2,1)}, bf16[2,3,200,768]{3,2,1,0:T(8,128)(2,1)S(1)}, u32[]{:S(2)}, u32[]{:S(2)}) collective-permute-start(bf16[2,3,200,768]{3,2,1,0:T(8,128)(2,1)} %refs_2_.1), channel_id=1, source_target_pairs={{0,1},{1,0},{2,3},{3,2},{4,5},{5,4},{6,7},{7,6},{8,9},{9,8},{10,11... | collective-permute-start | bytes 5529608 | tf_op jit(solution)/shard_map/ppermute | solution.py:43
  1.1 2.3 %copy-start = (bf16[1,1536,1536]{2,1,0:T(8,128)(2,1)S(1)}, bf16[1,1536,1536]{2,1,0:T(8,128)(2,1)}, u32[]{:S(2)}) copy-start(bf16[1,1536,1536]{2,1,0:T(8,128)(2,1)} %param.11) | copy-start | bytes 14155780
  3.5 0.9 %copy-start.7 = (f32[1,1536,32]{1,2,0:T(8,128)S(1)}, f32[1,1536,32]{1,2,0:T(8,128)}, u32[]{:S(2)}) copy-start(f32[1,1536,32]{1,2,0:T(8,128)} %param.10) | copy-start | bytes 589828
  4.4 0.7 copy-start.8
  5.1 20.0 %copy-start.1 = (bf16[1,1536,1536]{2,1,0:T(8,128)(2,1)S(1)}, bf16[1,1536,1536]{2,1,0:T(8,128)(2,1)}, u32[]{:S(2)}) copy-start(bf16[1,1536,1536]{2,1,0:T(8,128)(2,1)} %param.11) | copy-start | bytes 14155780
  7.3 5.2 %collective-permute-start = (bf16[32,1536]{1,0:T(8,128)(2,1)S(1)}, bf16[32,1536]{1,0:T(8,128)(2,1)S(1)}, u32[]{:S(2)}, u32[]{:S(2)}) collective-permute-start(bf16[32,1536]{1,0:T(8,128)(2,1)S(1)} %get-tuple-element.7), channel_id=1, source_target_pairs={{0,2},{1,5},{2,0},{3,7},{4,6},{5,1},{6,4},{7,3},{8,10},{9,13},{10,... | collective-permute-start | bytes 294920 | tf_op jit(solution)/shard_map/ppermute | solution.py:38
  12.5 4.7 %collective-permute-start.1 = (bf16[32,1536]{1,0:T(8,128)(2,1)S(1)}, bf16[32,1536]{1,0:T(8,128)(2,1)S(1)}, u32[]{:S(2)}, u32[]{:S(2)}) collective-permute-start(bf16[32,1536]{1,0:T(8,128)(2,1)S(1)} %add.36), channel_id=1, source_target_pairs={{0,4},{1,3},{2,6},{3,1},{4,0},{5,7},{6,2},{7,5},{8,12},{9,11},{10,... | collective-permute-start | bytes 294920 | tf_op jit(solution)/shard_map/ppermute | solution.py:38
  17.2 4.8 %collective-permute-start.2 = (bf16[32,1536]{1,0:T(8,128)(2,1)S(1)}, bf16[32,1536]{1,0:T(8,128)(2,1)S(1)}, u32[]{:S(2)}, u32[]{:S(2)}) collective-permute-start(bf16[32,1536]{1,0:T(8,128)(2,1)S(1)} %add.37), channel_id=1, source_target_pairs={{0,8},{1,17},{2,10},{3,19},{4,12},{5,21},{6,14},{7,23},{8,0},{9,25... | collective-permute-start | bytes 294920 | tf_op jit(solution)/shard_map/ppermute | solution.py:38
  22.0 6.8 %collective-permute-start.3 = (bf16[32,1536]{1,0:T(8,128)(2,1)S(1)}, bf16[32,1536]{1,0:T(8,128)(2,1)S(1)}, u32[]{:S(2)}, u32[]{:S(2)}) collective-permute-start(bf16[32,1536]{1,0:T(8,128)(2,1)S(1)} %add.38), channel_id=1, source_target_pairs={{0,16},{1,9},{2,18},{3,11},{4,20},{5,13},{6,22},{7,15},{8,24},{9,1... | collective-permute-start | bytes 294920 | tf_op jit(solution)/shard_map/ppermute | solution.py:38
  25.1 1.3 %copy-start.5 = (bf16[1,2,1536,200]{2,3,1,0:T(8,128)(2,1)S(1)}, bf16[1,2,1536,200]{2,3,1,0:T(8,128)(2,1)}, u32[]{:S(2)}) copy-start(bf16[1,2,1536,200]{2,3,1,0:T(8,128)(2,1)} %param.14) | copy-start | bytes 3686404
  26.4 2.5 %copy-start.4 = (bf16[1,2,1536,200]{2,3,1,0:T(8,128)(2,1)S(1)}, bf16[1,2,1536,200]{2,3,1,0:T(8,128)(2,1)}, u32[]{:S(2)}) copy-start(bf16[1,2,1536,200]{2,3,1,0:T(8,128)(2,1)} %param.13) | copy-start | bytes 3686404
  26.4 2.5 %copy-start.9 = (s32[3]{0:T(128)S(1)}, s32[3]{0:T(128)}, u32[]{:S(2)}) copy-start(s32[3]{0:T(128)} %owner_ref.5) | copy-start | bytes 40
  26.4 2.5 %copy-start.11 = (s32[1,2]{1,0:T(1,128)S(1)}, s32[1,2]{1,0:T(1,128)}, u32[]{:S(2)}) copy-start(s32[1,2]{1,0:T(1,128)} %ranks_ref.5) | copy-start | bytes 28
  30.1 5.7 %collective-permute-start.4 = (bf16[32,1536]{1,0:T(8,128)(2,1)S(1)}, bf16[32,1536]{1,0:T(8,128)(2,1)S(1)}, u32[]{:S(2)}, u32[]{:S(2)}) collective-permute-start(bf16[32,1536]{1,0:T(8,128)(2,1)S(1)} %get-tuple-element.9), channel_id=1, source_target_pairs={{0,2},{1,5},{2,0},{3,7},{4,6},{5,1},{6,4},{7,3},{8,10},{9,13},{10,... | collective-permute-start | bytes 294920 | tf_op jit(solution)/shard_map/ppermute | solution.py:38
  35.9 4.7 %collective-permute-start.5 = (bf16[32,1536]{1,0:T(8,128)(2,1)S(1)}, bf16[32,1536]{1,0:T(8,128)(2,1)S(1)}, u32[]{:S(2)}, u32[]{:S(2)}) collective-permute-start(bf16[32,1536]{1,0:T(8,128)(2,1)S(1)} %add.40), channel_id=1, source_target_pairs={{0,4},{1,3},{2,6},{3,1},{4,0},{5,7},{6,2},{7,5},{8,12},{9,11},{10,... | collective-permute-start | bytes 294920 | tf_op jit(solution)/shard_map/ppermute | solution.py:38
  40.6 5.4 %collective-permute-start.6 = (bf16[32,1536]{1,0:T(8,128)(2,1)S(1)}, bf16[32,1536]{1,0:T(8,128)(2,1)S(1)}, u32[]{:S(2)}, u32[]{:S(2)}) collective-permute-start(bf16[32,1536]{1,0:T(8,128)(2,1)S(1)} %add.41), channel_id=1, source_target_pairs={{0,8},{1,17},{2,10},{3,19},{4,12},{5,21},{6,14},{7,23},{8,0},{9,25... | collective-permute-start | bytes 294920 | tf_op jit(solution)/shard_map/ppermute | solution.py:38
  46.0 6.5 %collective-permute-start.7 = (bf16[32,1536]{1,0:T(8,128)(2,1)S(1)}, bf16[32,1536]{1,0:T(8,128)(2,1)S(1)}, u32[]{:S(2)}, u32[]{:S(2)}) collective-permute-start(bf16[32,1536]{1,0:T(8,128)(2,1)S(1)} %add.42), channel_id=1, source_target_pairs={{0,16},{1,9},{2,18},{3,11},{4,20},{5,13},{6,22},{7,15},{8,24},{9,1... | collective-permute-start | bytes 294920 | tf_op jit(solution)/shard_map/ppermute | solution.py:38
  52.5 22.1 %copy-start.2 = (bf16[2,3,200,768]{3,2,1,0:T(8,128)(2,1)S(1)}, bf16[2,3,200,768]{3,2,1,0:T(8,128)(2,1)}, u32[]{:S(2)}) copy-start(bf16[2,3,200,768]{3,2,1,0:T(8,128)(2,1)} %refs_2_.1) | copy-start | bytes 5529604
  52.6 22.1 %copy-start.10 = (s32[2,3]{1,0:T(2,128)S(1)}, s32[2,3]{1,0:T(2,128)}, u32[]{:S(2)}) copy-start(s32[2,3]{1,0:T(2,128)} %ranks_ref.7) | copy-start | bytes 76
  54.4 4.6 %collective-permute-start.8 = (bf16[32,1536]{1,0:T(8,128)(2,1)S(1)}, bf16[32,1536]{1,0:T(8,128)(2,1)S(1)}, u32[]{:S(2)}, u32[]{:S(2)}) collective-permute-start(bf16[32,1536]{1,0:T(8,128)(2,1)S(1)} %get-tuple-element.11), channel_id=1, source_target_pairs={{0,2},{1,5},{2,0},{3,7},{4,6},{5,1},{6,4},{7,3},{8,10},{9,13},{10,... | collective-permute-start | bytes 294920 | tf_op jit(solution)/shard_map/ppermute | solution.py:38
  59.1 4.7 %collective-permute-start.9 = (bf16[32,1536]{1,0:T(8,128)(2,1)S(1)}, bf16[32,1536]{1,0:T(8,128)(2,1)S(1)}, u32[]{:S(2)}, u32[]{:S(2)}) collective-permute-start(bf16[32,1536]{1,0:T(8,128)(2,1)S(1)} %add.44), channel_id=1, source_target_pairs={{0,4},{1,3},{2,6},{3,1},{4,0},{5,7},{6,2},{7,5},{8,12},{9,11},{10,... | collective-permute-start | bytes 294920 | tf_op jit(solution)/shard_map/ppermute | solution.py:38
  63.8 4.7 %collective-permute-start.10 = (bf16[32,1536]{1,0:T(8,128)(2,1)S(1)}, bf16[32,1536]{1,0:T(8,128)(2,1)S(1)}, u32[]{:S(2)}, u32[]{:S(2)}) collective-permute-start(bf16[32,1536]{1,0:T(8,128)(2,1)S(1)} %add.45), channel_id=1, source_target_pairs={{0,8},{1,17},{2,10},{3,19},{4,12},{5,21},{6,14},{7,23},{8,0},{9,25... | collective-permute-start | bytes 294920 | tf_op jit(solution)/shard_map/ppermute | solution.py:38
  68.5 6.1 %collective-permute-start.11 = (bf16[32,1536]{1,0:T(8,128)(2,1)S(1)}, bf16[32,1536]{1,0:T(8,128)(2,1)S(1)}, u32[]{:S(2)}, u32[]{:S(2)}) collective-permute-start(bf16[32,1536]{1,0:T(8,128)(2,1)S(1)} %add.46), channel_id=1, source_target_pairs={{0,16},{1,9},{2,18},{3,11},{4,20},{5,13},{6,22},{7,15},{8,24},{9,1... | collective-permute-start | bytes 294920 | tf_op jit(solution)/shard_map/ppermute | solution.py:38
  75.7 3.0 %copy-start.3 = (bf16[2,3,200,768]{3,2,1,0:T(8,128)(2,1)S(1)}, bf16[2,3,200,768]{3,2,1,0:T(8,128)(2,1)}, u32[]{:S(2)}) copy-start(bf16[2,3,200,768]{3,2,1,0:T(8,128)(2,1)} %right_ref.3) | copy-start | bytes 5529604
  75.7 3.0 %copy-start.6 = (f32[2,64,768]{2,1,0:T(8,128)S(1)}, f32[2,64,768]{2,1,0:T(8,128)}, u32[]{:S(2)}) copy-start(f32[2,64,768]{2,1,0:T(8,128)} %rhs_ref.1) | copy-start | bytes 1179652
  75.7 3.5 %collective-permute-start.13 = (bf16[2,1,32,200]{3,2,1,0:T(8,128)(2,1)S(1)}, bf16[2,1,32,200]{3,2,1,0:T(8,128)(2,1)S(1)}, u32[]{:S(2)}, u32[]{:S(2)}) collective-permute-start(bf16[2,1,32,200]{3,2,1,0:T(8,128)(2,1)S(1)} %shard_map.117.own_ref), channel_id=1, source_target_pairs={{0,1},{1,0},{2,3},{3,2},{4,5},{5,4},{6,7},{7,6},{8,9},{9,8},{10,11... | collective-permute-start | bytes 76808 | tf_op jit(solution)/shard_map/ppermute | solution.py:43
  77.2 1.5 %collective-permute-start.14 = (bf16[2,2,32,200]{3,2,1,0:T(8,128)(2,1)S(1)}, bf16[2,2,32,200]{3,2,1,0:T(8,128)(2,1)S(1)}, u32[]{:S(2)}, u32[]{:S(2)}) collective-permute-start(bf16[2,2,32,200]{3,2,1,0:T(8,128)(2,1)S(1)} %shard_map.118.own_ref), channel_id=1, source_target_pairs={{0,1},{1,0},{2,3},{3,2},{4,5},{5,4},{6,7},{7,6},{8,9},{9,8},{10,11... | collective-permute-start | bytes 153608 | tf_op jit(solution)/shard_map/ppermute | solution.py:43

commit v3 on v2

--- a/solution.py
+++ b/solution.py
@@ -11,32 +11,45 @@
 VMEM = pl.BlockSpec(memory_space=pltpu.VMEM)
 ANY = pl.BlockSpec(memory_space=pl.ANY)
 MIB = 1 << 20
-
-
-def doubling_orders(count, cores):
-    bits = [1 << place for place in range(count.bit_length() - 1)]
-    orders = []
-    for core in range(cores):
-        order = list(bits)
-        if core % 2:
-            for place in range(0, len(order) - 1, 2):
-                order[place], order[place + 1] = order[place + 1], order[place]
-        orders.append(order)
-    return orders
-
-
-def spread(block, slots, cores):
+FIRST_LIMIT = 56
+
+
+def exchanges(slots):
+    bits = [1 << place for place in range(slots.bit_length() - 1)]
+    steps = []
+    for place in range(2, len(bits), 2):
+        pair = bits[place : place + 2]
+        steps.append([(pair[0], pair[-1])])
+        if len(pair) == 2:
+            steps.append([(pair[1], pair[0])])
+    near = bits[:2]
+    if len(near) == 2:
+        steps.append([(near[0], near[1]), (near[1], near[0]), (near[0] | near[1],) * 2])
+    else:
+        steps += [[(bit, bit)] for bit in near]
+    return steps
+
+
+def spread(block, slots, cores, beside=()):
     if slots & (slots - 1):
-        return lax.psum(block, "tc")
-    orders = doubling_orders(slots, cores)
-    for step in range(len(orders[0])):
-        pairs = [
-            (slot * cores + core, (slot ^ orders[core][step]) * cores + core)
-            for slot in range(slots)
-            for core in range(cores)
-        ]
-        block = block + lax.ppermute(block, ("tc", "pr"), pairs)
-    return block
+        return lax.psum(block, "tc"), [work() for work in beside]
+    done = []
+    for step, flips in enumerate(exchanges(slots)):
+        received = []
+        for flip in flips:
+            pairs = [
+                (slot * cores + core, (slot ^ flip[core % 2]) * cores + core)
+                for slot in range(slots)
+                for core in range(cores)
+            ]
+            received.append(lax.ppermute(block, ("tc", "pr"), pairs))
+        if step < len(beside):
+            result = beside[step]()
+            block, received, result = lax.optimization_barrier((block, received, result))
+            done.append(result)
+        for part in received:
+            block = block + part
+    return block, done + [work() for work in beside[len(done) :]]
 
 
 def swap(block, cores):
@@ -60,10 +73,16 @@
     return copies, width
 
 
-def first_kernel(owner_ref, rhs_ref, inverse_ref, raw_ref, block_ref, buffer, sems):
+def first_kernel(owner_ref, rhs_ref, inverse_ref, raw_ref, block_ref, buffer, sems, rhs, owner, more_sems):
+    fetch_rhs = pltpu.make_async_copy(rhs_ref, rhs, more_sems.at[0])
+    fetch_owner = pltpu.make_async_copy(owner_ref, owner, more_sems.at[1])
+    fetch_rhs.start()
+    fetch_owner.start()
     copies, width = start_triangle(inverse_ref, buffer, sems)
-    is_root = owner_ref[owner_ref.shape[0] - 1] == lax.axis_index("tc")
-    pivot_in = rhs_ref[...].astype(jnp.bfloat16)
+    fetch_rhs.wait()
+    fetch_owner.wait()
+    is_root = owner[owner.shape[0] - 1] == lax.axis_index("tc")
+    pivot_in = rhs[...].astype(jnp.bfloat16)
     for place, copy in enumerate(copies):
         first = place * width
         copy.wait()
@@ -74,36 +93,38 @@
         block_ref[:, first : first + width] = jnp.where(is_root, raw, 0.0).astype(jnp.bfloat16)
 
 
-def ahead_kernel(right_ref, inverse_ref, ahead_ref, buffer, sems):
-    copies, width = start_triangle(inverse_ref, buffer, sems)
-    for place, copy in enumerate(copies):
-        first = place * width
-        copy.wait()
-        for entry in range(right_ref.shape[0]):
-            ahead_ref[entry, :, first : first + width] = jnp.dot(
-                right_ref[entry, :, first:],
-                buffer[first:, first : first + width],
-                preferred_element_type=jnp.float32,
-            ).astype(jnp.bfloat16)
-
-
-def step_kernel(current, owner_ref, ranks_ref, solved_ref, left_ref, ahead_ref, raw_ref, new_raw_ref, block_ref):
+def ahead_kernel(right_ref, inverse_ref, ahead_ref):
+    size = inverse_ref.shape[0]
+    width = block_width(size)
+    for first in range(0, size, width):
+        ahead_ref[:, first : first + width] = jnp.dot(
+            right_ref[:, first:], inverse_ref[first:, first : first + width], preferred_element_type=jnp.float32
+        ).astype(jnp.bfloat16)
+
+
+def step_kernel(current, owner_ref, ranks_ref, solved_ref, left_ref, *refs):
+    entries = left_ref.shape[0]
+    ahead_refs, raw_ref, outs = refs[:entries], refs[entries], refs[entries + 1 :]
     me = lax.axis_index("tc")
     own = jnp.int32(current)
     for place in range(owner_ref.shape[0]):
         own = jnp.where(owner_ref[place] == me, jnp.int32(place), own)
     active = own < current
-    entry = jnp.clip(current - own - 1, 0, left_ref.shape[0] - 1)
-    limit = jnp.where(active, ranks_ref[0, entry], 0)
-    factor = lax.dot_general(
-        solved_ref[...], left_ref[entry], (((1,), (1,)), ((), ())), preferred_element_type=jnp.float32
-    )
-    rank_ids = lax.broadcasted_iota(jnp.int32, factor.shape, 1)
-    factor = jnp.where(rank_ids < limit, factor, 0.0).astype(jnp.bfloat16)
-    raw = raw_ref[...] - jnp.dot(factor, ahead_ref[entry], preferred_element_type=jnp.float32)
-    new_raw_ref[...] = raw
     is_root = owner_ref[current - 1] == me
-    block_ref[...] = jnp.where(is_root, raw, 0.0).astype(jnp.bfloat16)
+    for entry in range(entries):
+
+        @pl.when(jnp.clip(current - own - 1, 0, entries - 1) == entry)
+        def _(entry=entry):
+            limit = jnp.where(active, ranks_ref[0, entry], 0)
+            factor = lax.dot_general(
+                solved_ref[...], left_ref[entry], (((1,), (1,)), ((), ())), preferred_element_type=jnp.float32
+            )
+            rank_ids = lax.broadcasted_iota(jnp.int32, factor.shape, 1)
+            factor = jnp.where(rank_ids < limit, factor, 0.0).astype(jnp.bfloat16)
+            raw = raw_ref[...] - jnp.dot(factor, ahead_refs[entry][...], preferred_element_type=jnp.float32)
+            outs[0][...] = jnp.where(is_root, raw, 0.0).astype(jnp.bfloat16)
+            if len(outs) > 1:
+                outs[1][...] = raw
 
 
 def weights_kernel(pivots, ranks_ref, *refs):
@@ -175,54 +196,92 @@
     rhs = jnp.swapaxes(pivot_rhs[0], 0, 1)
     left = jnp.swapaxes(coupling_left[0], 1, 2)
     right = jnp.swapaxes(coupling_right[0], 1, 2)
-    triangle = [pltpu.VMEM((size, size), jnp.bfloat16), pltpu.SemaphoreType.DMA((blocks,))]
     wide = jax.ShapeDtypeStruct((probes, size), jnp.float32)
     narrow = jax.ShapeDtypeStruct((probes, size), jnp.bfloat16)
 
     raw, block = call(
-        first_kernel, [wide, narrow], [SMEM, VMEM, ANY], triangle, probes * size * size, size * size
+        first_kernel,
+        [wide, narrow],
+        [ANY, ANY, ANY],
+        [
+            pltpu.VMEM((size, size), jnp.bfloat16),
+            pltpu.SemaphoreType.DMA((blocks,)),
+            pltpu.VMEM((probes, size), jnp.float32),
+            pltpu.SMEM((count,), jnp.int32),
+            pltpu.SemaphoreType.DMA((2,)),
+        ],
+        probes * size * size,
+        size * size,
+        FIRST_LIMIT,
     )(pivot_owner, rhs, inverse)
-    (ahead,) = call(
-        ahead_kernel,
-        [jax.ShapeDtypeStruct((entries, rank, size), jnp.bfloat16)],
-        [VMEM, ANY],
-        triangle,
-        entries * rank * size * size,
-        size * size + 4 * entries * rank * size,
-    )(right, inverse)
+    block, future_left = lax.optimization_barrier((block, future_left))
     other_left = swap(future_left, cores)
 
-    solved = [None] * count
-    for current in reversed(range(count)):
-        solved[current] = spread(block, slots, cores)
-        if current > 0:
-            raw, block = call(
-                functools.partial(step_kernel, current),
-                [wide, narrow],
-                [SMEM, SMEM] + [VMEM] * 4,
-                (),
-                4 * probes * rank * size,
-                4 * rank * size,
-            )(pivot_owner, coupling_ranks, solved[current], left, ahead, raw)
-
-    total = future_rhs
-    for pivots in (tuple(range(count - 1, 0, -1)), (0,)):
-        (weights,) = call(
+    def ahead(entry):
+        return call(
+            ahead_kernel,
+            [jax.ShapeDtypeStruct((rank, size), jnp.bfloat16)],
+            [VMEM, VMEM],
+            (),
+            rank * size * size,
+            size * size + 4 * rank * size,
+        )(right[entry], inverse)[0]
+
+    def weigh(*pivots):
+        return call(
             functools.partial(weights_kernel, pivots),
             [jax.ShapeDtypeStruct((rows, len(pivots), probes, rank), jnp.bfloat16)],
             [SMEM] + [VMEM] * (len(pivots) + 2),
             (),
             2 * rows * len(pivots) * probes * rank * size,
             2 * rows * len(pivots) * rank * size,
-        )(future_ranks, *[solved[pivot] for pivot in pivots], future_left, other_left)
-        (total,) = call(
+        )(future_ranks, *[solved[pivot] for pivot in pivots], future_left, other_left)[0]
+
+    def update(total, own, other, *pivots):
+        return call(
             functools.partial(update_kernel, pivots),
             [jax.ShapeDtypeStruct(total.shape, jnp.float32)],
             [VMEM] * 4,
             (),
             2 * rows * len(pivots) * probes * rank * size,
             rows * len(pivots) * rank * size + 2 * 4 * total.size,
-        )(weights, swap(weights, cores), future_right, total)
+        )(own, other, future_right, total)[0]
+
+    total = future_rhs
+    solved = [None] * count
+    weights = None
+    beside = [functools.partial(ahead, entry) for entry in range(entries)]
+    for current in reversed(range(count)):
+        solved[current], done = spread(block, slots, cores, beside)
+        if current == count - 1:
+            factors = done
+        else:
+            total = done[-1]
+        if current > 0:
+            last = current == 1
+            outs = call(
+                functools.partial(step_kernel, current),
+                [narrow] if last else [narrow, wide],
+                [SMEM, SMEM] + [VMEM] * (entries + 3),
+                (),
+                4 * probes * rank * size,
+                4 * rank * size,
+            )(pivot_owner, coupling_ranks, solved[current], left, *factors, raw)
+            block = outs[0]
+            raw = None if last else outs[1]
+            pair = []
+
+            def first_beside(current=current, pair=pair):
+                own = weigh(current)
+                pair += [own, swap(own, cores)]
+                return pair
+
+            def second_beside(current=current, pair=pair, total=total):
+                return update(total, pair[0], pair[1], current)
+
+            beside = [first_beside, second_beside]
+    own = weigh(0)
+    total = update(total, own, swap(own, cores), 0)
     return jnp.swapaxes(jnp.stack(solved), 1, 2), total
 
 

time: 80.6 us -> 69.1 us (0.86)
  waiting for transfers between devices: 41.3 us -> 29.6 us
  local copies, waits for them, and re-layouts: 5.25 us -> 1.39 us
  starting transfers between devices: 20.1 us -> 23.3 us
  Pallas kernels: 11.8 us -> 12.8 us
    ppermute x12 -> x15, waiting for transfers between devices: 41.1 us -> 27.9 us  [spread(): received.append(lax.ppermute(block, ('tc', 'pr'), pairs))]
    unnamed x24 -> x20, local copies, waits for them, and re-layouts: 5.25 us -> 0.05 us
    ppermute x12 -> x15, starting transfers between devices: 18.9 us -> 22.6 us  [spread(): received.append(lax.ppermute(block, ('tc', 'pr'), pairs))]
    ppermute x3 -> x4, waiting for transfers between devices: 0.17 us -> 1.64 us  [swap(): lax.ppermute(block, 'pr', [(core, cores - 1 - core) for core in range(cor...]
    squeeze x0 -> x1, local copies, waits for them, and re-layouts: none -> 1.34 us  [ahead(): right[entry]]
    pallas_call x8 -> x11, Pallas kernels: 11.8 us -> 12.8 us  [the longest x1 4.06 us: local(): call(first_kernel, [wide, narrow], [ANY, ANY, ANY], [pltpu.VMEM((size, si...]
  transfers between devices with their start and end apart: 15 -> 19, of which waited for: 12 -> 17; matrix products, arithmetic and copies ran while one was open for 1% -> 3% of each run, Pallas kernels for 12% -> 8%
where the time goes in v3:
time: 69.1 us; the launch traced here: 68.9 us
  waiting for transfers between devices  29.6 us (43%)
  starting transfers between devices  23.3 us (34%)
  Pallas kernels  12.8 us (19%)
  local copies, waits for them, and re-layouts  1.39 us (2%)
  other arithmetic  0.97 us (1%)
  between operations  0.89 us (1%)
    ppermute x15, waiting for transfers between devices, spread(): received.append(lax.ppermute(block, ('tc', 'pr'), pairs))  27.9 us
    ppermute x15, starting transfers between devices, spread(): received.append(lax.ppermute(block, ('tc', 'pr'), pairs))  22.6 us
    pallas_call x1, Pallas kernels, local(): call(first_kernel, [wide, narrow], [ANY, ANY, ANY], [pltpu.VMEM((size, si...  4.06 us
    pallas_call x3, Pallas kernels, weigh(): call(functools.partial(weights_kernel, pivots), [jax.ShapeDtypeStruct((ro...  3.07 us
    pallas_call x2, Pallas kernels, local(): call(functools.partial(step_kernel, current), [narrow] if last else [narr...  2.41 us
    pallas_call x3, Pallas kernels, update(): call(functools.partial(update_kernel, pivots), [jax.ShapeDtypeStruct(tota...  1.76 us
    ppermute x4, waiting for transfers between devices, swap(): lax.ppermute(block, 'pr', [(core, cores - 1 - core) for core in range(cor...  1.64 us
    pallas_call x2, Pallas kernels, ahead(): call(ahead_kernel, [jax.ShapeDtypeStruct((rank, size), jnp.bfloat16)], [V...  1.48 us
  transfers between devices with their start and end apart: 19, of which 17 were waited for; matrix products, arithmetic and copies ran while one was open for 3% of the time, Pallas kernels for 8%

profile of v3, /device:TPU:0, one launch (start us, length us, event | category | flops | bytes accessed | tf_op | source)
XLA Modules:
  0.0 68.9 jit_solution(14625818176618281619)
XLA Ops:
  0.6 4.1 %shard_map.113 = (f32[32,1536]{1,0:T(8,128)}, bf16[32,1536]{1,0:T(8,128)(2,1)}) custom-call(s32[3]{0:T(128)} %owner_ref.5, f32[32,1536]{1,0:T(8,128)} %bitcast.28, bf16[1536,1536]{1,0:T(8,128)(2,1)} %bitcast.19), custom_call_target="tpu_custom_call" | custom-call | flops 75497472 | bytes 2359296 | tf_op jit(solution)/shard_map/pallas_call | solution.py:202
  4.7 0.5 collective-permute-start.6
  5.2 2.7 %collective-permute-start = (bf16[32,1536]{1,0:T(8,128)(2,1)}, bf16[32,1536]{1,0:T(8,128)(2,1)S(1)}, u32[]{:S(2)}, u32[]{:S(2)}) collective-permute-start(bf16[32,1536]{1,0:T(8,128)(2,1)} %get-tuple-element.26), channel_id=1, source_target_pairs={{0,8},{1,17},{2,10},{3,19},{4,12},{5,21},{6,14},{7,23},{8,0},{9,25... | collective-permute-start | bytes 294920 | tf_op jit(solution)/shard_map/ppermute | solution.py:45
  7.9 1.3 %slice_bitcast_fusion = (bf16[200,1536]{1,0:T(8,128)(2,1)S(1)}, bf16[200,1536]{1,0:T(8,128)(2,1)S(1)}) fusion(bf16[2,200,1536]{2,1,0:T(8,128)(2,1)} %bitcast.27), kind=kLoop, calls=%fused_computation | loop fusion | bytes 2457600 | tf_op jit(solution)/shard_map/squeeze | solution.py:228
  9.2 0.7 %shard_map.114.refs_0_ = bf16[200,1536]{1,0:T(8,128)(2,1)S(1)} custom-call(bf16[200,1536]{1,0:T(8,128)(2,1)S(1)} %get-tuple-element.47.right_ref, bf16[1536,1536]{1,0:T(8,128)(2,1)S(1)} %bitcast.20), custom_call_target="tpu_custom_call" | custom-call | flops 471859200 | bytes 3588096 | tf_op jit(solution)/shard_map/pallas_call | solution.py:221
  10.0 1.7 %collective-permute-done = bf16[32,1536]{1,0:T(8,128)(2,1)S(1)} collective-permute-done((bf16[32,1536]{1,0:T(8,128)(2,1)}, bf16[32,1536]{1,0:T(8,128)(2,1)S(1)}, u32[]{:S(2)}, u32[]{:S(2)}) %collective-permute-start) | collective-permute-done | bytes 98336 | tf_op jit(solution)/shard_map/ppermute | solution.py:45
  11.8 2.4 %collective-permute-start.1 = (bf16[32,1536]{1,0:T(8,128)(2,1)S(1)}, bf16[32,1536]{1,0:T(8,128)(2,1)S(1)}, u32[]{:S(2)}, u32[]{:S(2)}) collective-permute-start(bf16[32,1536]{1,0:T(8,128)(2,1)S(1)} %add.45), channel_id=1, source_target_pairs={{0,16},{1,9},{2,18},{3,11},{4,20},{5,13},{6,22},{7,15},{8,24},{9,1... | collective-permute-start | bytes 294920 | tf_op jit(solution)/shard_map/ppermute | solution.py:45
  14.2 0.7 %shard_map.115.refs_1_ = bf16[200,1536]{1,0:T(8,128)(2,1)S(1)} custom-call(bf16[200,1536]{1,0:T(8,128)(2,1)S(1)} %get-tuple-element.46.right_ref, bf16[1536,1536]{1,0:T(8,128)(2,1)S(1)} %bitcast.21), custom_call_target="tpu_custom_call" | custom-call | flops 471859200 | bytes 3588096 | tf_op jit(solution)/shard_map/pallas_call | solution.py:221
  15.0 2.4 %collective-permute-done.1 = bf16[32,1536]{1,0:T(8,128)(2,1)S(1)} collective-permute-done((bf16[32,1536]{1,0:T(8,128)(2,1)S(1)}, bf16[32,1536]{1,0:T(8,128)(2,1)S(1)}, u32[]{:S(2)}, u32[]{:S(2)}) %collective-permute-start.1) | collective-permute-done | bytes 98336 | tf_op jit(solution)/shard_map/ppermute | solution.py:45
  17.4 3.5 %collective-permute-start.4 = (bf16[32,1536]{1,0:T(8,128)(2,1)S(1)}, bf16[32,1536]{1,0:T(8,128)(2,1)S(1)}, u32[]{:S(2)}, u32[]{:S(2)}) collective-permute-start(bf16[32,1536]{1,0:T(8,128)(2,1)S(1)} %add.46), channel_id=1, source_target_pairs={{0,6},{1,7},{2,4},{3,5},{4,2},{5,3},{6,0},{7,1},{8,14},{9,15},{10,... | collective-permute-start | bytes 294920 | tf_op jit(solution)/shard_map/ppermute | solution.py:45
  20.8 0.5 collective-permute-start.3
  21.3 0.1 collective-permute-start.2
  21.5 2.0 %collective-permute-done.4 = bf16[32,1536]{1,0:T(8,128)(2,1)S(1)} collective-permute-done((bf16[32,1536]{1,0:T(8,128)(2,1)S(1)}, bf16[32,1536]{1,0:T(8,128)(2,1)S(1)}, u32[]{:S(2)}, u32[]{:S(2)}) %collective-permute-start.4) | collective-permute-done | bytes 98336 | tf_op jit(solution)/shard_map/ppermute | solution.py:45
  23.4 2.0 %collective-permute-done.3 = bf16[32,1536]{1,0:T(8,128)(2,1)S(1)} collective-permute-done((bf16[32,1536]{1,0:T(8,128)(2,1)S(1)}, bf16[32,1536]{1,0:T(8,128)(2,1)S(1)}, u32[]{:S(2)}, u32[]{:S(2)}) %collective-permute-start.3) | collective-permute-done | bytes 98336 | tf_op jit(solution)/shard_map/ppermute | solution.py:45
  25.5 0.5 collective-permute-done.2
  26.0 1.2 %shard_map.116 = (bf16[32,1536]{1,0:T(8,128)(2,1)S(1)}, f32[32,1536]{1,0:T(8,128)S(1)}) custom-call(s32[3]{0:T(128)S(1)} %copy-done.7, s32[1,2]{1,0:T(1,128)S(1)} %copy-done.8, bf16[32,1536]{1,0:T(8,128)(2,1)S(1)} %add_add_fusion.2.solved_ref.refs_0_, bf16[2,200,1536]{2,1,0:T(8,128)(2,1)S(1)} %bitcast.22, bf16[200,1536]{1,0:T(8,128)(2,1)S(1)} %shard_map.114.refs_0_, ...), custom_call_target="tpu_custom_call" | custom-call | flops 39321600 | bytes 1228800 | tf_op jit(solution)/shard_map/pallas_call | solution.py:262
  27.3 1.3 %collective-permute-start.5 = (bf16[32,1536]{1,0:T(8,128)(2,1)S(1)}, bf16[32,1536]{1,0:T(8,128)(2,1)S(1)}, u32[]{:S(2)}, u32[]{:S(2)}) collective-permute-start(bf16[32,1536]{1,0:T(8,128)(2,1)S(1)} %get-tuple-element.35), channel_id=1, source_target_pairs={{0,8},{1,17},{2,10},{3,19},{4,12},{5,21},{6,14},{7,23},{8,0},{9,25... | collective-permute-start | bytes 294920 | tf_op jit(solution)/shard_map/ppermute | solution.py:45
  28.5 1.0 %shard_map.117.own_ref = bf16[2,1,32,200]{3,2,1,0:T(8,128)(2,1)S(1)} custom-call(s32[2,3]{1,0:T(2,128)S(1)} %copy-done.6, bf16[32,1536]{1,0:T(8,128)(2,1)S(1)} %add_add_fusion.2.solved_ref.refs_0_, bf16[2,3,200,768]{3,2,1,0:T(8,128)(2,1)S(1)} %copy-done.1, bf16[2,3,200,768]{3,2,1,0:T(8,128)(2,1)S(1)} %collective-permute-done.6.refs_2_), custom_call_target="tpu_custom_call" | custom-call | flops 39321600 | bytes 1228800 | tf_op jit(solution)/shard_map/pallas_call | solution.py:231
  29.6 0.1 collective-permute-start.7
  29.7 2.3 %collective-permute-done.5 = bf16[32,1536]{1,0:T(8,128)(2,1)S(1)} collective-permute-done((bf16[32,1536]{1,0:T(8,128)(2,1)S(1)}, bf16[32,1536]{1,0:T(8,128)(2,1)S(1)}, u32[]{:S(2)}, u32[]{:S(2)}) %collective-permute-start.5) | collective-permute-done | bytes 98336 | tf_op jit(solution)/shard_map/ppermute | solution.py:45
  32.0 2.0 %collective-permute-start.8 = (bf16[32,1536]{1,0:T(8,128)(2,1)S(1)}, bf16[32,1536]{1,0:T(8,128)(2,1)S(1)}, u32[]{:S(2)}, u32[]{:S(2)}) collective-permute-start(bf16[32,1536]{1,0:T(8,128)(2,1)S(1)} %add.50), channel_id=1, source_target_pairs={{0,16},{1,9},{2,18},{3,11},{4,20},{5,13},{6,22},{7,15},{8,24},{9,1... | collective-permute-start | bytes 294920 | tf_op jit(solution)/shard_map/ppermute | solution.py:45
  34.0 0.3 shard_map.118.rhs_ref
  34.3 4.3 %collective-permute-done.8 = bf16[32,1536]{1,0:T(8,128)(2,1)S(1)} collective-permute-done((bf16[32,1536]{1,0:T(8,128)(2,1)S(1)}, bf16[32,1536]{1,0:T(8,128)(2,1)S(1)}, u32[]{:S(2)}, u32[]{:S(2)}) %collective-permute-start.8) | collective-permute-done | bytes 98336 | tf_op jit(solution)/shard_map/ppermute | solution.py:45
  38.6 0.7 %collective-permute-start.11 = (bf16[32,1536]{1,0:T(8,128)(2,1)S(1)}, bf16[32,1536]{1,0:T(8,128)(2,1)S(1)}, u32[]{:S(2)}, u32[]{:S(2)}) collective-permute-start(bf16[32,1536]{1,0:T(8,128)(2,1)S(1)} %add.51), channel_id=1, source_target_pairs={{0,6},{1,7},{2,4},{3,5},{4,2},{5,3},{6,0},{7,1},{8,14},{9,15},{10,... | collective-permute-start | bytes 294920 | tf_op jit(solution)/shard_map/ppermute | solution.py:45
  39.4 0.9 %collective-permute-start.10 = (bf16[32,1536]{1,0:T(8,128)(2,1)S(1)}, bf16[32,1536]{1,0:T(8,128)(2,1)S(1)}, u32[]{:S(2)}, u32[]{:S(2)}) collective-permute-start(bf16[32,1536]{1,0:T(8,128)(2,1)S(1)} %add.51), channel_id=1, source_target_pairs={{0,4},{1,3},{2,6},{3,1},{4,0},{5,7},{6,2},{7,5},{8,12},{9,11},{10,... | collective-permute-start | bytes 294920 | tf_op jit(solution)/shard_map/ppermute | solution.py:45
  40.3 1.9 %collective-permute-start.9 = (bf16[32,1536]{1,0:T(8,128)(2,1)S(1)}, bf16[32,1536]{1,0:T(8,128)(2,1)S(1)}, u32[]{:S(2)}, u32[]{:S(2)}) collective-permute-start(bf16[32,1536]{1,0:T(8,128)(2,1)S(1)} %add.51), channel_id=1, source_target_pairs={{0,2},{1,5},{2,0},{3,7},{4,6},{5,1},{6,4},{7,3},{8,10},{9,13},{10,... | collective-permute-start | bytes 294920 | tf_op jit(solution)/shard_map/ppermute | solution.py:45
  42.2 2.1 %collective-permute-done.11 = bf16[32,1536]{1,0:T(8,128)(2,1)S(1)} collective-permute-done((bf16[32,1536]{1,0:T(8,128)(2,1)S(1)}, bf16[32,1536]{1,0:T(8,128)(2,1)S(1)}, u32[]{:S(2)}, u32[]{:S(2)}) %collective-permute-start.11) | collective-permute-done | bytes 98336 | tf_op jit(solution)/shard_map/ppermute | solution.py:45
  44.3 0.7 %collective-permute-done.10 = bf16[32,1536]{1,0:T(8,128)(2,1)S(1)} collective-permute-done((bf16[32,1536]{1,0:T(8,128)(2,1)S(1)}, bf16[32,1536]{1,0:T(8,128)(2,1)S(1)}, u32[]{:S(2)}, u32[]{:S(2)}) %collective-permute-start.10) | collective-permute-done | bytes 98336 | tf_op jit(solution)/shard_map/ppermute | solution.py:45
  45.0 0.3 collective-permute-done.9
  45.4 1.2 %shard_map.119 = bf16[32,1536]{1,0:T(8,128)(2,1)S(1)} custom-call(s32[3]{0:T(128)S(1)} %copy-done.7, s32[1,2]{1,0:T(1,128)S(1)} %copy-done.8, bf16[32,1536]{1,0:T(8,128)(2,1)S(1)} %add_add_fusion.1.solved_ref.refs_0_, bf16[2,200,1536]{2,1,0:T(8,128)(2,1)S(1)} %bitcast.23, bf16[200,1536]{1,0:T(8,128)(2,1)S(1)} %shard_map.114.refs_0_, ...), custom_call_target="tpu_custom_call" | custom-call | flops 39321600 | bytes 1228800 | tf_op jit(solution)/shard_map/pallas_call | solution.py:262
  46.6 1.2 %collective-permute-start.12 = (bf16[32,1536]{1,0:T(8,128)(2,1)S(1)}, bf16[32,1536]{1,0:T(8,128)(2,1)S(1)}, u32[]{:S(2)}, u32[]{:S(2)}) collective-permute-start(bf16[32,1536]{1,0:T(8,128)(2,1)S(1)} %shard_map.119), channel_id=1, source_target_pairs={{0,8},{1,17},{2,10},{3,19},{4,12},{5,21},{6,14},{7,23},{8,0},{9,25... | collective-permute-start | bytes 294920 | tf_op jit(solution)/shard_map/ppermute | solution.py:45
  47.8 1.0 %shard_map.120.own_ref = bf16[2,1,32,200]{3,2,1,0:T(8,128)(2,1)S(1)} custom-call(s32[2,3]{1,0:T(2,128)S(1)} %copy-done.6, bf16[32,1536]{1,0:T(8,128)(2,1)S(1)} %add_add_fusion.1.solved_ref.refs_0_, bf16[2,3,200,768]{3,2,1,0:T(8,128)(2,1)S(1)} %copy-done.1, bf16[2,3,200,768]{3,2,1,0:T(8,128)(2,1)S(1)} %collective-permute-done.6.refs_2_), custom_call_target="tpu_custom_call" | custom-call | flops 39321600 | bytes 1228800 | tf_op jit(solution)/shard_map/pallas_call | solution.py:231
  48.8 0.1 collective-permute-start.13
  48.9 1.2 %collective-permute-done.13.other_ref = bf16[2,1,32,200]{3,2,1,0:T(8,128)(2,1)S(1)} collective-permute-done((bf16[2,1,32,200]{3,2,1,0:T(8,128)(2,1)S(1)}, bf16[2,1,32,200]{3,2,1,0:T(8,128)(2,1)S(1)}, u32[]{:S(2)}, u32[]{:S(2)}) %collective-permute-start.13) | collective-permute-done | bytes 25632 | tf_op jit(solution)/shard_map/ppermute | solution.py:56
  50.1 1.2 %collective-permute-done.12 = bf16[32,1536]{1,0:T(8,128)(2,1)S(1)} collective-permute-done((bf16[32,1536]{1,0:T(8,128)(2,1)S(1)}, bf16[32,1536]{1,0:T(8,128)(2,1)S(1)}, u32[]{:S(2)}, u32[]{:S(2)}) %collective-permute-start.12) | collective-permute-done | bytes 98336 | tf_op jit(solution)/shard_map/ppermute | solution.py:45
  51.3 1.9 %collective-permute-start.14 = (bf16[32,1536]{1,0:T(8,128)(2,1)S(1)}, bf16[32,1536]{1,0:T(8,128)(2,1)S(1)}, u32[]{:S(2)}, u32[]{:S(2)}) collective-permute-start(bf16[32,1536]{1,0:T(8,128)(2,1)S(1)} %add.55), channel_id=1, source_target_pairs={{0,16},{1,9},{2,18},{3,11},{4,20},{5,13},{6,22},{7,15},{8,24},{9,1... | collective-permute-start | bytes 294920 | tf_op jit(solution)/shard_map/ppermute | solution.py:45
  53.2 0.3 shard_map.121.rhs_ref
  53.5 4.4 %collective-permute-done.14 = bf16[32,1536]{1,0:T(8,128)(2,1)S(1)} collective-permute-done((bf16[32,1536]{1,0:T(8,128)(2,1)S(1)}, bf16[32,1536]{1,0:T(8,128)(2,1)S(1)}, u32[]{:S(2)}, u32[]{:S(2)}) %collective-permute-start.14) | collective-permute-done | bytes 98336 | tf_op jit(solution)/shard_map/ppermute | solution.py:45
  58.0 2.4 %collective-permute-start.17 = (bf16[32,1536]{1,0:T(8,128)(2,1)S(1)}, bf16[32,1536]{1,0:T(8,128)(2,1)S(1)}, u32[]{:S(2)}, u32[]{:S(2)}) collective-permute-start(bf16[32,1536]{1,0:T(8,128)(2,1)S(1)} %add.56), channel_id=1, source_target_pairs={{0,6},{1,7},{2,4},{3,5},{4,2},{5,3},{6,0},{7,1},{8,14},{9,15},{10,... | collective-permute-start | bytes 294920 | tf_op jit(solution)/shard_map/ppermute | solution.py:45
  60.4 0.5 collective-permute-start.16
  60.9 0.7 collective-permute-start.15
  61.5 2.0 %collective-permute-done.17 = bf16[32,1536]{1,0:T(8,128)(2,1)S(1)} collective-permute-done((bf16[32,1536]{1,0:T(8,128)(2,1)S(1)}, bf16[32,1536]{1,0:T(8,128)(2,1)S(1)}, u32[]{:S(2)}, u32[]{:S(2)}) %collective-permute-start.17) | collective-permute-done | bytes 98336 | tf_op jit(solution)/shard_map/ppermute | solution.py:45
  63.6 1.4 %collective-permute-done.16 = bf16[32,1536]{1,0:T(8,128)(2,1)S(1)} collective-permute-done((bf16[32,1536]{1,0:T(8,128)(2,1)S(1)}, bf16[32,1536]{1,0:T(8,128)(2,1)S(1)}, u32[]{:S(2)}, u32[]{:S(2)}) %collective-permute-start.16) | collective-permute-done | bytes 98336 | tf_op jit(solution)/shard_map/ppermute | solution.py:45
  65.0 0.5 collective-permute-done.15
  65.5 1.0 %shard_map.122.own_ref = bf16[2,1,32,200]{3,2,1,0:T(8,128)(2,1)S(1)} custom-call(s32[2,3]{1,0:T(2,128)S(1)} %copy-done.6, bf16[32,1536]{1,0:T(8,128)(2,1)S(1)} %add_add_fusion.refs_0_, bf16[2,3,200,768]{3,2,1,0:T(8,128)(2,1)S(1)} %copy-done.1, bf16[2,3,200,768]{3,2,1,0:T(8,128)(2,1)S(1)} %collective-permute-done.6.refs_2_), custom_call_target="tpu_custom_call" | custom-call | flops 39321600 | bytes 1228800 | tf_op jit(solution)/shard_map/pallas_call | solution.py:231
  66.6 0.7 %maximum_bitcast_fusion = bf16[3,1536,32]{1,2,0:T(8,128)(2,1)} fusion(bf16[1,32,1536]{2,1,0:T(8,128)(2,1)S(1)} %bitcast.24, bf16[1,32,1536]{2,1,0:T(8,128)(2,1)S(1)} %bitcast.25, bf16[1,32,1536]{2,1,0:T(8,128)(2,1)S(1)} %bitcast.26), kind=kLoop, calls=%fused_computation.2 | loop fusion | flops 294912 | bytes 589824 | tf_op jit(solution)/shard_map/transpose | solution.py:285
  67.4 0.4 collective-permute-done.18.other_ref
  67.8 1.1 %shard_map.123 = f32[2,64,768]{2,1,0:T(8,128)} custom-call(bf16[2,1,32,200]{3,2,1,0:T(8,128)(2,1)S(1)} %shard_map.122.own_ref, bf16[2,1,32,200]{3,2,1,0:T(8,128)(2,1)S(1)} %collective-permute-done.18.other_ref, bf16[2,3,200,768]{3,2,1,0:T(8,128)(2,1)S(1)} %copy-done.2, f32[2,64,768]{2,1,0:T(8,128)S(1)} %shard_map.121.rhs_ref), custom_call_target="tpu_custom_call" | custom-call | flops 39321600 | bytes 1400832 | tf_op jit(solution)/shard_map/pallas_call | solution.py:241
  (32 shorter events, 0.3 us)
Async XLA Ops:
  0.6 8.6 %copy-start = (bf16[1,1536,1536]{2,1,0:T(8,128)(2,1)S(1)}, bf16[1,1536,1536]{2,1,0:T(8,128)(2,1)}, u32[]{:S(2)}) copy-start(bf16[1,1536,1536]{2,1,0:T(8,128)(2,1)} %param.11) | copy-start | bytes 14155780
  4.7 23.8 %collective-permute-start.6 = (bf16[2,3,200,768]{3,2,1,0:T(8,128)(2,1)}, bf16[2,3,200,768]{3,2,1,0:T(8,128)(2,1)S(1)}, u32[]{:S(2)}, u32[]{:S(2)}) collective-permute-start(bf16[2,3,200,768]{3,2,1,0:T(8,128)(2,1)} %refs_1_.2), channel_id=1, source_target_pairs={{0,1},{1,0},{2,3},{3,2},{4,5},{5,4},{6,7},{7,6},{8,9},{9,8},{10,11... | collective-permute-start | bytes 5529608 | tf_op jit(solution)/shard_map/ppermute | solution.py:56
  5.2 6.5 %collective-permute-start = (bf16[32,1536]{1,0:T(8,128)(2,1)}, bf16[32,1536]{1,0:T(8,128)(2,1)S(1)}, u32[]{:S(2)}, u32[]{:S(2)}) collective-permute-start(bf16[32,1536]{1,0:T(8,128)(2,1)} %get-tuple-element.26), channel_id=1, source_target_pairs={{0,8},{1,17},{2,10},{3,19},{4,12},{5,21},{6,14},{7,23},{8,0},{9,25... | collective-permute-start | bytes 294920 | tf_op jit(solution)/shard_map/ppermute | solution.py:45
  9.2 2.5 %copy-start.9 = (bf16[32,1536]{1,0:T(8,128)(2,1)S(1)}, bf16[32,1536]{1,0:T(8,128)(2,1)}, u32[]{:S(2)}) copy-start(bf16[32,1536]{1,0:T(8,128)(2,1)} %get-tuple-element.26) | copy-start | bytes 294916
  11.8 5.6 %collective-permute-start.1 = (bf16[32,1536]{1,0:T(8,128)(2,1)S(1)}, bf16[32,1536]{1,0:T(8,128)(2,1)S(1)}, u32[]{:S(2)}, u32[]{:S(2)}) collective-permute-start(bf16[32,1536]{1,0:T(8,128)(2,1)S(1)} %add.45), channel_id=1, source_target_pairs={{0,16},{1,9},{2,18},{3,11},{4,20},{5,13},{6,22},{7,15},{8,24},{9,1... | collective-permute-start | bytes 294920 | tf_op jit(solution)/shard_map/ppermute | solution.py:45
  14.2 11.8 %copy-start.3 = (bf16[1,2,1536,200]{2,3,1,0:T(8,128)(2,1)S(1)}, bf16[1,2,1536,200]{2,3,1,0:T(8,128)(2,1)}, u32[]{:S(2)}) copy-start(bf16[1,2,1536,200]{2,3,1,0:T(8,128)(2,1)} %param.13) | copy-start | bytes 3686404
  14.2 11.8 %copy-start.5 = (f32[32,1536]{1,0:T(8,128)S(1)}, f32[32,1536]{1,0:T(8,128)}, u32[]{:S(2)}) copy-start(f32[32,1536]{1,0:T(8,128)} %get-tuple-element.32.refs_2_) | copy-start | bytes 589828
  14.2 11.8 %copy-start.7 = (s32[3]{0:T(128)S(1)}, s32[3]{0:T(128)}, u32[]{:S(2)}) copy-start(s32[3]{0:T(128)} %owner_ref.5) | copy-start | bytes 40
  14.2 11.8 %copy-start.8 = (s32[1,2]{1,0:T(1,128)S(1)}, s32[1,2]{1,0:T(1,128)}, u32[]{:S(2)}) copy-start(s32[1,2]{1,0:T(1,128)} %ranks_ref.7) | copy-start | bytes 28
  15.0 13.6 %copy-start.1 = (bf16[2,3,200,768]{3,2,1,0:T(8,128)(2,1)S(1)}, bf16[2,3,200,768]{3,2,1,0:T(8,128)(2,1)}, u32[]{:S(2)}) copy-start(bf16[2,3,200,768]{3,2,1,0:T(8,128)(2,1)} %refs_1_.2) | copy-start | bytes 5529604
  15.0 13.6 %copy-start.6 = (s32[2,3]{1,0:T(2,128)S(1)}, s32[2,3]{1,0:T(2,128)}, u32[]{:S(2)}) copy-start(s32[2,3]{1,0:T(2,128)} %ranks_ref.9) | copy-start | bytes 76
  17.4 6.1 %collective-permute-start.4 = (bf16[32,1536]{1,0:T(8,128)(2,1)S(1)}, bf16[32,1536]{1,0:T(8,128)(2,1)S(1)}, u32[]{:S(2)}, u32[]{:S(2)}) collective-permute-start(bf16[32,1536]{1,0:T(8,128)(2,1)S(1)} %add.46), channel_id=1, source_target_pairs={{0,6},{1,7},{2,4},{3,5},{4,2},{5,3},{6,0},{7,1},{8,14},{9,15},{10,... | collective-permute-start | bytes 294920 | tf_op jit(solution)/shard_map/ppermute | solution.py:45
  20.8 4.6 %collective-permute-start.3 = (bf16[32,1536]{1,0:T(8,128)(2,1)S(1)}, bf16[32,1536]{1,0:T(8,128)(2,1)S(1)}, u32[]{:S(2)}, u32[]{:S(2)}) collective-permute-start(bf16[32,1536]{1,0:T(8,128)(2,1)S(1)} %add.46), channel_id=1, source_target_pairs={{0,4},{1,3},{2,6},{3,1},{4,0},{5,7},{6,2},{7,5},{8,12},{9,11},{10,... | collective-permute-start | bytes 294920 | tf_op jit(solution)/shard_map/ppermute | solution.py:45
  21.3 4.6 %collective-permute-start.2 = (bf16[32,1536]{1,0:T(8,128)(2,1)S(1)}, bf16[32,1536]{1,0:T(8,128)(2,1)S(1)}, u32[]{:S(2)}, u32[]{:S(2)}) collective-permute-start(bf16[32,1536]{1,0:T(8,128)(2,1)S(1)} %add.46), channel_id=1, source_target_pairs={{0,2},{1,5},{2,0},{3,7},{4,6},{5,1},{6,4},{7,3},{8,10},{9,13},{10,... | collective-permute-start | bytes 294920 | tf_op jit(solution)/shard_map/ppermute | solution.py:45
  27.2 6.7 %copy-start.2 = (bf16[2,3,200,768]{3,2,1,0:T(8,128)(2,1)S(1)}, bf16[2,3,200,768]{3,2,1,0:T(8,128)(2,1)}, u32[]{:S(2)}) copy-start(bf16[2,3,200,768]{3,2,1,0:T(8,128)(2,1)} %right_ref.5) | copy-start | bytes 5529604
  27.3 6.7 %copy-start.4 = (f32[2,64,768]{2,1,0:T(8,128)S(1)}, f32[2,64,768]{2,1,0:T(8,128)}, u32[]{:S(2)}) copy-start(f32[2,64,768]{2,1,0:T(8,128)} %rhs_ref.1) | copy-start | bytes 1179652
  27.3 4.7 %collective-permute-start.5 = (bf16[32,1536]{1,0:T(8,128)(2,1)S(1)}, bf16[32,1536]{1,0:T(8,128)(2,1)S(1)}, u32[]{:S(2)}, u32[]{:S(2)}) collective-permute-start(bf16[32,1536]{1,0:T(8,128)(2,1)S(1)} %get-tuple-element.35), channel_id=1, source_target_pairs={{0,8},{1,17},{2,10},{3,19},{4,12},{5,21},{6,14},{7,23},{8,0},{9,25... | collective-permute-start | bytes 294920 | tf_op jit(solution)/shard_map/ppermute | solution.py:45
  29.6 2.4 %collective-permute-start.7 = (bf16[2,1,32,200]{3,2,1,0:T(8,128)(2,1)S(1)}, bf16[2,1,32,200]{3,2,1,0:T(8,128)(2,1)S(1)}, u32[]{:S(2)}, u32[]{:S(2)}) collective-permute-start(bf16[2,1,32,200]{3,2,1,0:T(8,128)(2,1)S(1)} %shard_map.117.own_ref), channel_id=1, source_target_pairs={{0,1},{1,0},{2,3},{3,2},{4,5},{5,4},{6,7},{7,6},{8,9},{9,8},{10,11... | collective-permute-start | bytes 76808 | tf_op jit(solution)/shard_map/ppermute | solution.py:56
  32.0 6.6 %collective-permute-start.8 = (bf16[32,1536]{1,0:T(8,128)(2,1)S(1)}, bf16[32,1536]{1,0:T(8,128)(2,1)S(1)}, u32[]{:S(2)}, u32[]{:S(2)}) collective-permute-start(bf16[32,1536]{1,0:T(8,128)(2,1)S(1)} %add.50), channel_id=1, source_target_pairs={{0,16},{1,9},{2,18},{3,11},{4,20},{5,13},{6,22},{7,15},{8,24},{9,1... | collective-permute-start | bytes 294920 | tf_op jit(solution)/shard_map/ppermute | solution.py:45
  38.6 5.7 %collective-permute-start.11 = (bf16[32,1536]{1,0:T(8,128)(2,1)S(1)}, bf16[32,1536]{1,0:T(8,128)(2,1)S(1)}, u32[]{:S(2)}, u32[]{:S(2)}) collective-permute-start(bf16[32,1536]{1,0:T(8,128)(2,1)S(1)} %add.51), channel_id=1, source_target_pairs={{0,6},{1,7},{2,4},{3,5},{4,2},{5,3},{6,0},{7,1},{8,14},{9,15},{10,... | collective-permute-start | bytes 294920 | tf_op jit(solution)/shard_map/ppermute | solution.py:45
  39.4 5.7 %collective-permute-start.10 = (bf16[32,1536]{1,0:T(8,128)(2,1)S(1)}, bf16[32,1536]{1,0:T(8,128)(2,1)S(1)}, u32[]{:S(2)}, u32[]{:S(2)}) collective-permute-start(bf16[32,1536]{1,0:T(8,128)(2,1)S(1)} %add.51), channel_id=1, source_target_pairs={{0,4},{1,3},{2,6},{3,1},{4,0},{5,7},{6,2},{7,5},{8,12},{9,11},{10,... | collective-permute-start | bytes 294920 | tf_op jit(solution)/shard_map/ppermute | solution.py:45
  40.3 5.1 %collective-permute-start.9 = (bf16[32,1536]{1,0:T(8,128)(2,1)S(1)}, bf16[32,1536]{1,0:T(8,128)(2,1)S(1)}, u32[]{:S(2)}, u32[]{:S(2)}) collective-permute-start(bf16[32,1536]{1,0:T(8,128)(2,1)S(1)} %add.51), channel_id=1, source_target_pairs={{0,2},{1,5},{2,0},{3,7},{4,6},{5,1},{6,4},{7,3},{8,10},{9,13},{10,... | collective-permute-start | bytes 294920 | tf_op jit(solution)/shard_map/ppermute | solution.py:45
  46.6 4.7 %collective-permute-start.12 = (bf16[32,1536]{1,0:T(8,128)(2,1)S(1)}, bf16[32,1536]{1,0:T(8,128)(2,1)S(1)}, u32[]{:S(2)}, u32[]{:S(2)}) collective-permute-start(bf16[32,1536]{1,0:T(8,128)(2,1)S(1)} %shard_map.119), channel_id=1, source_target_pairs={{0,8},{1,17},{2,10},{3,19},{4,12},{5,21},{6,14},{7,23},{8,0},{9,25... | collective-permute-start | bytes 294920 | tf_op jit(solution)/shard_map/ppermute | solution.py:45
  48.8 1.3 %collective-permute-start.13 = (bf16[2,1,32,200]{3,2,1,0:T(8,128)(2,1)S(1)}, bf16[2,1,32,200]{3,2,1,0:T(8,128)(2,1)S(1)}, u32[]{:S(2)}, u32[]{:S(2)}) collective-permute-start(bf16[2,1,32,200]{3,2,1,0:T(8,128)(2,1)S(1)} %shard_map.120.own_ref), channel_id=1, source_target_pairs={{0,1},{1,0},{2,3},{3,2},{4,5},{5,4},{6,7},{7,6},{8,9},{9,8},{10,11... | collective-permute-start | bytes 76808 | tf_op jit(solution)/shard_map/ppermute | solution.py:56
  51.3 6.6 %collective-permute-start.14 = (bf16[32,1536]{1,0:T(8,128)(2,1)S(1)}, bf16[32,1536]{1,0:T(8,128)(2,1)S(1)}, u32[]{:S(2)}, u32[]{:S(2)}) collective-permute-start(bf16[32,1536]{1,0:T(8,128)(2,1)S(1)} %add.55), channel_id=1, source_target_pairs={{0,16},{1,9},{2,18},{3,11},{4,20},{5,13},{6,22},{7,15},{8,24},{9,1... | collective-permute-start | bytes 294920 | tf_op jit(solution)/shard_map/ppermute | solution.py:45
  58.0 5.6 %collective-permute-start.17 = (bf16[32,1536]{1,0:T(8,128)(2,1)S(1)}, bf16[32,1536]{1,0:T(8,128)(2,1)S(1)}, u32[]{:S(2)}, u32[]{:S(2)}) collective-permute-start(bf16[32,1536]{1,0:T(8,128)(2,1)S(1)} %add.56), channel_id=1, source_target_pairs={{0,6},{1,7},{2,4},{3,5},{4,2},{5,3},{6,0},{7,1},{8,14},{9,15},{10,... | collective-permute-start | bytes 294920 | tf_op jit(solution)/shard_map/ppermute | solution.py:45
  60.4 4.6 %collective-permute-start.16 = (bf16[32,1536]{1,0:T(8,128)(2,1)S(1)}, bf16[32,1536]{1,0:T(8,128)(2,1)S(1)}, u32[]{:S(2)}, u32[]{:S(2)}) collective-permute-start(bf16[32,1536]{1,0:T(8,128)(2,1)S(1)} %add.56), channel_id=1, source_target_pairs={{0,4},{1,3},{2,6},{3,1},{4,0},{5,7},{6,2},{7,5},{8,12},{9,11},{10,... | collective-permute-start | bytes 294920 | tf_op jit(solution)/shard_map/ppermute | solution.py:45
  60.9 4.6 %collective-permute-start.15 = (bf16[32,1536]{1,0:T(8,128)(2,1)S(1)}, bf16[32,1536]{1,0:T(8,128)(2,1)S(1)}, u32[]{:S(2)}, u32[]{:S(2)}) collective-permute-start(bf16[32,1536]{1,0:T(8,128)(2,1)S(1)} %add.56), channel_id=1, source_target_pairs={{0,2},{1,5},{2,0},{3,7},{4,6},{5,1},{6,4},{7,3},{8,10},{9,13},{10,... | collective-permute-start | bytes 294920 | tf_op jit(solution)/shard_map/ppermute | solution.py:45
  66.5 1.3 %collective-permute-start.18 = (bf16[2,1,32,200]{3,2,1,0:T(8,128)(2,1)S(1)}, bf16[2,1,32,200]{3,2,1,0:T(8,128)(2,1)S(1)}, u32[]{:S(2)}, u32[]{:S(2)}) collective-permute-start(bf16[2,1,32,200]{3,2,1,0:T(8,128)(2,1)S(1)} %shard_map.122.own_ref), channel_id=1, source_target_pairs={{0,1},{1,0},{2,3},{3,2},{4,5},{5,4},{6,7},{7,6},{8,9},{9,8},{10,11... | collective-permute-start | bytes 76808 | tf_op jit(solution)/shard_map/ppermute | solution.py:56

commit v4 on v3

--- a/solution.py
+++ b/solution.py
@@ -16,18 +16,15 @@
 
 def exchanges(slots):
     bits = [1 << place for place in range(slots.bit_length() - 1)]
-    steps = []
-    for place in range(2, len(bits), 2):
-        pair = bits[place : place + 2]
-        steps.append([(pair[0], pair[-1])])
-        if len(pair) == 2:
-            steps.append([(pair[1], pair[0])])
-    near = bits[:2]
-    if len(near) == 2:
-        steps.append([(near[0], near[1]), (near[1], near[0]), (near[0] | near[1],) * 2])
-    else:
-        steps += [[(bit, bit)] for bit in near]
-    return steps
+    groups = [
+        [bits[place], bits[place + 1], bits[place] | bits[place + 1]] if place + 1 < len(bits) else [bits[place]]
+        for place in range(0, len(bits), 2)
+    ]
+    others = list(groups)
+    for place in range(0, len(groups) - 1, 2):
+        if len(groups[place]) == len(groups[place + 1]):
+            others[place], others[place + 1] = groups[place + 1], groups[place]
+    return [list(zip(group, other)) for group, other in zip(groups, others)]
 
 
 def spread(block, slots, cores, beside=()):

time: 69.1 us -> 61.1 us (0.88)
  waiting for transfers between devices: 29.6 us -> 19.7 us
  starting transfers between devices: 23.3 us -> 25.4 us
    ppermute x15 -> x18, waiting for transfers between devices: 27.9 us -> 18 us  [spread(): received.append(lax.ppermute(block, ('tc', 'pr'), pairs))]
    ppermute x15 -> x18, starting transfers between devices: 22.6 us -> 24.6 us  [spread(): received.append(lax.ppermute(block, ('tc', 'pr'), pairs))]
  transfers between devices with their start and end apart: 19 -> 22, of which waited for: 17 -> 16; matrix products, arithmetic and copies ran while one was open for 3% -> 3% of each run, Pallas kernels for 8% -> 9%
where the time goes in v4:
time: 61.1 us; the launch traced here: 61 us
  starting transfers between devices  25.4 us (42%)
  waiting for transfers between devices  19.7 us (32%)
  Pallas kernels  12.8 us (21%)
  local copies, waits for them, and re-layouts  1.39 us (2%)
  other arithmetic  0.88 us (1%)
  between operations  0.88 us (1%)
    ppermute x18, starting transfers between devices, spread(): received.append(lax.ppermute(block, ('tc', 'pr'), pairs))  24.6 us
    ppermute x18, waiting for transfers between devices, spread(): received.append(lax.ppermute(block, ('tc', 'pr'), pairs))  18 us
    pallas_call x1, Pallas kernels, local(): call(first_kernel, [wide, narrow], [ANY, ANY, ANY], [pltpu.VMEM((size, si...  4.06 us
    pallas_call x3, Pallas kernels, weigh(): call(functools.partial(weights_kernel, pivots), [jax.ShapeDtypeStruct((ro...  3.06 us
    pallas_call x2, Pallas kernels, local(): call(functools.partial(step_kernel, current), [narrow] if last else [narr...  2.41 us
    pallas_call x3, Pallas kernels, update(): call(functools.partial(update_kernel, pivots), [jax.ShapeDtypeStruct(tota...  1.76 us
    ppermute x4, waiting for transfers between devices, swap(): lax.ppermute(block, 'pr', [(core, cores - 1 - core) for core in range(cor...  1.64 us
    pallas_call x2, Pallas kernels, ahead(): call(ahead_kernel, [jax.ShapeDtypeStruct((rank, size), jnp.bfloat16)], [V...  1.48 us
  transfers between devices with their start and end apart: 22, of which 16 were waited for; matrix products, arithmetic and copies ran while one was open for 3% of the time, Pallas kernels for 9%

profile of v4, /device:TPU:0, one launch (start us, length us, event | category | flops | bytes accessed | tf_op | source)
XLA Modules:
  0.0 61.0 jit_solution(12671931599815543114)
XLA Ops:
  0.6 4.1 %shard_map.113 = (f32[32,1536]{1,0:T(8,128)}, bf16[32,1536]{1,0:T(8,128)(2,1)}) custom-call(s32[3]{0:T(128)} %owner_ref.5, f32[32,1536]{1,0:T(8,128)} %bitcast.28, bf16[1536,1536]{1,0:T(8,128)(2,1)} %bitcast.19), custom_call_target="tpu_custom_call" | custom-call | flops 75497472 | bytes 2359296 | tf_op jit(solution)/shard_map/pallas_call | solution.py:199
  4.7 0.5 collective-permute-start.9
  5.2 3.5 %collective-permute-start.2 = (bf16[32,1536]{1,0:T(8,128)(2,1)}, bf16[32,1536]{1,0:T(8,128)(2,1)S(1)}, u32[]{:S(2)}, u32[]{:S(2)}) collective-permute-start(bf16[32,1536]{1,0:T(8,128)(2,1)} %get-tuple-element.38), channel_id=1, source_target_pairs={{0,6},{1,25},{2,4},{3,27},{4,2},{5,29},{6,0},{7,31},{8,14},{9,17},... | collective-permute-start | bytes 294920 | tf_op jit(solution)/shard_map/ppermute | solution.py:42
  8.7 0.5 collective-permute-start.1
  9.3 0.1 collective-permute-start
  9.4 1.3 %slice_bitcast_fusion = (bf16[200,1536]{1,0:T(8,128)(2,1)S(1)}, bf16[200,1536]{1,0:T(8,128)(2,1)S(1)}) fusion(bf16[2,200,1536]{2,1,0:T(8,128)(2,1)} %bitcast.27), kind=kLoop, calls=%fused_computation | loop fusion | bytes 2457600 | tf_op jit(solution)/shard_map/squeeze | solution.py:225
  10.8 0.7 %shard_map.114.refs_0_ = bf16[200,1536]{1,0:T(8,128)(2,1)S(1)} custom-call(bf16[200,1536]{1,0:T(8,128)(2,1)S(1)} %get-tuple-element.71.right_ref, bf16[1536,1536]{1,0:T(8,128)(2,1)S(1)} %bitcast.20), custom_call_target="tpu_custom_call" | custom-call | flops 471859200 | bytes 3588096 | tf_op jit(solution)/shard_map/pallas_call | solution.py:218
  11.6 2.0 %collective-permute-done.1 = bf16[32,1536]{1,0:T(8,128)(2,1)S(1)} collective-permute-done((bf16[32,1536]{1,0:T(8,128)(2,1)}, bf16[32,1536]{1,0:T(8,128)(2,1)S(1)}, u32[]{:S(2)}, u32[]{:S(2)}) %collective-permute-start.1) | collective-permute-done | bytes 98336 | tf_op jit(solution)/shard_map/ppermute | solution.py:42
  13.6 0.5 collective-permute-done
  14.1 3.7 %collective-permute-start.5 = (bf16[32,1536]{1,0:T(8,128)(2,1)S(1)}, bf16[32,1536]{1,0:T(8,128)(2,1)S(1)}, u32[]{:S(2)}, u32[]{:S(2)}) collective-permute-start(bf16[32,1536]{1,0:T(8,128)(2,1)S(1)} %add_add_fusion.5), channel_id=1, source_target_pairs={{0,24},{1,7},{2,26},{3,5},{4,28},{5,3},{6,30},{7,1},{8,16},{9,15},... | collective-permute-start | bytes 294920 | tf_op jit(solution)/shard_map/ppermute | solution.py:42
  17.8 0.8 %collective-permute-start.3 = (bf16[32,1536]{1,0:T(8,128)(2,1)S(1)}, bf16[32,1536]{1,0:T(8,128)(2,1)S(1)}, u32[]{:S(2)}, u32[]{:S(2)}) collective-permute-start(bf16[32,1536]{1,0:T(8,128)(2,1)S(1)} %add_add_fusion.5), channel_id=1, source_target_pairs={{0,8},{1,3},{2,10},{3,1},{4,12},{5,7},{6,14},{7,5},{8,0},{9,11},{1... | collective-permute-start | bytes 294920 | tf_op jit(solution)/shard_map/ppermute | solution.py:42
  18.6 0.7 %shard_map.115.refs_1_ = bf16[200,1536]{1,0:T(8,128)(2,1)S(1)} custom-call(bf16[200,1536]{1,0:T(8,128)(2,1)S(1)} %get-tuple-element.70.right_ref, bf16[1536,1536]{1,0:T(8,128)(2,1)S(1)} %bitcast.21), custom_call_target="tpu_custom_call" | custom-call | flops 471859200 | bytes 3588096 | tf_op jit(solution)/shard_map/pallas_call | solution.py:218
  19.4 1.3 %collective-permute-done.5 = bf16[32,1536]{1,0:T(8,128)(2,1)S(1)} collective-permute-done((bf16[32,1536]{1,0:T(8,128)(2,1)S(1)}, bf16[32,1536]{1,0:T(8,128)(2,1)S(1)}, u32[]{:S(2)}, u32[]{:S(2)}) %collective-permute-start.5) | collective-permute-done | bytes 98336 | tf_op jit(solution)/shard_map/ppermute | solution.py:42
  20.7 2.7 %collective-permute-done.4 = bf16[32,1536]{1,0:T(8,128)(2,1)S(1)} collective-permute-done((bf16[32,1536]{1,0:T(8,128)(2,1)S(1)}, bf16[32,1536]{1,0:T(8,128)(2,1)S(1)}, u32[]{:S(2)}, u32[]{:S(2)}) %collective-permute-start.4) | collective-permute-done | bytes 98336 | tf_op jit(solution)/shard_map/ppermute | solution.py:42
  23.5 1.2 %shard_map.116 = (bf16[32,1536]{1,0:T(8,128)(2,1)S(1)}, f32[32,1536]{1,0:T(8,128)S(1)}) custom-call(s32[3]{0:T(128)S(1)} %copy-done.7, s32[1,2]{1,0:T(1,128)S(1)} %copy-done.8, bf16[32,1536]{1,0:T(8,128)(2,1)S(1)} %add_add_fusion.4.solved_ref.refs_0_, bf16[2,200,1536]{2,1,0:T(8,128)(2,1)S(1)} %bitcast.22, bf16[200,1536]{1,0:T(8,128)(2,1)S(1)} %shard_map.114.refs_0_, ...), custom_call_target="tpu_custom_call" | custom-call | flops 39321600 | bytes 1228800 | tf_op jit(solution)/shard_map/pallas_call | solution.py:259
  24.8 1.6 %collective-permute-start.8 = (bf16[32,1536]{1,0:T(8,128)(2,1)S(1)}, bf16[32,1536]{1,0:T(8,128)(2,1)S(1)}, u32[]{:S(2)}, u32[]{:S(2)}) collective-permute-start(bf16[32,1536]{1,0:T(8,128)(2,1)S(1)} %get-tuple-element.51), channel_id=1, source_target_pairs={{0,6},{1,25},{2,4},{3,27},{4,2},{5,29},{6,0},{7,31},{8,14},{9,17},... | collective-permute-start | bytes 294920 | tf_op jit(solution)/shard_map/ppermute | solution.py:42
  26.3 0.6 collective-permute-start.7
  26.9 1.4 %collective-permute-start.6 = (bf16[32,1536]{1,0:T(8,128)(2,1)S(1)}, bf16[32,1536]{1,0:T(8,128)(2,1)S(1)}, u32[]{:S(2)}, u32[]{:S(2)}) collective-permute-start(bf16[32,1536]{1,0:T(8,128)(2,1)S(1)} %get-tuple-element.51), channel_id=1, source_target_pairs={{0,2},{1,9},{2,0},{3,11},{4,6},{5,13},{6,4},{7,15},{8,10},{9,1},{1... | collective-permute-start | bytes 294920 | tf_op jit(solution)/shard_map/ppermute | solution.py:42
  28.3 1.0 %shard_map.117.own_ref = bf16[2,1,32,200]{3,2,1,0:T(8,128)(2,1)S(1)} custom-call(s32[2,3]{1,0:T(2,128)S(1)} %copy-done.6, bf16[32,1536]{1,0:T(8,128)(2,1)S(1)} %add_add_fusion.4.solved_ref.refs_0_, bf16[2,3,200,768]{3,2,1,0:T(8,128)(2,1)S(1)} %copy-done.1, bf16[2,3,200,768]{3,2,1,0:T(8,128)(2,1)S(1)} %collective-permute-done.9.refs_2_), custom_call_target="tpu_custom_call" | custom-call | flops 39321600 | bytes 1228800 | tf_op jit(solution)/shard_map/pallas_call | solution.py:228
  29.4 0.1 collective-permute-start.10
  29.4 0.9 %collective-permute-done.8 = bf16[32,1536]{1,0:T(8,128)(2,1)S(1)} collective-permute-done((bf16[32,1536]{1,0:T(8,128)(2,1)S(1)}, bf16[32,1536]{1,0:T(8,128)(2,1)S(1)}, u32[]{:S(2)}, u32[]{:S(2)}) %collective-permute-start.8) | collective-permute-done | bytes 98336 | tf_op jit(solution)/shard_map/ppermute | solution.py:42
  30.4 1.0 %collective-permute-done.7 = bf16[32,1536]{1,0:T(8,128)(2,1)S(1)} collective-permute-done((bf16[32,1536]{1,0:T(8,128)(2,1)S(1)}, bf16[32,1536]{1,0:T(8,128)(2,1)S(1)}, u32[]{:S(2)}, u32[]{:S(2)}) %collective-permute-start.7) | collective-permute-done | bytes 98336 | tf_op jit(solution)/shard_map/ppermute | solution.py:42
  31.4 0.1 collective-permute-done.6
  31.5 2.2 %collective-permute-start.13 = (bf16[32,1536]{1,0:T(8,128)(2,1)S(1)}, bf16[32,1536]{1,0:T(8,128)(2,1)S(1)}, u32[]{:S(2)}, u32[]{:S(2)}) collective-permute-start(bf16[32,1536]{1,0:T(8,128)(2,1)S(1)} %add_add_fusion.3), channel_id=1, source_target_pairs={{0,24},{1,7},{2,26},{3,5},{4,28},{5,3},{6,30},{7,1},{8,16},{9,15},... | collective-permute-start | bytes 294920 | tf_op jit(solution)/shard_map/ppermute | solution.py:42
  33.8 0.4 collective-permute-start.12
  34.2 1.8 %collective-permute-start.11 = (bf16[32,1536]{1,0:T(8,128)(2,1)S(1)}, bf16[32,1536]{1,0:T(8,128)(2,1)S(1)}, u32[]{:S(2)}, u32[]{:S(2)}) collective-permute-start(bf16[32,1536]{1,0:T(8,128)(2,1)S(1)} %add_add_fusion.3), channel_id=1, source_target_pairs={{0,8},{1,3},{2,10},{3,1},{4,12},{5,7},{6,14},{7,5},{8,0},{9,11},{1... | collective-permute-start | bytes 294920 | tf_op jit(solution)/shard_map/ppermute | solution.py:42
  36.0 0.3 shard_map.118.rhs_ref
  36.3 1.7 %collective-permute-done.13 = bf16[32,1536]{1,0:T(8,128)(2,1)S(1)} collective-permute-done((bf16[32,1536]{1,0:T(8,128)(2,1)S(1)}, bf16[32,1536]{1,0:T(8,128)(2,1)S(1)}, u32[]{:S(2)}, u32[]{:S(2)}) %collective-permute-start.13) | collective-permute-done | bytes 98336 | tf_op jit(solution)/shard_map/ppermute | solution.py:42
  38.0 2.1 %collective-permute-done.12 = bf16[32,1536]{1,0:T(8,128)(2,1)S(1)} collective-permute-done((bf16[32,1536]{1,0:T(8,128)(2,1)S(1)}, bf16[32,1536]{1,0:T(8,128)(2,1)S(1)}, u32[]{:S(2)}, u32[]{:S(2)}) %collective-permute-start.12) | collective-permute-done | bytes 98336 | tf_op jit(solution)/shard_map/ppermute | solution.py:42
  40.1 1.2 %shard_map.119 = bf16[32,1536]{1,0:T(8,128)(2,1)S(1)} custom-call(s32[3]{0:T(128)S(1)} %copy-done.7, s32[1,2]{1,0:T(1,128)S(1)} %copy-done.8, bf16[32,1536]{1,0:T(8,128)(2,1)S(1)} %add_add_fusion.2.solved_ref.refs_0_, bf16[2,200,1536]{2,1,0:T(8,128)(2,1)S(1)} %bitcast.23, bf16[200,1536]{1,0:T(8,128)(2,1)S(1)} %shard_map.114.refs_0_, ...), custom_call_target="tpu_custom_call" | custom-call | flops 39321600 | bytes 1228800 | tf_op jit(solution)/shard_map/pallas_call | solution.py:259
  41.3 2.5 %collective-permute-start.16 = (bf16[32,1536]{1,0:T(8,128)(2,1)S(1)}, bf16[32,1536]{1,0:T(8,128)(2,1)S(1)}, u32[]{:S(2)}, u32[]{:S(2)}) collective-permute-start(bf16[32,1536]{1,0:T(8,128)(2,1)S(1)} %shard_map.119), channel_id=1, source_target_pairs={{0,6},{1,25},{2,4},{3,27},{4,2},{5,29},{6,0},{7,31},{8,14},{9,17},... | collective-permute-start | bytes 294920 | tf_op jit(solution)/shard_map/ppermute | solution.py:42
  43.8 0.5 collective-permute-start.15
  44.3 0.6 collective-permute-start.14
  44.9 1.0 %shard_map.120.own_ref = bf16[2,1,32,200]{3,2,1,0:T(8,128)(2,1)S(1)} custom-call(s32[2,3]{1,0:T(2,128)S(1)} %copy-done.6, bf16[32,1536]{1,0:T(8,128)(2,1)S(1)} %add_add_fusion.2.solved_ref.refs_0_, bf16[2,3,200,768]{3,2,1,0:T(8,128)(2,1)S(1)} %copy-done.1, bf16[2,3,200,768]{3,2,1,0:T(8,128)(2,1)S(1)} %collective-permute-done.9.refs_2_), custom_call_target="tpu_custom_call" | custom-call | flops 39321600 | bytes 1228800 | tf_op jit(solution)/shard_map/pallas_call | solution.py:228
  45.9 0.1 collective-permute-start.17
  46.0 1.2 %collective-permute-done.17.other_ref = bf16[2,1,32,200]{3,2,1,0:T(8,128)(2,1)S(1)} collective-permute-done((bf16[2,1,32,200]{3,2,1,0:T(8,128)(2,1)S(1)}, bf16[2,1,32,200]{3,2,1,0:T(8,128)(2,1)S(1)}, u32[]{:S(2)}, u32[]{:S(2)}) %collective-permute-start.17) | collective-permute-done | bytes 25632 | tf_op jit(solution)/shard_map/ppermute | solution.py:53
  47.2 1.2 %collective-permute-done.15 = bf16[32,1536]{1,0:T(8,128)(2,1)S(1)} collective-permute-done((bf16[32,1536]{1,0:T(8,128)(2,1)S(1)}, bf16[32,1536]{1,0:T(8,128)(2,1)S(1)}, u32[]{:S(2)}, u32[]{:S(2)}) %collective-permute-start.15) | collective-permute-done | bytes 98336 | tf_op jit(solution)/shard_map/ppermute | solution.py:42
  48.4 0.5 collective-permute-done.14
  48.9 2.2 %collective-permute-start.20 = (bf16[32,1536]{1,0:T(8,128)(2,1)S(1)}, bf16[32,1536]{1,0:T(8,128)(2,1)S(1)}, u32[]{:S(2)}, u32[]{:S(2)}) collective-permute-start(bf16[32,1536]{1,0:T(8,128)(2,1)S(1)} %add_add_fusion.1), channel_id=1, source_target_pairs={{0,24},{1,7},{2,26},{3,5},{4,28},{5,3},{6,30},{7,1},{8,16},{9,15},... | collective-permute-start | bytes 294920 | tf_op jit(solution)/shard_map/ppermute | solution.py:42
  51.2 2.2 %collective-permute-start.18 = (bf16[32,1536]{1,0:T(8,128)(2,1)S(1)}, bf16[32,1536]{1,0:T(8,128)(2,1)S(1)}, u32[]{:S(2)}, u32[]{:S(2)}) collective-permute-start(bf16[32,1536]{1,0:T(8,128)(2,1)S(1)} %add_add_fusion.1), channel_id=1, source_target_pairs={{0,8},{1,3},{2,10},{3,1},{4,12},{5,7},{6,14},{7,5},{8,0},{9,11},{1... | collective-permute-start | bytes 294920 | tf_op jit(solution)/shard_map/ppermute | solution.py:42
  53.4 0.3 shard_map.121.rhs_ref
  53.7 1.7 %collective-permute-done.20 = bf16[32,1536]{1,0:T(8,128)(2,1)S(1)} collective-permute-done((bf16[32,1536]{1,0:T(8,128)(2,1)S(1)}, bf16[32,1536]{1,0:T(8,128)(2,1)S(1)}, u32[]{:S(2)}, u32[]{:S(2)}) %collective-permute-start.20) | collective-permute-done | bytes 98336 | tf_op jit(solution)/shard_map/ppermute | solution.py:42
  55.5 2.1 %collective-permute-done.19 = bf16[32,1536]{1,0:T(8,128)(2,1)S(1)} collective-permute-done((bf16[32,1536]{1,0:T(8,128)(2,1)S(1)}, bf16[32,1536]{1,0:T(8,128)(2,1)S(1)}, u32[]{:S(2)}, u32[]{:S(2)}) %collective-permute-start.19) | collective-permute-done | bytes 98336 | tf_op jit(solution)/shard_map/ppermute | solution.py:42
  57.6 1.0 %shard_map.122.own_ref = bf16[2,1,32,200]{3,2,1,0:T(8,128)(2,1)S(1)} custom-call(s32[2,3]{1,0:T(2,128)S(1)} %copy-done.6, bf16[32,1536]{1,0:T(8,128)(2,1)S(1)} %add_add_fusion.refs_0_, bf16[2,3,200,768]{3,2,1,0:T(8,128)(2,1)S(1)} %copy-done.1, bf16[2,3,200,768]{3,2,1,0:T(8,128)(2,1)S(1)} %collective-permute-done.9.refs_2_), custom_call_target="tpu_custom_call" | custom-call | flops 39321600 | bytes 1228800 | tf_op jit(solution)/shard_map/pallas_call | solution.py:228
  58.6 0.1 collective-permute-start.21
  58.7 0.7 %maximum_bitcast_fusion = bf16[3,1536,32]{1,2,0:T(8,128)(2,1)} fusion(bf16[1,32,1536]{2,1,0:T(8,128)(2,1)S(1)} %bitcast.24, bf16[1,32,1536]{2,1,0:T(8,128)(2,1)S(1)} %bitcast.25, bf16[1,32,1536]{2,1,0:T(8,128)(2,1)S(1)} %bitcast.26), kind=kLoop, calls=%fused_computation.2 | loop fusion | flops 294912 | bytes 589824 | tf_op jit(solution)/shard_map/transpose | solution.py:282
  59.4 0.4 collective-permute-done.21.other_ref
  59.9 1.1 %shard_map.123 = f32[2,64,768]{2,1,0:T(8,128)} custom-call(bf16[2,1,32,200]{3,2,1,0:T(8,128)(2,1)S(1)} %shard_map.122.own_ref, bf16[2,1,32,200]{3,2,1,0:T(8,128)(2,1)S(1)} %collective-permute-done.21.other_ref, bf16[2,3,200,768]{3,2,1,0:T(8,128)(2,1)S(1)} %copy-done.2, f32[2,64,768]{2,1,0:T(8,128)S(1)} %shard_map.121.rhs_ref), custom_call_target="tpu_custom_call" | custom-call | flops 39321600 | bytes 1400832 | tf_op jit(solution)/shard_map/pallas_call | solution.py:238
  (35 shorter events, 0.3 us)
Async XLA Ops:
  0.6 10.1 %copy-start = (bf16[1,1536,1536]{2,1,0:T(8,128)(2,1)S(1)}, bf16[1,1536,1536]{2,1,0:T(8,128)(2,1)}, u32[]{:S(2)}) copy-start(bf16[1,1536,1536]{2,1,0:T(8,128)(2,1)} %param.11) | copy-start | bytes 14155780
  4.7 23.6 %collective-permute-start.9 = (bf16[2,3,200,768]{3,2,1,0:T(8,128)(2,1)}, bf16[2,3,200,768]{3,2,1,0:T(8,128)(2,1)S(1)}, u32[]{:S(2)}, u32[]{:S(2)}) collective-permute-start(bf16[2,3,200,768]{3,2,1,0:T(8,128)(2,1)} %refs_1_.2), channel_id=1, source_target_pairs={{0,1},{1,0},{2,3},{3,2},{4,5},{5,4},{6,7},{7,6},{8,9},{9,8},{10,11... | collective-permute-start | bytes 5529608 | tf_op jit(solution)/shard_map/ppermute | solution.py:53
  5.2 6.3 %collective-permute-start.2 = (bf16[32,1536]{1,0:T(8,128)(2,1)}, bf16[32,1536]{1,0:T(8,128)(2,1)S(1)}, u32[]{:S(2)}, u32[]{:S(2)}) collective-permute-start(bf16[32,1536]{1,0:T(8,128)(2,1)} %get-tuple-element.38), channel_id=1, source_target_pairs={{0,6},{1,25},{2,4},{3,27},{4,2},{5,29},{6,0},{7,31},{8,14},{9,17},... | collective-permute-start | bytes 294920 | tf_op jit(solution)/shard_map/ppermute | solution.py:42
  8.7 4.8 %collective-permute-start.1 = (bf16[32,1536]{1,0:T(8,128)(2,1)}, bf16[32,1536]{1,0:T(8,128)(2,1)S(1)}, u32[]{:S(2)}, u32[]{:S(2)}) collective-permute-start(bf16[32,1536]{1,0:T(8,128)(2,1)} %get-tuple-element.38), channel_id=1, source_target_pairs={{0,4},{1,17},{2,6},{3,19},{4,0},{5,21},{6,2},{7,23},{8,12},{9,25},... | collective-permute-start | bytes 294920 | tf_op jit(solution)/shard_map/ppermute | solution.py:42
  9.3 4.8 %collective-permute-start = (bf16[32,1536]{1,0:T(8,128)(2,1)}, bf16[32,1536]{1,0:T(8,128)(2,1)S(1)}, u32[]{:S(2)}, u32[]{:S(2)}) collective-permute-start(bf16[32,1536]{1,0:T(8,128)(2,1)} %get-tuple-element.38), channel_id=1, source_target_pairs={{0,2},{1,9},{2,0},{3,11},{4,6},{5,13},{6,4},{7,15},{8,10},{9,1},{1... | collective-permute-start | bytes 294920 | tf_op jit(solution)/shard_map/ppermute | solution.py:42
  10.7 3.3 %copy-start.9 = (bf16[32,1536]{1,0:T(8,128)(2,1)S(1)}, bf16[32,1536]{1,0:T(8,128)(2,1)}, u32[]{:S(2)}) copy-start(bf16[32,1536]{1,0:T(8,128)(2,1)} %get-tuple-element.38) | copy-start | bytes 294916
  14.1 6.6 %collective-permute-start.5 = (bf16[32,1536]{1,0:T(8,128)(2,1)S(1)}, bf16[32,1536]{1,0:T(8,128)(2,1)S(1)}, u32[]{:S(2)}, u32[]{:S(2)}) collective-permute-start(bf16[32,1536]{1,0:T(8,128)(2,1)S(1)} %add_add_fusion.5), channel_id=1, source_target_pairs={{0,24},{1,7},{2,26},{3,5},{4,28},{5,3},{6,30},{7,1},{8,16},{9,15},... | collective-permute-start | bytes 294920 | tf_op jit(solution)/shard_map/ppermute | solution.py:42
  17.8 5.7 %collective-permute-start.4 = (bf16[32,1536]{1,0:T(8,128)(2,1)S(1)}, bf16[32,1536]{1,0:T(8,128)(2,1)S(1)}, u32[]{:S(2)}, u32[]{:S(2)}) collective-permute-start(bf16[32,1536]{1,0:T(8,128)(2,1)S(1)} %add_add_fusion.5), channel_id=1, source_target_pairs={{0,16},{1,5},{2,18},{3,7},{4,20},{5,1},{6,22},{7,3},{8,24},{9,13},... | collective-permute-start | bytes 294920 | tf_op jit(solution)/shard_map/ppermute | solution.py:42
  17.8 5.7 %collective-permute-start.3 = (bf16[32,1536]{1,0:T(8,128)(2,1)S(1)}, bf16[32,1536]{1,0:T(8,128)(2,1)S(1)}, u32[]{:S(2)}, u32[]{:S(2)}) collective-permute-start(bf16[32,1536]{1,0:T(8,128)(2,1)S(1)} %add_add_fusion.5), channel_id=1, source_target_pairs={{0,8},{1,3},{2,10},{3,1},{4,12},{5,7},{6,14},{7,5},{8,0},{9,11},{1... | collective-permute-start | bytes 294920 | tf_op jit(solution)/shard_map/ppermute | solution.py:42
  18.6 4.9 %copy-start.3 = (bf16[1,2,1536,200]{2,3,1,0:T(8,128)(2,1)S(1)}, bf16[1,2,1536,200]{2,3,1,0:T(8,128)(2,1)}, u32[]{:S(2)}) copy-start(bf16[1,2,1536,200]{2,3,1,0:T(8,128)(2,1)} %param.13) | copy-start | bytes 3686404
  18.6 4.9 %copy-start.5 = (f32[32,1536]{1,0:T(8,128)S(1)}, f32[32,1536]{1,0:T(8,128)}, u32[]{:S(2)}) copy-start(f32[32,1536]{1,0:T(8,128)} %get-tuple-element.48.refs_2_) | copy-start | bytes 589828
  18.6 4.9 %copy-start.7 = (s32[3]{0:T(128)S(1)}, s32[3]{0:T(128)}, u32[]{:S(2)}) copy-start(s32[3]{0:T(128)} %owner_ref.5) | copy-start | bytes 40
  18.6 4.9 %copy-start.8 = (s32[1,2]{1,0:T(1,128)S(1)}, s32[1,2]{1,0:T(1,128)}, u32[]{:S(2)}) copy-start(s32[1,2]{1,0:T(1,128)} %ranks_ref.7) | copy-start | bytes 28
  19.3 9.0 %copy-start.1 = (bf16[2,3,200,768]{3,2,1,0:T(8,128)(2,1)S(1)}, bf16[2,3,200,768]{3,2,1,0:T(8,128)(2,1)}, u32[]{:S(2)}) copy-start(bf16[2,3,200,768]{3,2,1,0:T(8,128)(2,1)} %refs_1_.2) | copy-start | bytes 5529604
  19.3 9.0 %copy-start.6 = (s32[2,3]{1,0:T(2,128)S(1)}, s32[2,3]{1,0:T(2,128)}, u32[]{:S(2)}) copy-start(s32[2,3]{1,0:T(2,128)} %ranks_ref.9) | copy-start | bytes 76
  24.7 11.2 %copy-start.2 = (bf16[2,3,200,768]{3,2,1,0:T(8,128)(2,1)S(1)}, bf16[2,3,200,768]{3,2,1,0:T(8,128)(2,1)}, u32[]{:S(2)}) copy-start(bf16[2,3,200,768]{3,2,1,0:T(8,128)(2,1)} %right_ref.5) | copy-start | bytes 5529604
  24.7 11.2 %copy-start.4 = (f32[2,64,768]{2,1,0:T(8,128)S(1)}, f32[2,64,768]{2,1,0:T(8,128)}, u32[]{:S(2)}) copy-start(f32[2,64,768]{2,1,0:T(8,128)} %rhs_ref.1) | copy-start | bytes 1179652
  24.8 5.6 %collective-permute-start.8 = (bf16[32,1536]{1,0:T(8,128)(2,1)S(1)}, bf16[32,1536]{1,0:T(8,128)(2,1)S(1)}, u32[]{:S(2)}, u32[]{:S(2)}) collective-permute-start(bf16[32,1536]{1,0:T(8,128)(2,1)S(1)} %get-tuple-element.51), channel_id=1, source_target_pairs={{0,6},{1,25},{2,4},{3,27},{4,2},{5,29},{6,0},{7,31},{8,14},{9,17},... | collective-permute-start | bytes 294920 | tf_op jit(solution)/shard_map/ppermute | solution.py:42
  26.3 5.1 %collective-permute-start.7 = (bf16[32,1536]{1,0:T(8,128)(2,1)S(1)}, bf16[32,1536]{1,0:T(8,128)(2,1)S(1)}, u32[]{:S(2)}, u32[]{:S(2)}) collective-permute-start(bf16[32,1536]{1,0:T(8,128)(2,1)S(1)} %get-tuple-element.51), channel_id=1, source_target_pairs={{0,4},{1,17},{2,6},{3,19},{4,0},{5,21},{6,2},{7,23},{8,12},{9,25},... | collective-permute-start | bytes 294920 | tf_op jit(solution)/shard_map/ppermute | solution.py:42
  26.9 4.6 %collective-permute-start.6 = (bf16[32,1536]{1,0:T(8,128)(2,1)S(1)}, bf16[32,1536]{1,0:T(8,128)(2,1)S(1)}, u32[]{:S(2)}, u32[]{:S(2)}) collective-permute-start(bf16[32,1536]{1,0:T(8,128)(2,1)S(1)} %get-tuple-element.51), channel_id=1, source_target_pairs={{0,2},{1,9},{2,0},{3,11},{4,6},{5,13},{6,4},{7,15},{8,10},{9,1},{1... | collective-permute-start | bytes 294920 | tf_op jit(solution)/shard_map/ppermute | solution.py:42
  29.4 2.1 %collective-permute-start.10 = (bf16[2,1,32,200]{3,2,1,0:T(8,128)(2,1)S(1)}, bf16[2,1,32,200]{3,2,1,0:T(8,128)(2,1)S(1)}, u32[]{:S(2)}, u32[]{:S(2)}) collective-permute-start(bf16[2,1,32,200]{3,2,1,0:T(8,128)(2,1)S(1)} %shard_map.117.own_ref), channel_id=1, source_target_pairs={{0,1},{1,0},{2,3},{3,2},{4,5},{5,4},{6,7},{7,6},{8,9},{9,8},{10,11... | collective-permute-start | bytes 76808 | tf_op jit(solution)/shard_map/ppermute | solution.py:53
  31.5 6.5 %collective-permute-start.13 = (bf16[32,1536]{1,0:T(8,128)(2,1)S(1)}, bf16[32,1536]{1,0:T(8,128)(2,1)S(1)}, u32[]{:S(2)}, u32[]{:S(2)}) collective-permute-start(bf16[32,1536]{1,0:T(8,128)(2,1)S(1)} %add_add_fusion.3), channel_id=1, source_target_pairs={{0,24},{1,7},{2,26},{3,5},{4,28},{5,3},{6,30},{7,1},{8,16},{9,15},... | collective-permute-start | bytes 294920 | tf_op jit(solution)/shard_map/ppermute | solution.py:42
  33.8 6.3 %collective-permute-start.12 = (bf16[32,1536]{1,0:T(8,128)(2,1)S(1)}, bf16[32,1536]{1,0:T(8,128)(2,1)S(1)}, u32[]{:S(2)}, u32[]{:S(2)}) collective-permute-start(bf16[32,1536]{1,0:T(8,128)(2,1)S(1)} %add_add_fusion.3), channel_id=1, source_target_pairs={{0,16},{1,5},{2,18},{3,7},{4,20},{5,1},{6,22},{7,3},{8,24},{9,13},... | collective-permute-start | bytes 294920 | tf_op jit(solution)/shard_map/ppermute | solution.py:42
  34.2 6.0 %collective-permute-start.11 = (bf16[32,1536]{1,0:T(8,128)(2,1)S(1)}, bf16[32,1536]{1,0:T(8,128)(2,1)S(1)}, u32[]{:S(2)}, u32[]{:S(2)}) collective-permute-start(bf16[32,1536]{1,0:T(8,128)(2,1)S(1)} %add_add_fusion.3), channel_id=1, source_target_pairs={{0,8},{1,3},{2,10},{3,1},{4,12},{5,7},{6,14},{7,5},{8,0},{9,11},{1... | collective-permute-start | bytes 294920 | tf_op jit(solution)/shard_map/ppermute | solution.py:42
  41.3 5.9 %collective-permute-start.16 = (bf16[32,1536]{1,0:T(8,128)(2,1)S(1)}, bf16[32,1536]{1,0:T(8,128)(2,1)S(1)}, u32[]{:S(2)}, u32[]{:S(2)}) collective-permute-start(bf16[32,1536]{1,0:T(8,128)(2,1)S(1)} %shard_map.119), channel_id=1, source_target_pairs={{0,6},{1,25},{2,4},{3,27},{4,2},{5,29},{6,0},{7,31},{8,14},{9,17},... | collective-permute-start | bytes 294920 | tf_op jit(solution)/shard_map/ppermute | solution.py:42
  43.8 4.6 %collective-permute-start.15 = (bf16[32,1536]{1,0:T(8,128)(2,1)S(1)}, bf16[32,1536]{1,0:T(8,128)(2,1)S(1)}, u32[]{:S(2)}, u32[]{:S(2)}) collective-permute-start(bf16[32,1536]{1,0:T(8,128)(2,1)S(1)} %shard_map.119), channel_id=1, source_target_pairs={{0,4},{1,17},{2,6},{3,19},{4,0},{5,21},{6,2},{7,23},{8,12},{9,25},... | collective-permute-start | bytes 294920 | tf_op jit(solution)/shard_map/ppermute | solution.py:42
  44.3 4.6 %collective-permute-start.14 = (bf16[32,1536]{1,0:T(8,128)(2,1)S(1)}, bf16[32,1536]{1,0:T(8,128)(2,1)S(1)}, u32[]{:S(2)}, u32[]{:S(2)}) collective-permute-start(bf16[32,1536]{1,0:T(8,128)(2,1)S(1)} %shard_map.119), channel_id=1, source_target_pairs={{0,2},{1,9},{2,0},{3,11},{4,6},{5,13},{6,4},{7,15},{8,10},{9,1},{1... | collective-permute-start | bytes 294920 | tf_op jit(solution)/shard_map/ppermute | solution.py:42
  45.9 1.3 %collective-permute-start.17 = (bf16[2,1,32,200]{3,2,1,0:T(8,128)(2,1)S(1)}, bf16[2,1,32,200]{3,2,1,0:T(8,128)(2,1)S(1)}, u32[]{:S(2)}, u32[]{:S(2)}) collective-permute-start(bf16[2,1,32,200]{3,2,1,0:T(8,128)(2,1)S(1)} %shard_map.120.own_ref), channel_id=1, source_target_pairs={{0,1},{1,0},{2,3},{3,2},{4,5},{5,4},{6,7},{7,6},{8,9},{9,8},{10,11... | collective-permute-start | bytes 76808 | tf_op jit(solution)/shard_map/ppermute | solution.py:53
  48.9 6.5 %collective-permute-start.20 = (bf16[32,1536]{1,0:T(8,128)(2,1)S(1)}, bf16[32,1536]{1,0:T(8,128)(2,1)S(1)}, u32[]{:S(2)}, u32[]{:S(2)}) collective-permute-start(bf16[32,1536]{1,0:T(8,128)(2,1)S(1)} %add_add_fusion.1), channel_id=1, source_target_pairs={{0,24},{1,7},{2,26},{3,5},{4,28},{5,3},{6,30},{7,1},{8,16},{9,15},... | collective-permute-start | bytes 294920 | tf_op jit(solution)/shard_map/ppermute | solution.py:42
  51.2 6.3 %collective-permute-start.19 = (bf16[32,1536]{1,0:T(8,128)(2,1)S(1)}, bf16[32,1536]{1,0:T(8,128)(2,1)S(1)}, u32[]{:S(2)}, u32[]{:S(2)}) collective-permute-start(bf16[32,1536]{1,0:T(8,128)(2,1)S(1)} %add_add_fusion.1), channel_id=1, source_target_pairs={{0,16},{1,5},{2,18},{3,7},{4,20},{5,1},{6,22},{7,3},{8,24},{9,13},... | collective-permute-start | bytes 294920 | tf_op jit(solution)/shard_map/ppermute | solution.py:42
  51.2 6.3 %collective-permute-start.18 = (bf16[32,1536]{1,0:T(8,128)(2,1)S(1)}, bf16[32,1536]{1,0:T(8,128)(2,1)S(1)}, u32[]{:S(2)}, u32[]{:S(2)}) collective-permute-start(bf16[32,1536]{1,0:T(8,128)(2,1)S(1)} %add_add_fusion.1), channel_id=1, source_target_pairs={{0,8},{1,3},{2,10},{3,1},{4,12},{5,7},{6,14},{7,5},{8,0},{9,11},{1... | collective-permute-start | bytes 294920 | tf_op jit(solution)/shard_map/ppermute | solution.py:42
  58.6 1.3 %collective-permute-start.21 = (bf16[2,1,32,200]{3,2,1,0:T(8,128)(2,1)S(1)}, bf16[2,1,32,200]{3,2,1,0:T(8,128)(2,1)S(1)}, u32[]{:S(2)}, u32[]{:S(2)}) collective-permute-start(bf16[2,1,32,200]{3,2,1,0:T(8,128)(2,1)S(1)} %shard_map.122.own_ref), channel_id=1, source_target_pairs={{0,1},{1,0},{2,3},{3,2},{4,5},{5,4},{6,7},{7,6},{8,9},{9,8},{10,11... | collective-permute-start | bytes 76808 | tf_op jit(solution)/shard_map/ppermute | solution.py:53

commit v5 on v4

v5 whole, which is shorter than its diff:
```python
import functools

import jax
import jax.numpy as jnp
from jax import lax
from jax.experimental import pallas as pl
from jax.experimental.pallas import tpu as pltpu
from jax.sharding import PartitionSpec as P

SMEM = pl.BlockSpec(memory_space=pltpu.SMEM)
VMEM = pl.BlockSpec(memory_space=pltpu.VMEM)
ANY = pl.BlockSpec(memory_space=pl.ANY)
MIB = 1 << 20
FIRST_LIMIT = 56


def exchanges(slots):
    bits = [1 << place for place in range(slots.bit_length() - 1)]
    groups = [
        [bits[place], bits[place + 1], bits[place] | bits[place + 1]] if place + 1 < len(bits) else [bits[place]]
        for place in range(0, len(bits), 2)
    ]
    others = list(groups)
    for place in range(0, len(groups) - 1, 2):
        if len(groups[place]) == len(groups[place + 1]):
            others[place], others[place + 1] = groups[place + 1], groups[place]
    return [list(zip(group, other)) for group, other in zip(groups, others)]


def spread(block, slots, cores, turn, beside=()):
    if slots & (slots - 1):
        for work in beside:
            work()
        return lax.psum(block, "tc")
    beside = list(beside)
    for flips in exchanges(slots):
        received = []
        for flip in flips:
            pairs = [
                (slot * cores + core, (slot ^ flip[(core + turn) % 2]) * cores + core)
                for slot in range(slots)
                for core in range(cores)
            ]
            received.append(lax.ppermute(block, ("tc", "pr"), pairs))
        if beside:
            block, received, _ = lax.optimization_barrier((block, received, beside.pop(0)()))
        for part in received:
            block = block + part
    for work in beside:
        work()
    return block


def swap(block, cores):
    return lax.ppermute(block, "pr", [(core, cores - 1 - core) for core in range(cores)])


def block_width(size):
    return 256 if size % 256 == 0 else size


def start_triangle(inverse_ref, buffer, sems):
    size = inverse_ref.shape[0]
    width = block_width(size)
    copies = []
    for place in range(size // width):
        first = place * width
        part = (pl.ds(first, width), pl.ds(0, first + width))
        copies.append(pltpu.make_async_copy(inverse_ref.at[part], buffer.at[part], sems.at[place]))
    for copy in copies:
        copy.start()
    return copies, width


def first_kernel(owner_ref, rhs_ref, inverse_ref, raw_ref, block_ref, buffer, sems, rhs, owner, more_sems):
    fetch_rhs = pltpu.make_async_copy(rhs_ref, rhs, more_sems.at[0])
    fetch_owner = pltpu.make_async_copy(owner_ref, owner, more_sems.at[1])
    fetch_rhs.start()
    fetch_owner.start()
    copies, width = start_triangle(inverse_ref, buffer, sems)
    fetch_rhs.wait()
    fetch_owner.wait()
    is_root = owner[owner.shape[0] - 1] == lax.axis_index("tc")
    pivot_in = rhs[...].astype(jnp.bfloat16)
    for place, copy in enumerate(copies):
        first = place * width
        copy.wait()
        raw = jnp.dot(
            pivot_in[:, first : first + width], buffer[first : first + width, : first + width], preferred_element_type=jnp.float32
        )
        if place:
            raw_ref[:, :first] += raw[:, :first]
        raw_ref[:, first : first + width] = raw[:, first:]
    block_ref[...] = jnp.where(is_root, raw_ref[...], 0.0).astype(jnp.bfloat16)


def ahead_kernel(
    current, owner_ref, ranks_ref, right_ref, left_ref, inverse_ref, ahead_ref, turned_ref, flag_ref
):
    me = lax.axis_index("tc")
    own = jnp.int32(current)
    for place in range(owner_ref.shape[0]):
        own = jnp.where(owner_ref[place] == me, jnp.int32(place), own)
    entry = jnp.clip(current - own - 1, 0, right_ref.shape[0] - 1)
    limit = jnp.where(own < current, ranks_ref[0, entry], 0)
    size = inverse_ref.shape[0]
    width = block_width(size)
    keep = lax.broadcasted_iota(jnp.int32, (right_ref.shape[1], width), 0) < limit
    for first in range(0, size, width):
        product = jnp.dot(
            right_ref[entry, :, first:], inverse_ref[first:, first : first + width], preferred_element_type=jnp.float32
        )
        ahead_ref[:, first : first + width] = jnp.where(keep, product, 0.0).astype(jnp.bfloat16)
    turned_ref[...] = left_ref[entry].T
    flag_ref[...] = jnp.full(flag_ref.shape, jnp.where(owner_ref[current - 1] == me, 1.0, 0.0), jnp.float32)


def mask_kernel(ranks_ref, right_ref, out_ref):
    rank_ids = lax.broadcasted_iota(jnp.int32, right_ref.shape[2:], 0)
    for row in range(right_ref.shape[0]):
        for pivot in range(right_ref.shape[1]):
            tile = right_ref[row, pivot].astype(jnp.float32)
            out_ref[row, pivot] = jnp.where(rank_ids < ranks_ref[row, pivot], tile, 0.0).astype(jnp.bfloat16)


def step_kernel(solved_ref, ahead_ref, turned_ref, flag_ref, raw_ref, *outs):
    factor = jnp.dot(solved_ref[...], turned_ref[...], preferred_element_type=jnp.float32).astype(jnp.bfloat16)
    raw = raw_ref[...] - jnp.dot(factor, ahead_ref[...], preferred_element_type=jnp.float32)
    outs[0][...] = jnp.where(flag_ref[...] > 0.5, raw, 0.0).astype(jnp.bfloat16)
    if len(outs) > 1:
        outs[1][...] = raw


def weights_kernel(pivot, solved_ref, own_ref, other_ref, weights_ref):
    core = lax.axis_index("pr")
    half = own_ref.shape[3]
    own_part = solved_ref[:, pl.ds(pl.multiple_of(core * half, half), half)]
    other_part = solved_ref[:, pl.ds(pl.multiple_of((1 - core) * half, half), half)]
    dims = (((1,), (1,)), ((), ()))
    for row in range(own_ref.shape[0]):
        weights_ref[row] = (
            lax.dot_general(own_part, own_ref[row, pivot], dims, preferred_element_type=jnp.float32)
            + lax.dot_general(other_part, other_ref[row, pivot], dims, preferred_element_type=jnp.float32)
        ).astype(jnp.bfloat16)


def probe_rows(slot, probes):
    return pl.ds(pl.multiple_of(slot * probes, probes), probes)


def update_kernel(pivot, own_ref, other_ref, right_ref, rhs_ref, out_ref):
    core = lax.axis_index("pr")
    for row in range(rhs_ref.shape[0]):
        for ref, slot in ((own_ref, core), (other_ref, 1 - core)):
            rows = probe_rows(slot, own_ref.shape[1])
            out_ref[row, rows, :] = rhs_ref[row, rows, :] - jnp.dot(
                ref[row], right_ref[row, pivot], preferred_element_type=jnp.float32
            )


def part_update(slot, weights_ref, right_ref, rhs_ref, out_ref, part, sems):
    copies = []
    rows = probe_rows(slot, weights_ref.shape[1])
    for row in range(rhs_ref.shape[0]):
        part[row] = rhs_ref[row, rows, :] - jnp.dot(
            weights_ref[row], right_ref[row, 0], preferred_element_type=jnp.float32
        )
        copies.append(pltpu.make_async_copy(part.at[row], out_ref.at[row, rows, :], sems.at[row]))
        copies[-1].start()
    return copies


def own_kernel(count, weights_ref, right_ref, rhs_ref, *refs):
    solved_refs, (out_ref, stack_ref, part, sems, stack_sems) = refs[:count], refs[count:]
    copies = [
        pltpu.make_async_copy(solved_refs[place], stack_ref.at[place], stack_sems.at[place])
        for place in range(count)
    ]
    for copy in copies:
        copy.start()
    copies += part_update(lax.axis_index("pr"), weights_ref, right_ref, rhs_ref, out_ref, part, sems)
    for copy in copies:
        copy.wait()


def other_kernel(weights_ref, right_ref, rhs_ref, held_ref, out_ref, part, sems):
    del held_ref
    for copy in part_update(1 - lax.axis_index("pr"), weights_ref, right_ref, rhs_ref, out_ref, part, sems):
        copy.wait()


def call(kernel, shapes, specs, scratch=(), flops=0, read=0, limit=16, out=VMEM, aliases=None):
    return pl.pallas_call(
        kernel,
        out_shape=shapes,
        in_specs=specs,
        out_specs=[out] * len(shapes),
        scratch_shapes=list(scratch),
        input_output_aliases=aliases or {},
        compiler_params=pltpu.CompilerParams(vmem_limit_bytes=limit * MIB),
        cost_estimate=pl.CostEstimate(flops=flops, bytes_accessed=read, transcendentals=0),
    )


def local(
    slots,
    cores,
    pivot_rhs,
    pivot_inverse,
    pivot_owner,
    coupling_left,
    coupling_right,
    coupling_ranks,
    future_left,
    future_right,
    future_ranks,
    future_rhs,
):
    count = pivot_owner.shape[0]
    size, probes = pivot_rhs.shape[1:]
    rank = coupling_left.shape[3]
    rows = future_left.shape[0]
    blocks = size // block_width(size)
    inverse = pivot_inverse[0]
    rhs = jnp.swapaxes(pivot_rhs[0], 0, 1)
    left = jnp.swapaxes(coupling_left[0], 1, 2)
    right = jnp.swapaxes(coupling_right[0], 1, 2)
    wide = jax.ShapeDtypeStruct((probes, size), jnp.float32)
    narrow = jax.ShapeDtypeStruct((probes, size), jnp.bfloat16)

    raw, block = call(
        first_kernel,
        [wide, narrow],
        [ANY, ANY, ANY],
        [
            pltpu.VMEM((size, size), jnp.bfloat16),
            pltpu.SemaphoreType.DMA((blocks,)),
            pltpu.VMEM((probes, size), jnp.float32),
            pltpu.SMEM((count,), jnp.int32),
            pltpu.SemaphoreType.DMA((2,)),
        ],
        probes * size * size,
        size * size,
        FIRST_LIMIT,
    )(pivot_owner, rhs, inverse)
    block, future_left = lax.optimization_barrier((block, future_left))
    other_left = swap(future_left, cores)

    def ahead(current):
        return call(
            functools.partial(ahead_kernel, current),
            [
                jax.ShapeDtypeStruct((rank, size), jnp.bfloat16),
                jax.ShapeDtypeStruct((size, rank), jnp.bfloat16),
                jax.ShapeDtypeStruct((1, size), jnp.float32),
            ],
            [SMEM, SMEM, VMEM, VMEM, VMEM],
            (),
            rank * size * size,
            size * size + 4 * rank * size,
        )(pivot_owner, coupling_ranks, right, left, inverse)

    def mask():
        return call(
            mask_kernel,
            [jax.ShapeDtypeStruct(future_right.shape, jnp.bfloat16)],
            [SMEM, VMEM],
            (),
            future_right.size,
            4 * future_right.size,
        )(future_ranks, future_right)[0]

    product_flops = 2 * rows * probes * rank * size

    def weigh(pivot):
        return call(
            functools.partial(weights_kernel, pivot),
            [jax.ShapeDtypeStruct((rows, probes, rank), jnp.bfloat16)],
            [VMEM] * 3,
            (),
            product_flops,
            2 * rows * rank * size,
        )(solved[pivot], future_left, other_left)[0]

    solved = [None] * count
    total = future_rhs
    masked = None
    for current in reversed(range(count)):
        before = current + 1
        held = {}

        def early(current=current, before=before, held=held):
            if before == count:
                held["ready"] = ahead(current) if current > 0 else ()
                return held["ready"]
            held["own"] = weigh(before)
            held["other"] = swap(held["own"], cores)
            if current > 0:
                held["ready"] = ahead(current)
            return held["other"], held.get("ready")

        def late(current=current, before=before, held=held, total=total, masked=masked):
            if before == count:
                return None
            held["masked"] = mask() if masked is None else masked
            held["total"] = call(
                functools.partial(update_kernel, before),
                [jax.ShapeDtypeStruct(total.shape, jnp.float32)],
                [VMEM] * 4,
                (),
                product_flops,
                rows * rank * size + 2 * 4 * total.size,
            )(held["own"], held["other"], held["masked"], total)[0]
            return held["total"]

        solved[current] = spread(block, slots, cores, count - 1 - current, [early, late])
        total, masked = held.get("total", total), held.get("masked", masked)
        if current > 0:
            outs = call(
                step_kernel,
                [narrow, wide] if current > 1 else [narrow],
                [VMEM] * 5,
                (),
                4 * probes * rank * size,
                4 * rank * size,
            )(solved[current], *held["ready"], raw)
            block, raw = outs[0], outs[-1]
    if masked is None:
        masked = mask()
    own = weigh(0)
    other = swap(own, cores)
    half = total.shape[2]
    scratch = [pltpu.VMEM((rows, probes, half), jnp.float32), pltpu.SemaphoreType.DMA((rows,))]
    partial, stacked = call(
        functools.partial(own_kernel, count),
        [
            jax.ShapeDtypeStruct(total.shape, jnp.float32),
            jax.ShapeDtypeStruct((count, probes, size), jnp.bfloat16),
        ],
        [VMEM] * (3 + count),
        scratch + [pltpu.SemaphoreType.DMA((count,))],
        product_flops // 2,
        4 * total.size,
        out=ANY,
    )(own, masked, total, *solved)
    (out,) = call(
        other_kernel,
        [jax.ShapeDtypeStruct(total.shape, jnp.float32)],
        [VMEM] * 3 + [ANY],
        scratch,
        product_flops // 2,
        4 * total.size,
        out=ANY,
        aliases={3: 0},
    )(other, masked, total, partial)
    return jnp.swapaxes(stacked, 1, 2), out


def solution(mesh):
    return jax.shard_map(
        functools.partial(local, mesh.shape["tc"], mesh.shape["pr"]),
        mesh=mesh,
        in_specs=(
            P("tc", None, "pr"),
            P("tc", None, None),
            P(),
            P("tc", None, None, None),
            P("tc", None, None, None),
            P("tc", None),
            P("tc", None, None, "pr"),
            P("tc", None, None, "pr"),
            P("tc", None),
            P("tc", None, "pr"),
        ),
        out_specs=(P(None, None, "pr"), P("tc", None, "pr")),
        check_vma=False,
    )
```

time: 61.1 us -> 57.9 us (0.948)
  waiting for transfers between devices: 19.7 us -> 17.4 us
  Pallas kernels: 12.8 us -> 11.4 us
  local copies, waits for them, and re-layouts: 1.39 us -> 2.63 us
  other arithmetic: 0.88 us -> 0.13 us
    unnamed x20 -> x22, local copies, waits for them, and re-layouts: 0.05 us -> 2.63 us
    ppermute x18, waiting for transfers between devices: 18 us -> 16 us  [spread(): received.append(lax.ppermute(block, ('tc', 'pr'), pairs))]
    squeeze x1 -> x0, local copies, waits for them, and re-layouts: 1.34 us -> none  [ahead(): right[entry]]
    pallas_call x1, Pallas kernels: 4.06 us -> 2.98 us  [local(): call(first_kernel, [wide, narrow], [ANY, ANY, ANY], [pltpu.VMEM((size, si...]
    transpose x1 -> x0, other arithmetic: 0.75 us -> none  [local(): return (jnp.swapaxes(jnp.stack(solved), 1, 2), total)]
    pallas_call x10 -> x12, Pallas kernels: 8.72 us -> 8.42 us  [the longest x2 2.58 us: ahead(): call(functools.partial(ahead_kernel, current), [jax.ShapeDtypeStruct((ran...]
  transfers between devices with their start and end apart: 22 -> 22, of which waited for: 16 -> 16; matrix products, arithmetic and copies ran while one was open for 3% -> 0% of each run, Pallas kernels for 9% -> 11%
where the time goes in v5:
time: 57.9 us; the launch traced here: 57.7 us
  starting transfers between devices  25.3 us (44%)
  waiting for transfers between devices  17.4 us (30%)
  Pallas kernels  11.4 us (20%)
  local copies, waits for them, and re-layouts  2.63 us (5%)
  between operations  0.83 us (1%)
    ppermute x18, starting transfers between devices, spread(): received.append(lax.ppermute(block, ('tc', 'pr'), pairs))  24.6 us
    ppermute x18, waiting for transfers between devices, spread(): received.append(lax.ppermute(block, ('tc', 'pr'), pairs))  16 us
    pallas_call x1, Pallas kernels, local(): call(first_kernel, [wide, narrow], [ANY, ANY, ANY], [pltpu.VMEM((size, si...  2.98 us
    unnamed x22, local copies, waits for them, and re-layouts  2.63 us
    pallas_call x2, Pallas kernels, ahead(): call(functools.partial(ahead_kernel, current), [jax.ShapeDtypeStruct((ran...  2.58 us
    ppermute x4, waiting for transfers between devices, swap(): lax.ppermute(block, 'pr', [(core, cores - 1 - core) for core in range(cor...  1.47 us
    pallas_call x3, Pallas kernels, weigh(): call(functools.partial(weights_kernel, pivot), [jax.ShapeDtypeStruct((row...  1.41 us
  transfers between devices with their start and end apart: 22, of which 16 were waited for; matrix products, arithmetic and copies ran while one was open for 0% of the time, Pallas kernels for 11%

profile of v5, /device:TPU:0, one launch (start us, length us, event | category | flops | bytes accessed | tf_op | source)
XLA Modules:
  0.0 57.7 jit_solution(6853193624185587371)
XLA Ops:
  0.7 3.0 %shard_map.113 = (f32[32,1536]{1,0:T(8,128)}, bf16[32,1536]{1,0:T(8,128)(2,1)}) custom-call(s32[3]{0:T(128)} %owner_ref.5, f32[32,1536]{1,0:T(8,128)} %bitcast.18, bf16[1536,1536]{1,0:T(8,128)(2,1)} %bitcast.11), custom_call_target="tpu_custom_call" | custom-call | flops 75497472 | bytes 2359296 | tf_op jit(solution)/shard_map/pallas_call | solution.py:231
  3.6 0.5 collective-permute-start.9
  4.2 3.5 %collective-permute-start.2 = (bf16[32,1536]{1,0:T(8,128)(2,1)}, bf16[32,1536]{1,0:T(8,128)(2,1)S(1)}, u32[]{:S(2)}, u32[]{:S(2)}) collective-permute-start(bf16[32,1536]{1,0:T(8,128)(2,1)} %get-tuple-element.45), channel_id=1, source_target_pairs={{0,6},{1,25},{2,4},{3,27},{4,2},{5,29},{6,0},{7,31},{8,14},{9,17},... | collective-permute-start | bytes 294920 | tf_op jit(solution)/shard_map/ppermute | solution.py:44
  7.7 0.5 collective-permute-start.1
  8.2 0.1 collective-permute-start
  8.3 1.3 %copy-done.2 = bf16[1,2,1536,200]{2,3,1,0:T(8,128)(2,1)S(1)} copy-done((bf16[1,2,1536,200]{2,3,1,0:T(8,128)(2,1)S(1)}, bf16[1,2,1536,200]{2,3,1,0:T(8,128)(2,1)}, u32[]{:S(2)}) %copy-start.2) | copy-done | bytes 1228824
  9.6 1.3 %copy-done.3 = bf16[1,2,1536,200]{2,3,1,0:T(8,128)(2,1)S(1)} copy-done((bf16[1,2,1536,200]{2,3,1,0:T(8,128)(2,1)S(1)}, bf16[1,2,1536,200]{2,3,1,0:T(8,128)(2,1)}, u32[]{:S(2)}) %copy-start.3) | copy-done | bytes 1228824
  10.9 1.3 %shard_map.114 = (bf16[200,1536]{1,0:T(8,128)(2,1)S(1)}, bf16[1536,200]{1,0:T(8,128)(2,1)S(1)}, f32[1,1536]{1,0:T(1,128)S(1)}) custom-call(s32[3]{0:T(128)S(1)} %copy-done.7, s32[1,2]{1,0:T(1,128)S(1)} %copy-done.8, bf16[2,200,1536]{2,1,0:T(8,128)(2,1)S(1)} %bitcast.14, bf16[2,200,1536]{2,1,0:T(8,128)(2,1)S(1)} %bitcast.16, bf16[1536,1536]{1,0:T(8,128)(2,1)S(1)} %bitcast.12), custom_call_target="tpu_custom_call" | custom-call | flops 471859200 | bytes 3588096 | tf_op jit(solution)/shard_map/pallas_call | solution.py:250
  12.2 0.3 collective-permute-done.1
  12.5 0.5 collective-permute-done
  13.1 3.7 %collective-permute-start.5 = (bf16[32,1536]{1,0:T(8,128)(2,1)S(1)}, bf16[32,1536]{1,0:T(8,128)(2,1)S(1)}, u32[]{:S(2)}, u32[]{:S(2)}) collective-permute-start(bf16[32,1536]{1,0:T(8,128)(2,1)S(1)} %add_add_fusion.5), channel_id=1, source_target_pairs={{0,24},{1,7},{2,26},{3,5},{4,28},{5,3},{6,30},{7,1},{8,16},{9,15},... | collective-permute-start | bytes 294920 | tf_op jit(solution)/shard_map/ppermute | solution.py:44
  16.7 0.8 %collective-permute-start.3 = (bf16[32,1536]{1,0:T(8,128)(2,1)S(1)}, bf16[32,1536]{1,0:T(8,128)(2,1)S(1)}, u32[]{:S(2)}, u32[]{:S(2)}) collective-permute-start(bf16[32,1536]{1,0:T(8,128)(2,1)S(1)} %add_add_fusion.5), channel_id=1, source_target_pairs={{0,8},{1,3},{2,10},{3,1},{4,12},{5,7},{6,14},{7,5},{8,0},{9,11},{1... | collective-permute-start | bytes 294920 | tf_op jit(solution)/shard_map/ppermute | solution.py:44
  17.5 2.1 %collective-permute-done.5 = bf16[32,1536]{1,0:T(8,128)(2,1)S(1)} collective-permute-done((bf16[32,1536]{1,0:T(8,128)(2,1)S(1)}, bf16[32,1536]{1,0:T(8,128)(2,1)S(1)}, u32[]{:S(2)}, u32[]{:S(2)}) %collective-permute-start.5) | collective-permute-done | bytes 98336 | tf_op jit(solution)/shard_map/ppermute | solution.py:44
  19.6 2.7 %collective-permute-done.4 = bf16[32,1536]{1,0:T(8,128)(2,1)S(1)} collective-permute-done((bf16[32,1536]{1,0:T(8,128)(2,1)S(1)}, bf16[32,1536]{1,0:T(8,128)(2,1)S(1)}, u32[]{:S(2)}, u32[]{:S(2)}) %collective-permute-start.4) | collective-permute-done | bytes 98336 | tf_op jit(solution)/shard_map/ppermute | solution.py:44
  22.4 0.5 shard_map.115
  23.0 2.2 %collective-permute-start.8 = (bf16[32,1536]{1,0:T(8,128)(2,1)S(1)}, bf16[32,1536]{1,0:T(8,128)(2,1)S(1)}, u32[]{:S(2)}, u32[]{:S(2)}) collective-permute-start(bf16[32,1536]{1,0:T(8,128)(2,1)S(1)} %get-tuple-element.59), channel_id=1, source_target_pairs={{0,24},{1,7},{2,26},{3,5},{4,28},{5,3},{6,30},{7,1},{8,16},{9,15},... | collective-permute-start | bytes 294920 | tf_op jit(solution)/shard_map/ppermute | solution.py:44
  25.2 0.4 collective-permute-start.7
  25.6 1.8 %collective-permute-start.6 = (bf16[32,1536]{1,0:T(8,128)(2,1)S(1)}, bf16[32,1536]{1,0:T(8,128)(2,1)S(1)}, u32[]{:S(2)}, u32[]{:S(2)}) collective-permute-start(bf16[32,1536]{1,0:T(8,128)(2,1)S(1)} %get-tuple-element.59), channel_id=1, source_target_pairs={{0,8},{1,3},{2,10},{3,1},{4,12},{5,7},{6,14},{7,5},{8,0},{9,11},{1... | collective-permute-start | bytes 294920 | tf_op jit(solution)/shard_map/ppermute | solution.py:44
  27.4 0.5 shard_map.116.own_ref
  28.0 1.3 %shard_map.117 = (bf16[200,1536]{1,0:T(8,128)(2,1)S(1)}, bf16[1536,200]{1,0:T(8,128)(2,1)S(1)}, f32[1,1536]{1,0:T(1,128)S(1)}) custom-call(s32[3]{0:T(128)S(1)} %copy-done.7, s32[1,2]{1,0:T(1,128)S(1)} %copy-done.8, bf16[2,200,1536]{2,1,0:T(8,128)(2,1)S(1)} %bitcast.15, bf16[2,200,1536]{2,1,0:T(8,128)(2,1)S(1)} %bitcast.17, bf16[1536,1536]{1,0:T(8,128)(2,1)S(1)} %bitcast.13), custom_call_target="tpu_custom_call" | custom-call | flops 471859200 | bytes 3588096 | tf_op jit(solution)/shard_map/pallas_call | solution.py:250
  29.3 0.2 collective-permute-done.8
  29.5 2.1 %collective-permute-done.7 = bf16[32,1536]{1,0:T(8,128)(2,1)S(1)} collective-permute-done((bf16[32,1536]{1,0:T(8,128)(2,1)S(1)}, bf16[32,1536]{1,0:T(8,128)(2,1)S(1)}, u32[]{:S(2)}, u32[]{:S(2)}) %collective-permute-start.7) | collective-permute-done | bytes 98336 | tf_op jit(solution)/shard_map/ppermute | solution.py:44
  31.6 2.2 %collective-permute-start.13 = (bf16[32,1536]{1,0:T(8,128)(2,1)S(1)}, bf16[32,1536]{1,0:T(8,128)(2,1)S(1)}, u32[]{:S(2)}, u32[]{:S(2)}) collective-permute-start(bf16[32,1536]{1,0:T(8,128)(2,1)S(1)} %add_add_fusion.3), channel_id=1, source_target_pairs={{0,6},{1,25},{2,4},{3,27},{4,2},{5,29},{6,0},{7,31},{8,14},{9,17},... | collective-permute-start | bytes 294920 | tf_op jit(solution)/shard_map/ppermute | solution.py:44
  33.8 0.5 collective-permute-start.12
  34.3 0.9 %collective-permute-start.11 = (bf16[32,1536]{1,0:T(8,128)(2,1)S(1)}, bf16[32,1536]{1,0:T(8,128)(2,1)S(1)}, u32[]{:S(2)}, u32[]{:S(2)}) collective-permute-start(bf16[32,1536]{1,0:T(8,128)(2,1)S(1)} %add_add_fusion.3), channel_id=1, source_target_pairs={{0,2},{1,9},{2,0},{3,11},{4,6},{5,13},{6,4},{7,15},{8,10},{9,1},{1... | collective-permute-start | bytes 294920 | tf_op jit(solution)/shard_map/ppermute | solution.py:44
  35.2 0.9 %shard_map.118.right_ref = bf16[2,3,200,768]{3,2,1,0:T(8,128)(2,1)S(1)} custom-call(s32[2,3]{1,0:T(2,128)S(1)} %copy-done.9, bf16[2,3,200,768]{3,2,1,0:T(8,128)(2,1)S(1)} %copy-done.4), custom_call_target="tpu_custom_call" | custom-call | flops 921600 | bytes 3686400 | tf_op jit(solution)/shard_map/pallas_call | solution.py:264
  36.0 0.3 shard_map.119.rhs_ref
  36.4 0.8 %collective-permute-done.13 = bf16[32,1536]{1,0:T(8,128)(2,1)S(1)} collective-permute-done((bf16[32,1536]{1,0:T(8,128)(2,1)S(1)}, bf16[32,1536]{1,0:T(8,128)(2,1)S(1)}, u32[]{:S(2)}, u32[]{:S(2)}) %collective-permute-start.13) | collective-permute-done | bytes 98336 | tf_op jit(solution)/shard_map/ppermute | solution.py:44
  37.2 1.2 %collective-permute-done.12 = bf16[32,1536]{1,0:T(8,128)(2,1)S(1)} collective-permute-done((bf16[32,1536]{1,0:T(8,128)(2,1)S(1)}, bf16[32,1536]{1,0:T(8,128)(2,1)S(1)}, u32[]{:S(2)}, u32[]{:S(2)}) %collective-permute-start.12) | collective-permute-done | bytes 98336 | tf_op jit(solution)/shard_map/ppermute | solution.py:44
  38.4 0.5 collective-permute-done.11
  38.9 0.5 shard_map.120
  39.5 1.9 %collective-permute-start.16 = (bf16[32,1536]{1,0:T(8,128)(2,1)S(1)}, bf16[32,1536]{1,0:T(8,128)(2,1)S(1)}, u32[]{:S(2)}, u32[]{:S(2)}) collective-permute-start(bf16[32,1536]{1,0:T(8,128)(2,1)S(1)} %shard_map.120), channel_id=1, source_target_pairs={{0,6},{1,25},{2,4},{3,27},{4,2},{5,29},{6,0},{7,31},{8,14},{9,17},... | collective-permute-start | bytes 294920 | tf_op jit(solution)/shard_map/ppermute | solution.py:44
  41.4 0.5 collective-permute-start.15
  41.9 1.1 %collective-permute-start.14 = (bf16[32,1536]{1,0:T(8,128)(2,1)S(1)}, bf16[32,1536]{1,0:T(8,128)(2,1)S(1)}, u32[]{:S(2)}, u32[]{:S(2)}) collective-permute-start(bf16[32,1536]{1,0:T(8,128)(2,1)S(1)} %shard_map.120), channel_id=1, source_target_pairs={{0,2},{1,9},{2,0},{3,11},{4,6},{5,13},{6,4},{7,15},{8,10},{9,1},{1... | collective-permute-start | bytes 294920 | tf_op jit(solution)/shard_map/ppermute | solution.py:44
  43.0 0.5 shard_map.121.own_ref
  43.5 1.2 %collective-permute-done.17.other_ref = bf16[2,32,200]{2,1,0:T(8,128)(2,1)S(1)} collective-permute-done((bf16[2,32,200]{2,1,0:T(8,128)(2,1)S(1)}, bf16[2,32,200]{2,1,0:T(8,128)(2,1)S(1)}, u32[]{:S(2)}, u32[]{:S(2)}) %collective-permute-start.17) | collective-permute-done | bytes 25632 | tf_op jit(solution)/shard_map/ppermute | solution.py:55
  44.7 0.3 collective-permute-done.16
  45.0 1.0 %collective-permute-done.15 = bf16[32,1536]{1,0:T(8,128)(2,1)S(1)} collective-permute-done((bf16[32,1536]{1,0:T(8,128)(2,1)S(1)}, bf16[32,1536]{1,0:T(8,128)(2,1)S(1)}, u32[]{:S(2)}, u32[]{:S(2)}) %collective-permute-start.15) | collective-permute-done | bytes 98336 | tf_op jit(solution)/shard_map/ppermute | solution.py:44
  46.1 0.4 collective-permute-done.14
  46.5 2.2 %collective-permute-start.20 = (bf16[32,1536]{1,0:T(8,128)(2,1)S(1)}, bf16[32,1536]{1,0:T(8,128)(2,1)S(1)}, u32[]{:S(2)}, u32[]{:S(2)}) collective-permute-start(bf16[32,1536]{1,0:T(8,128)(2,1)S(1)} %add_add_fusion.1), channel_id=1, source_target_pairs={{0,24},{1,7},{2,26},{3,5},{4,28},{5,3},{6,30},{7,1},{8,16},{9,15},... | collective-permute-start | bytes 294920 | tf_op jit(solution)/shard_map/ppermute | solution.py:44
  48.7 2.2 %collective-permute-start.18 = (bf16[32,1536]{1,0:T(8,128)(2,1)S(1)}, bf16[32,1536]{1,0:T(8,128)(2,1)S(1)}, u32[]{:S(2)}, u32[]{:S(2)}) collective-permute-start(bf16[32,1536]{1,0:T(8,128)(2,1)S(1)} %add_add_fusion.1), channel_id=1, source_target_pairs={{0,8},{1,3},{2,10},{3,1},{4,12},{5,7},{6,14},{7,5},{8,0},{9,11},{1... | collective-permute-start | bytes 294920 | tf_op jit(solution)/shard_map/ppermute | solution.py:44
  51.0 0.3 shard_map.122.rhs_ref
  51.3 1.7 %collective-permute-done.20 = bf16[32,1536]{1,0:T(8,128)(2,1)S(1)} collective-permute-done((bf16[32,1536]{1,0:T(8,128)(2,1)S(1)}, bf16[32,1536]{1,0:T(8,128)(2,1)S(1)}, u32[]{:S(2)}, u32[]{:S(2)}) %collective-permute-start.20) | collective-permute-done | bytes 98336 | tf_op jit(solution)/shard_map/ppermute | solution.py:44
  53.0 2.1 %collective-permute-done.19 = bf16[32,1536]{1,0:T(8,128)(2,1)S(1)} collective-permute-done((bf16[32,1536]{1,0:T(8,128)(2,1)S(1)}, bf16[32,1536]{1,0:T(8,128)(2,1)S(1)}, u32[]{:S(2)}, u32[]{:S(2)}) %collective-permute-start.19) | collective-permute-done | bytes 98336 | tf_op jit(solution)/shard_map/ppermute | solution.py:44
  55.1 0.5 shard_map.123.weights_ref
  55.6 0.9 %shard_map.124 = (f32[2,64,768]{2,1,0:T(8,128)}, bf16[3,32,1536]{2,1,0:T(8,128)(2,1)}) custom-call(bf16[2,32,200]{2,1,0:T(8,128)(2,1)S(1)} %shard_map.123.weights_ref, bf16[2,3,200,768]{3,2,1,0:T(8,128)(2,1)S(1)} %shard_map.118.right_ref, f32[2,64,768]{2,1,0:T(8,128)S(1)} %shard_map.122.rhs_ref, bf16[32,1536]{1,0:T(8,128)(2,1)S(1)} %add_add_fusion.solved_ref.refs_0_, ...), custom_call_target="tpu_custom_call" | custom-call | flops 19660800 | bytes 393216 | tf_op jit(solution)/shard_map/pallas_call | solution.py:334
  56.6 0.3 collective-permute-done.21.weights_ref
  56.8 0.9 %shard_map.125 = f32[2,64,768]{2,1,0:T(8,128)} custom-call(bf16[2,32,200]{2,1,0:T(8,128)(2,1)S(1)} %collective-permute-done.21.weights_ref, bf16[2,3,200,768]{3,2,1,0:T(8,128)(2,1)S(1)} %shard_map.118.right_ref, f32[2,64,768]{2,1,0:T(8,128)S(1)} %shard_map.122.rhs_ref, f32[2,64,768]{2,1,0:T(8,128)} %get-tuple-element.77.held_ref), custom_call_target="tpu_custom_call", output_to_operand_aliasing={{}: (3, {})} | custom-call | flops 19660800 | bytes 393216 | tf_op jit(solution)/shard_map/pallas_call | solution.py:346
  (37 shorter events, 0.4 us)
Async XLA Ops:
  0.6 7.7 %copy-start = (bf16[1,1536,1536]{2,1,0:T(8,128)(2,1)S(1)}, bf16[1,1536,1536]{2,1,0:T(8,128)(2,1)}, u32[]{:S(2)}) copy-start(bf16[1,1536,1536]{2,1,0:T(8,128)(2,1)} %param.11) | copy-start | bytes 14155780
  0.6 7.7 %copy-start.7 = (s32[3]{0:T(128)S(1)}, s32[3]{0:T(128)}, u32[]{:S(2)}) copy-start(s32[3]{0:T(128)} %owner_ref.5) | copy-start | bytes 40
  0.7 7.7 %copy-start.8 = (s32[1,2]{1,0:T(1,128)S(1)}, s32[1,2]{1,0:T(1,128)}, u32[]{:S(2)}) copy-start(s32[1,2]{1,0:T(1,128)} %ranks_ref.4) | copy-start | bytes 28
  3.6 23.8 %collective-permute-start.9 = (bf16[2,3,200,768]{3,2,1,0:T(8,128)(2,1)}, bf16[2,3,200,768]{3,2,1,0:T(8,128)(2,1)S(1)}, u32[]{:S(2)}, u32[]{:S(2)}) collective-permute-start(bf16[2,3,200,768]{3,2,1,0:T(8,128)(2,1)} %own_ref.2), channel_id=1, source_target_pairs={{0,1},{1,0},{2,3},{3,2},{4,5},{5,4},{6,7},{7,6},{8,9},{9,8},{10,11... | collective-permute-start | bytes 5529608 | tf_op jit(solution)/shard_map/ppermute | solution.py:55
  4.2 8.1 %collective-permute-start.2 = (bf16[32,1536]{1,0:T(8,128)(2,1)}, bf16[32,1536]{1,0:T(8,128)(2,1)S(1)}, u32[]{:S(2)}, u32[]{:S(2)}) collective-permute-start(bf16[32,1536]{1,0:T(8,128)(2,1)} %get-tuple-element.45), channel_id=1, source_target_pairs={{0,6},{1,25},{2,4},{3,27},{4,2},{5,29},{6,0},{7,31},{8,14},{9,17},... | collective-permute-start | bytes 294920 | tf_op jit(solution)/shard_map/ppermute | solution.py:44
  7.7 4.8 %collective-permute-start.1 = (bf16[32,1536]{1,0:T(8,128)(2,1)}, bf16[32,1536]{1,0:T(8,128)(2,1)S(1)}, u32[]{:S(2)}, u32[]{:S(2)}) collective-permute-start(bf16[32,1536]{1,0:T(8,128)(2,1)} %get-tuple-element.45), channel_id=1, source_target_pairs={{0,4},{1,17},{2,6},{3,19},{4,0},{5,21},{6,2},{7,23},{8,12},{9,25},... | collective-permute-start | bytes 294920 | tf_op jit(solution)/shard_map/ppermute | solution.py:44
  8.2 4.8 %collective-permute-start = (bf16[32,1536]{1,0:T(8,128)(2,1)}, bf16[32,1536]{1,0:T(8,128)(2,1)S(1)}, u32[]{:S(2)}, u32[]{:S(2)}) collective-permute-start(bf16[32,1536]{1,0:T(8,128)(2,1)} %get-tuple-element.45), channel_id=1, source_target_pairs={{0,2},{1,9},{2,0},{3,11},{4,6},{5,13},{6,4},{7,15},{8,10},{9,1},{1... | collective-permute-start | bytes 294920 | tf_op jit(solution)/shard_map/ppermute | solution.py:44
  8.3 1.3 %copy-start.2 = (bf16[1,2,1536,200]{2,3,1,0:T(8,128)(2,1)S(1)}, bf16[1,2,1536,200]{2,3,1,0:T(8,128)(2,1)}, u32[]{:S(2)}) copy-start(bf16[1,2,1536,200]{2,3,1,0:T(8,128)(2,1)} %param.14) | copy-start | bytes 3686404
  9.6 1.3 %copy-start.3 = (bf16[1,2,1536,200]{2,3,1,0:T(8,128)(2,1)S(1)}, bf16[1,2,1536,200]{2,3,1,0:T(8,128)(2,1)}, u32[]{:S(2)}) copy-start(bf16[1,2,1536,200]{2,3,1,0:T(8,128)(2,1)} %param.13) | copy-start | bytes 3686404
  10.9 2.1 %copy-start.10 = (bf16[32,1536]{1,0:T(8,128)(2,1)S(1)}, bf16[32,1536]{1,0:T(8,128)(2,1)}, u32[]{:S(2)}) copy-start(bf16[32,1536]{1,0:T(8,128)(2,1)} %get-tuple-element.45) | copy-start | bytes 294916
  10.9 11.5 %copy-start.6 = (f32[32,1536]{1,0:T(8,128)S(1)}, f32[32,1536]{1,0:T(8,128)}, u32[]{:S(2)}) copy-start(f32[32,1536]{1,0:T(8,128)} %get-tuple-element.53.raw_ref) | copy-start | bytes 589828
  12.2 15.2 %copy-start.1 = (bf16[2,3,200,768]{3,2,1,0:T(8,128)(2,1)S(1)}, bf16[2,3,200,768]{3,2,1,0:T(8,128)(2,1)}, u32[]{:S(2)}) copy-start(bf16[2,3,200,768]{3,2,1,0:T(8,128)(2,1)} %own_ref.2) | copy-start | bytes 5529604
  13.1 6.6 %collective-permute-start.5 = (bf16[32,1536]{1,0:T(8,128)(2,1)S(1)}, bf16[32,1536]{1,0:T(8,128)(2,1)S(1)}, u32[]{:S(2)}, u32[]{:S(2)}) collective-permute-start(bf16[32,1536]{1,0:T(8,128)(2,1)S(1)} %add_add_fusion.5), channel_id=1, source_target_pairs={{0,24},{1,7},{2,26},{3,5},{4,28},{5,3},{6,30},{7,1},{8,16},{9,15},... | collective-permute-start | bytes 294920 | tf_op jit(solution)/shard_map/ppermute | solution.py:44
  16.7 5.7 %collective-permute-start.4 = (bf16[32,1536]{1,0:T(8,128)(2,1)S(1)}, bf16[32,1536]{1,0:T(8,128)(2,1)S(1)}, u32[]{:S(2)}, u32[]{:S(2)}) collective-permute-start(bf16[32,1536]{1,0:T(8,128)(2,1)S(1)} %add_add_fusion.5), channel_id=1, source_target_pairs={{0,16},{1,5},{2,18},{3,7},{4,20},{5,1},{6,22},{7,3},{8,24},{9,13},... | collective-permute-start | bytes 294920 | tf_op jit(solution)/shard_map/ppermute | solution.py:44
  16.7 5.7 %collective-permute-start.3 = (bf16[32,1536]{1,0:T(8,128)(2,1)S(1)}, bf16[32,1536]{1,0:T(8,128)(2,1)S(1)}, u32[]{:S(2)}, u32[]{:S(2)}) collective-permute-start(bf16[32,1536]{1,0:T(8,128)(2,1)S(1)} %add_add_fusion.5), channel_id=1, source_target_pairs={{0,8},{1,3},{2,10},{3,1},{4,12},{5,7},{6,14},{7,5},{8,0},{9,11},{1... | collective-permute-start | bytes 294920 | tf_op jit(solution)/shard_map/ppermute | solution.py:44
  23.0 6.5 %collective-permute-start.8 = (bf16[32,1536]{1,0:T(8,128)(2,1)S(1)}, bf16[32,1536]{1,0:T(8,128)(2,1)S(1)}, u32[]{:S(2)}, u32[]{:S(2)}) collective-permute-start(bf16[32,1536]{1,0:T(8,128)(2,1)S(1)} %get-tuple-element.59), channel_id=1, source_target_pairs={{0,24},{1,7},{2,26},{3,5},{4,28},{5,3},{6,30},{7,1},{8,16},{9,15},... | collective-permute-start | bytes 294920 | tf_op jit(solution)/shard_map/ppermute | solution.py:44
  25.2 6.3 %collective-permute-start.7 = (bf16[32,1536]{1,0:T(8,128)(2,1)S(1)}, bf16[32,1536]{1,0:T(8,128)(2,1)S(1)}, u32[]{:S(2)}, u32[]{:S(2)}) collective-permute-start(bf16[32,1536]{1,0:T(8,128)(2,1)S(1)} %get-tuple-element.59), channel_id=1, source_target_pairs={{0,16},{1,5},{2,18},{3,7},{4,20},{5,1},{6,22},{7,3},{8,24},{9,13},... | collective-permute-start | bytes 294920 | tf_op jit(solution)/shard_map/ppermute | solution.py:44
  25.6 6.0 %collective-permute-start.6 = (bf16[32,1536]{1,0:T(8,128)(2,1)S(1)}, bf16[32,1536]{1,0:T(8,128)(2,1)S(1)}, u32[]{:S(2)}, u32[]{:S(2)}) collective-permute-start(bf16[32,1536]{1,0:T(8,128)(2,1)S(1)} %get-tuple-element.59), channel_id=1, source_target_pairs={{0,8},{1,3},{2,10},{3,1},{4,12},{5,7},{6,14},{7,5},{8,0},{9,11},{1... | collective-permute-start | bytes 294920 | tf_op jit(solution)/shard_map/ppermute | solution.py:44
  27.9 7.3 %copy-start.4 = (bf16[2,3,200,768]{3,2,1,0:T(8,128)(2,1)S(1)}, bf16[2,3,200,768]{3,2,1,0:T(8,128)(2,1)}, u32[]{:S(2)}) copy-start(bf16[2,3,200,768]{3,2,1,0:T(8,128)(2,1)} %right_ref.1) | copy-start | bytes 5529604
  27.9 7.2 %copy-start.9 = (s32[2,3]{1,0:T(2,128)S(1)}, s32[2,3]{1,0:T(2,128)}, u32[]{:S(2)}) copy-start(s32[2,3]{1,0:T(2,128)} %ranks_ref.5) | copy-start | bytes 76
  27.9 3.6 %collective-permute-start.10 = (bf16[2,32,200]{2,1,0:T(8,128)(2,1)S(1)}, bf16[2,32,200]{2,1,0:T(8,128)(2,1)S(1)}, u32[]{:S(2)}, u32[]{:S(2)}) collective-permute-start(bf16[2,32,200]{2,1,0:T(8,128)(2,1)S(1)} %shard_map.116.own_ref), channel_id=1, source_target_pairs={{0,1},{1,0},{2,3},{3,2},{4,5},{5,4},{6,7},{7,6},{8,9},{9,8},{10,11... | collective-permute-start | bytes 76808 | tf_op jit(solution)/shard_map/ppermute | solution.py:55
  31.6 4.5 %copy-start.5 = (f32[2,64,768]{2,1,0:T(8,128)S(1)}, f32[2,64,768]{2,1,0:T(8,128)}, u32[]{:S(2)}) copy-start(f32[2,64,768]{2,1,0:T(8,128)} %rhs_ref.1) | copy-start | bytes 1179652
  31.6 5.6 %collective-permute-start.13 = (bf16[32,1536]{1,0:T(8,128)(2,1)S(1)}, bf16[32,1536]{1,0:T(8,128)(2,1)S(1)}, u32[]{:S(2)}, u32[]{:S(2)}) collective-permute-start(bf16[32,1536]{1,0:T(8,128)(2,1)S(1)} %add_add_fusion.3), channel_id=1, source_target_pairs={{0,6},{1,25},{2,4},{3,27},{4,2},{5,29},{6,0},{7,31},{8,14},{9,17},... | collective-permute-start | bytes 294920 | tf_op jit(solution)/shard_map/ppermute | solution.py:44
  33.8 4.6 %collective-permute-start.12 = (bf16[32,1536]{1,0:T(8,128)(2,1)S(1)}, bf16[32,1536]{1,0:T(8,128)(2,1)S(1)}, u32[]{:S(2)}, u32[]{:S(2)}) collective-permute-start(bf16[32,1536]{1,0:T(8,128)(2,1)S(1)} %add_add_fusion.3), channel_id=1, source_target_pairs={{0,4},{1,17},{2,6},{3,19},{4,0},{5,21},{6,2},{7,23},{8,12},{9,25},... | collective-permute-start | bytes 294920 | tf_op jit(solution)/shard_map/ppermute | solution.py:44
  34.3 4.6 %collective-permute-start.11 = (bf16[32,1536]{1,0:T(8,128)(2,1)S(1)}, bf16[32,1536]{1,0:T(8,128)(2,1)S(1)}, u32[]{:S(2)}, u32[]{:S(2)}) collective-permute-start(bf16[32,1536]{1,0:T(8,128)(2,1)S(1)} %add_add_fusion.3), channel_id=1, source_target_pairs={{0,2},{1,9},{2,0},{3,11},{4,6},{5,13},{6,4},{7,15},{8,10},{9,1},{1... | collective-permute-start | bytes 294920 | tf_op jit(solution)/shard_map/ppermute | solution.py:44
  39.5 5.6 %collective-permute-start.16 = (bf16[32,1536]{1,0:T(8,128)(2,1)S(1)}, bf16[32,1536]{1,0:T(8,128)(2,1)S(1)}, u32[]{:S(2)}, u32[]{:S(2)}) collective-permute-start(bf16[32,1536]{1,0:T(8,128)(2,1)S(1)} %shard_map.120), channel_id=1, source_target_pairs={{0,6},{1,25},{2,4},{3,27},{4,2},{5,29},{6,0},{7,31},{8,14},{9,17},... | collective-permute-start | bytes 294920 | tf_op jit(solution)/shard_map/ppermute | solution.py:44
  41.4 4.7 %collective-permute-start.15 = (bf16[32,1536]{1,0:T(8,128)(2,1)S(1)}, bf16[32,1536]{1,0:T(8,128)(2,1)S(1)}, u32[]{:S(2)}, u32[]{:S(2)}) collective-permute-start(bf16[32,1536]{1,0:T(8,128)(2,1)S(1)} %shard_map.120), channel_id=1, source_target_pairs={{0,4},{1,17},{2,6},{3,19},{4,0},{5,21},{6,2},{7,23},{8,12},{9,25},... | collective-permute-start | bytes 294920 | tf_op jit(solution)/shard_map/ppermute | solution.py:44
  41.9 4.6 %collective-permute-start.14 = (bf16[32,1536]{1,0:T(8,128)(2,1)S(1)}, bf16[32,1536]{1,0:T(8,128)(2,1)S(1)}, u32[]{:S(2)}, u32[]{:S(2)}) collective-permute-start(bf16[32,1536]{1,0:T(8,128)(2,1)S(1)} %shard_map.120), channel_id=1, source_target_pairs={{0,2},{1,9},{2,0},{3,11},{4,6},{5,13},{6,4},{7,15},{8,10},{9,1},{1... | collective-permute-start | bytes 294920 | tf_op jit(solution)/shard_map/ppermute | solution.py:44
  43.5 1.2 %collective-permute-start.17 = (bf16[2,32,200]{2,1,0:T(8,128)(2,1)S(1)}, bf16[2,32,200]{2,1,0:T(8,128)(2,1)S(1)}, u32[]{:S(2)}, u32[]{:S(2)}) collective-permute-start(bf16[2,32,200]{2,1,0:T(8,128)(2,1)S(1)} %shard_map.121.own_ref), channel_id=1, source_target_pairs={{0,1},{1,0},{2,3},{3,2},{4,5},{5,4},{6,7},{7,6},{8,9},{9,8},{10,11... | collective-permute-start | bytes 76808 | tf_op jit(solution)/shard_map/ppermute | solution.py:55
  46.5 6.5 %collective-permute-start.20 = (bf16[32,1536]{1,0:T(8,128)(2,1)S(1)}, bf16[32,1536]{1,0:T(8,128)(2,1)S(1)}, u32[]{:S(2)}, u32[]{:S(2)}) collective-permute-start(bf16[32,1536]{1,0:T(8,128)(2,1)S(1)} %add_add_fusion.1), channel_id=1, source_target_pairs={{0,24},{1,7},{2,26},{3,5},{4,28},{5,3},{6,30},{7,1},{8,16},{9,15},... | collective-permute-start | bytes 294920 | tf_op jit(solution)/shard_map/ppermute | solution.py:44
  48.7 6.3 %collective-permute-start.19 = (bf16[32,1536]{1,0:T(8,128)(2,1)S(1)}, bf16[32,1536]{1,0:T(8,128)(2,1)S(1)}, u32[]{:S(2)}, u32[]{:S(2)}) collective-permute-start(bf16[32,1536]{1,0:T(8,128)(2,1)S(1)} %add_add_fusion.1), channel_id=1, source_target_pairs={{0,16},{1,5},{2,18},{3,7},{4,20},{5,1},{6,22},{7,3},{8,24},{9,13},... | collective-permute-start | bytes 294920 | tf_op jit(solution)/shard_map/ppermute | solution.py:44
  48.7 6.3 %collective-permute-start.18 = (bf16[32,1536]{1,0:T(8,128)(2,1)S(1)}, bf16[32,1536]{1,0:T(8,128)(2,1)S(1)}, u32[]{:S(2)}, u32[]{:S(2)}) collective-permute-start(bf16[32,1536]{1,0:T(8,128)(2,1)S(1)} %add_add_fusion.1), channel_id=1, source_target_pairs={{0,8},{1,3},{2,10},{3,1},{4,12},{5,7},{6,14},{7,5},{8,0},{9,11},{1... | collective-permute-start | bytes 294920 | tf_op jit(solution)/shard_map/ppermute | solution.py:44
  55.6 1.2 %collective-permute-start.21 = (bf16[2,32,200]{2,1,0:T(8,128)(2,1)S(1)}, bf16[2,32,200]{2,1,0:T(8,128)(2,1)S(1)}, u32[]{:S(2)}, u32[]{:S(2)}) collective-permute-start(bf16[2,32,200]{2,1,0:T(8,128)(2,1)S(1)} %shard_map.123.weights_ref), channel_id=1, source_target_pairs={{0,1},{1,0},{2,3},{3,2},{4,5},{5,4},{6,7},{7,6},{8,9},{9,8},{10,11... | collective-permute-start | bytes 76808 | tf_op jit(solution)/shard_map/ppermute | solution.py:55

commit v6 on v5

--- a/solution.py
+++ b/solution.py
@@ -29,10 +29,8 @@
 
 def spread(block, slots, cores, turn, beside=()):
     if slots & (slots - 1):
-        for work in beside:
-            work()
-        return lax.psum(block, "tc")
-    beside = list(beside)
+        return lax.psum(block, "tc"), [work() for work in beside]
+    beside, done = list(beside), []
     for flips in exchanges(slots):
         received = []
         for flip in flips:
@@ -43,12 +41,11 @@
             ]
             received.append(lax.ppermute(block, ("tc", "pr"), pairs))
         if beside:
-            block, received, _ = lax.optimization_barrier((block, received, beside.pop(0)()))
+            block, received, result = lax.optimization_barrier((block, received, beside.pop(0)()))
+            done.append(result)
         for part in received:
             block = block + part
-    for work in beside:
-        work()
-    return block
+    return block, done + [work() for work in beside]
 
 
 def swap(block, cores):
@@ -243,8 +240,6 @@
         size * size,
         FIRST_LIMIT,
     )(pivot_owner, rhs, inverse)
-    block, future_left = lax.optimization_barrier((block, future_left))
-    other_left = swap(future_left, cores)
 
     def ahead(current):
         return call(
@@ -280,11 +275,12 @@
             (),
             product_flops,
             2 * rows * rank * size,
-        )(solved[pivot], future_left, other_left)[0]
+        )(solved[pivot], future_left, halves["other"])[0]
 
     solved = [None] * count
     total = future_rhs
     masked = None
+    halves = {}
     for current in reversed(range(count)):
         before = current + 1
         held = {}
@@ -292,7 +288,7 @@
         def early(current=current, before=before, held=held):
             if before == count:
                 held["ready"] = ahead(current) if current > 0 else ()
-                return held["ready"]
+                return held["ready"], future_left
             held["own"] = weigh(before)
             held["other"] = swap(held["own"], cores)
             if current > 0:
@@ -313,7 +309,9 @@
             )(held["own"], held["other"], held["masked"], total)[0]
             return held["total"]
 
-        solved[current] = spread(block, slots, cores, count - 1 - current, [early, late])
+        solved[current], done = spread(block, slots, cores, count - 1 - current, [early, late])
+        if before == count:
+            halves["other"] = swap(done[0][1], cores)
         total, masked = held.get("total", total), held.get("masked", masked)
         if current > 0:
             outs = call(

time: 57.9 us -> 57.8 us (level)
  no operation moved by 1% of the time
where the time goes in v6:
time: 57.8 us; the launch traced here: 57.6 us
  starting transfers between devices  25.3 us (44%)
  waiting for transfers between devices  17.3 us (30%)
  Pallas kernels  11.4 us (20%)
  local copies, waits for them, and re-layouts  2.63 us (5%)
  between operations  0.82 us (1%)
    ppermute x18, starting transfers between devices, spread(): received.append(lax.ppermute(block, ('tc', 'pr'), pairs))  25 us
    ppermute x18, waiting for transfers between devices, spread(): received.append(lax.ppermute(block, ('tc', 'pr'), pairs))  15.9 us
    pallas_call x1, Pallas kernels, local(): call(first_kernel, [wide, narrow], [ANY, ANY, ANY], [pltpu.VMEM((size, si...  2.98 us
    unnamed x22, local copies, waits for them, and re-layouts  2.63 us
    pallas_call x2, Pallas kernels, ahead(): call(functools.partial(ahead_kernel, current), [jax.ShapeDtypeStruct((ran...  2.59 us
    ppermute x4, waiting for transfers between devices, swap(): lax.ppermute(block, 'pr', [(core, cores - 1 - core) for core in range(cor...  1.47 us
    pallas_call x3, Pallas kernels, weigh(): call(functools.partial(weights_kernel, pivot), [jax.ShapeDtypeStruct((row...  1.41 us
  transfers between devices with their start and end apart: 22, of which 16 were waited for; matrix products, arithmetic and copies ran while one was open for 0% of the time, Pallas kernels for 11%

profile of v6, /device:TPU:0, one launch (start us, length us, event | category | flops | bytes accessed | tf_op | source)
XLA Modules:
  0.0 57.6 jit_solution(18331647766537274743)
XLA Ops:
  0.7 3.0 %shard_map.113 = (f32[32,1536]{1,0:T(8,128)}, bf16[32,1536]{1,0:T(8,128)(2,1)}) custom-call(s32[3]{0:T(128)} %owner_ref.5, f32[32,1536]{1,0:T(8,128)} %bitcast.18, bf16[1536,1536]{1,0:T(8,128)(2,1)} %bitcast.11), custom_call_target="tpu_custom_call" | custom-call | flops 75497472 | bytes 2359296 | tf_op jit(solution)/shard_map/pallas_call | solution.py:228
  3.6 4.0 %collective-permute-start.2 = (bf16[32,1536]{1,0:T(8,128)(2,1)}, bf16[32,1536]{1,0:T(8,128)(2,1)S(1)}, u32[]{:S(2)}, u32[]{:S(2)}) collective-permute-start(bf16[32,1536]{1,0:T(8,128)(2,1)} %get-tuple-element.43), channel_id=1, source_target_pairs={{0,6},{1,25},{2,4},{3,27},{4,2},{5,29},{6,0},{7,31},{8,14},{9,17},... | collective-permute-start | bytes 294920 | tf_op jit(solution)/shard_map/ppermute | solution.py:42
  7.6 0.5 collective-permute-start.1
  8.1 0.1 collective-permute-start
  8.3 1.3 %copy-done.2 = bf16[1,2,1536,200]{2,3,1,0:T(8,128)(2,1)S(1)} copy-done((bf16[1,2,1536,200]{2,3,1,0:T(8,128)(2,1)S(1)}, bf16[1,2,1536,200]{2,3,1,0:T(8,128)(2,1)}, u32[]{:S(2)}) %copy-start.2) | copy-done | bytes 1228824
  9.5 1.3 %copy-done.3 = bf16[1,2,1536,200]{2,3,1,0:T(8,128)(2,1)S(1)} copy-done((bf16[1,2,1536,200]{2,3,1,0:T(8,128)(2,1)S(1)}, bf16[1,2,1536,200]{2,3,1,0:T(8,128)(2,1)}, u32[]{:S(2)}) %copy-start.3) | copy-done | bytes 1228824
  10.8 1.3 %shard_map.114 = (bf16[200,1536]{1,0:T(8,128)(2,1)S(1)}, bf16[1536,200]{1,0:T(8,128)(2,1)S(1)}, f32[1,1536]{1,0:T(1,128)S(1)}) custom-call(s32[3]{0:T(128)S(1)} %copy-done.7, s32[1,2]{1,0:T(1,128)S(1)} %copy-done.8, bf16[2,200,1536]{2,1,0:T(8,128)(2,1)S(1)} %bitcast.14, bf16[2,200,1536]{2,1,0:T(8,128)(2,1)S(1)} %bitcast.16, bf16[1536,1536]{1,0:T(8,128)(2,1)S(1)} %bitcast.12), custom_call_target="tpu_custom_call" | custom-call | flops 471859200 | bytes 3588096 | tf_op jit(solution)/shard_map/pallas_call | solution.py:245
  12.1 0.3 collective-permute-done.1
  12.4 0.5 collective-permute-done
  12.9 0.1 collective-permute-start.9
  13.1 3.6 %collective-permute-start.5 = (bf16[32,1536]{1,0:T(8,128)(2,1)S(1)}, bf16[32,1536]{1,0:T(8,128)(2,1)S(1)}, u32[]{:S(2)}, u32[]{:S(2)}) collective-permute-start(bf16[32,1536]{1,0:T(8,128)(2,1)S(1)} %add_add_fusion.5), channel_id=1, source_target_pairs={{0,24},{1,7},{2,26},{3,5},{4,28},{5,3},{6,30},{7,1},{8,16},{9,15},... | collective-permute-start | bytes 294920 | tf_op jit(solution)/shard_map/ppermute | solution.py:42
  16.7 0.9 %collective-permute-start.3 = (bf16[32,1536]{1,0:T(8,128)(2,1)S(1)}, bf16[32,1536]{1,0:T(8,128)(2,1)S(1)}, u32[]{:S(2)}, u32[]{:S(2)}) collective-permute-start(bf16[32,1536]{1,0:T(8,128)(2,1)S(1)} %add_add_fusion.5), channel_id=1, source_target_pairs={{0,8},{1,3},{2,10},{3,1},{4,12},{5,7},{6,14},{7,5},{8,0},{9,11},{1... | collective-permute-start | bytes 294920 | tf_op jit(solution)/shard_map/ppermute | solution.py:42
  17.5 2.1 %collective-permute-done.5 = bf16[32,1536]{1,0:T(8,128)(2,1)S(1)} collective-permute-done((bf16[32,1536]{1,0:T(8,128)(2,1)S(1)}, bf16[32,1536]{1,0:T(8,128)(2,1)S(1)}, u32[]{:S(2)}, u32[]{:S(2)}) %collective-permute-start.5) | collective-permute-done | bytes 98336 | tf_op jit(solution)/shard_map/ppermute | solution.py:42
  19.7 2.6 %collective-permute-done.4 = bf16[32,1536]{1,0:T(8,128)(2,1)S(1)} collective-permute-done((bf16[32,1536]{1,0:T(8,128)(2,1)S(1)}, bf16[32,1536]{1,0:T(8,128)(2,1)S(1)}, u32[]{:S(2)}, u32[]{:S(2)}) %collective-permute-start.4) | collective-permute-done | bytes 98336 | tf_op jit(solution)/shard_map/ppermute | solution.py:42
  22.4 0.5 shard_map.115
  22.9 2.3 %collective-permute-start.8 = (bf16[32,1536]{1,0:T(8,128)(2,1)S(1)}, bf16[32,1536]{1,0:T(8,128)(2,1)S(1)}, u32[]{:S(2)}, u32[]{:S(2)}) collective-permute-start(bf16[32,1536]{1,0:T(8,128)(2,1)S(1)} %get-tuple-element.57), channel_id=1, source_target_pairs={{0,24},{1,7},{2,26},{3,5},{4,28},{5,3},{6,30},{7,1},{8,16},{9,15},... | collective-permute-start | bytes 294920 | tf_op jit(solution)/shard_map/ppermute | solution.py:42
  25.2 0.3 collective-permute-start.7
  25.5 1.8 %collective-permute-start.6 = (bf16[32,1536]{1,0:T(8,128)(2,1)S(1)}, bf16[32,1536]{1,0:T(8,128)(2,1)S(1)}, u32[]{:S(2)}, u32[]{:S(2)}) collective-permute-start(bf16[32,1536]{1,0:T(8,128)(2,1)S(1)} %get-tuple-element.57), channel_id=1, source_target_pairs={{0,8},{1,3},{2,10},{3,1},{4,12},{5,7},{6,14},{7,5},{8,0},{9,11},{1... | collective-permute-start | bytes 294920 | tf_op jit(solution)/shard_map/ppermute | solution.py:42
  27.4 0.5 shard_map.116.own_ref
  27.9 1.3 %shard_map.117 = (bf16[200,1536]{1,0:T(8,128)(2,1)S(1)}, bf16[1536,200]{1,0:T(8,128)(2,1)S(1)}, f32[1,1536]{1,0:T(1,128)S(1)}) custom-call(s32[3]{0:T(128)S(1)} %copy-done.7, s32[1,2]{1,0:T(1,128)S(1)} %copy-done.8, bf16[2,200,1536]{2,1,0:T(8,128)(2,1)S(1)} %bitcast.15, bf16[2,200,1536]{2,1,0:T(8,128)(2,1)S(1)} %bitcast.17, bf16[1536,1536]{1,0:T(8,128)(2,1)S(1)} %bitcast.13), custom_call_target="tpu_custom_call" | custom-call | flops 471859200 | bytes 3588096 | tf_op jit(solution)/shard_map/pallas_call | solution.py:245
  29.2 0.2 collective-permute-done.8
  29.4 2.1 %collective-permute-done.7 = bf16[32,1536]{1,0:T(8,128)(2,1)S(1)} collective-permute-done((bf16[32,1536]{1,0:T(8,128)(2,1)S(1)}, bf16[32,1536]{1,0:T(8,128)(2,1)S(1)}, u32[]{:S(2)}, u32[]{:S(2)}) %collective-permute-start.7) | collective-permute-done | bytes 98336 | tf_op jit(solution)/shard_map/ppermute | solution.py:42
  31.5 2.3 %collective-permute-start.13 = (bf16[32,1536]{1,0:T(8,128)(2,1)S(1)}, bf16[32,1536]{1,0:T(8,128)(2,1)S(1)}, u32[]{:S(2)}, u32[]{:S(2)}) collective-permute-start(bf16[32,1536]{1,0:T(8,128)(2,1)S(1)} %add_add_fusion.3), channel_id=1, source_target_pairs={{0,6},{1,25},{2,4},{3,27},{4,2},{5,29},{6,0},{7,31},{8,14},{9,17},... | collective-permute-start | bytes 294920 | tf_op jit(solution)/shard_map/ppermute | solution.py:42
  33.8 0.5 collective-permute-start.12
  34.3 0.8 %collective-permute-start.11 = (bf16[32,1536]{1,0:T(8,128)(2,1)S(1)}, bf16[32,1536]{1,0:T(8,128)(2,1)S(1)}, u32[]{:S(2)}, u32[]{:S(2)}) collective-permute-start(bf16[32,1536]{1,0:T(8,128)(2,1)S(1)} %add_add_fusion.3), channel_id=1, source_target_pairs={{0,2},{1,9},{2,0},{3,11},{4,6},{5,13},{6,4},{7,15},{8,10},{9,1},{1... | collective-permute-start | bytes 294920 | tf_op jit(solution)/shard_map/ppermute | solution.py:42
  35.1 0.9 %shard_map.118.right_ref = bf16[2,3,200,768]{3,2,1,0:T(8,128)(2,1)S(1)} custom-call(s32[2,3]{1,0:T(2,128)S(1)} %copy-done.9, bf16[2,3,200,768]{3,2,1,0:T(8,128)(2,1)S(1)} %copy-done.4), custom_call_target="tpu_custom_call" | custom-call | flops 921600 | bytes 3686400 | tf_op jit(solution)/shard_map/pallas_call | solution.py:259
  36.0 0.3 shard_map.119.rhs_ref
  36.3 0.8 %collective-permute-done.13 = bf16[32,1536]{1,0:T(8,128)(2,1)S(1)} collective-permute-done((bf16[32,1536]{1,0:T(8,128)(2,1)S(1)}, bf16[32,1536]{1,0:T(8,128)(2,1)S(1)}, u32[]{:S(2)}, u32[]{:S(2)}) %collective-permute-start.13) | collective-permute-done | bytes 98336 | tf_op jit(solution)/shard_map/ppermute | solution.py:42
  37.1 1.3 %collective-permute-done.12 = bf16[32,1536]{1,0:T(8,128)(2,1)S(1)} collective-permute-done((bf16[32,1536]{1,0:T(8,128)(2,1)S(1)}, bf16[32,1536]{1,0:T(8,128)(2,1)S(1)}, u32[]{:S(2)}, u32[]{:S(2)}) %collective-permute-start.12) | collective-permute-done | bytes 98336 | tf_op jit(solution)/shard_map/ppermute | solution.py:42
  38.4 0.5 collective-permute-done.11
  39.0 0.5 shard_map.120
  39.5 1.8 %collective-permute-start.16 = (bf16[32,1536]{1,0:T(8,128)(2,1)S(1)}, bf16[32,1536]{1,0:T(8,128)(2,1)S(1)}, u32[]{:S(2)}, u32[]{:S(2)}) collective-permute-start(bf16[32,1536]{1,0:T(8,128)(2,1)S(1)} %shard_map.120), channel_id=1, source_target_pairs={{0,6},{1,25},{2,4},{3,27},{4,2},{5,29},{6,0},{7,31},{8,14},{9,17},... | collective-permute-start | bytes 294920 | tf_op jit(solution)/shard_map/ppermute | solution.py:42
  41.3 0.5 collective-permute-start.15
  41.8 1.3 %collective-permute-start.14 = (bf16[32,1536]{1,0:T(8,128)(2,1)S(1)}, bf16[32,1536]{1,0:T(8,128)(2,1)S(1)}, u32[]{:S(2)}, u32[]{:S(2)}) collective-permute-start(bf16[32,1536]{1,0:T(8,128)(2,1)S(1)} %shard_map.120), channel_id=1, source_target_pairs={{0,2},{1,9},{2,0},{3,11},{4,6},{5,13},{6,4},{7,15},{8,10},{9,1},{1... | collective-permute-start | bytes 294920 | tf_op jit(solution)/shard_map/ppermute | solution.py:42
  43.1 0.5 shard_map.121.own_ref
  43.6 1.2 %collective-permute-done.17.other_ref = bf16[2,32,200]{2,1,0:T(8,128)(2,1)S(1)} collective-permute-done((bf16[2,32,200]{2,1,0:T(8,128)(2,1)S(1)}, bf16[2,32,200]{2,1,0:T(8,128)(2,1)S(1)}, u32[]{:S(2)}, u32[]{:S(2)}) %collective-permute-start.17) | collective-permute-done | bytes 25632 | tf_op jit(solution)/shard_map/ppermute | solution.py:52
  44.8 0.3 collective-permute-done.16
  45.1 1.0 %collective-permute-done.15 = bf16[32,1536]{1,0:T(8,128)(2,1)S(1)} collective-permute-done((bf16[32,1536]{1,0:T(8,128)(2,1)S(1)}, bf16[32,1536]{1,0:T(8,128)(2,1)S(1)}, u32[]{:S(2)}, u32[]{:S(2)}) %collective-permute-start.15) | collective-permute-done | bytes 98336 | tf_op jit(solution)/shard_map/ppermute | solution.py:42
  46.1 0.3 collective-permute-done.14
  46.4 2.4 %collective-permute-start.20 = (bf16[32,1536]{1,0:T(8,128)(2,1)S(1)}, bf16[32,1536]{1,0:T(8,128)(2,1)S(1)}, u32[]{:S(2)}, u32[]{:S(2)}) collective-permute-start(bf16[32,1536]{1,0:T(8,128)(2,1)S(1)} %add_add_fusion.1), channel_id=1, source_target_pairs={{0,24},{1,7},{2,26},{3,5},{4,28},{5,3},{6,30},{7,1},{8,16},{9,15},... | collective-permute-start | bytes 294920 | tf_op jit(solution)/shard_map/ppermute | solution.py:42
  48.8 2.1 %collective-permute-start.18 = (bf16[32,1536]{1,0:T(8,128)(2,1)S(1)}, bf16[32,1536]{1,0:T(8,128)(2,1)S(1)}, u32[]{:S(2)}, u32[]{:S(2)}) collective-permute-start(bf16[32,1536]{1,0:T(8,128)(2,1)S(1)} %add_add_fusion.1), channel_id=1, source_target_pairs={{0,8},{1,3},{2,10},{3,1},{4,12},{5,7},{6,14},{7,5},{8,0},{9,11},{1... | collective-permute-start | bytes 294920 | tf_op jit(solution)/shard_map/ppermute | solution.py:42
  50.9 0.3 shard_map.122.rhs_ref
  51.2 1.7 %collective-permute-done.20 = bf16[32,1536]{1,0:T(8,128)(2,1)S(1)} collective-permute-done((bf16[32,1536]{1,0:T(8,128)(2,1)S(1)}, bf16[32,1536]{1,0:T(8,128)(2,1)S(1)}, u32[]{:S(2)}, u32[]{:S(2)}) %collective-permute-start.20) | collective-permute-done | bytes 98336 | tf_op jit(solution)/shard_map/ppermute | solution.py:42
  53.0 2.1 %collective-permute-done.19 = bf16[32,1536]{1,0:T(8,128)(2,1)S(1)} collective-permute-done((bf16[32,1536]{1,0:T(8,128)(2,1)S(1)}, bf16[32,1536]{1,0:T(8,128)(2,1)S(1)}, u32[]{:S(2)}, u32[]{:S(2)}) %collective-permute-start.19) | collective-permute-done | bytes 98336 | tf_op jit(solution)/shard_map/ppermute | solution.py:42
  55.1 0.5 shard_map.123.weights_ref
  55.6 0.9 %shard_map.124 = (f32[2,64,768]{2,1,0:T(8,128)}, bf16[3,32,1536]{2,1,0:T(8,128)(2,1)}) custom-call(bf16[2,32,200]{2,1,0:T(8,128)(2,1)S(1)} %shard_map.123.weights_ref, bf16[2,3,200,768]{3,2,1,0:T(8,128)(2,1)S(1)} %shard_map.118.right_ref, f32[2,64,768]{2,1,0:T(8,128)S(1)} %shard_map.122.rhs_ref, bf16[32,1536]{1,0:T(8,128)(2,1)S(1)} %add_add_fusion.solved_ref.refs_0_, ...), custom_call_target="tpu_custom_call" | custom-call | flops 19660800 | bytes 393216 | tf_op jit(solution)/shard_map/pallas_call | solution.py:332
  56.5 0.3 collective-permute-done.21.weights_ref
  56.8 0.9 %shard_map.125 = f32[2,64,768]{2,1,0:T(8,128)} custom-call(bf16[2,32,200]{2,1,0:T(8,128)(2,1)S(1)} %collective-permute-done.21.weights_ref, bf16[2,3,200,768]{3,2,1,0:T(8,128)(2,1)S(1)} %shard_map.118.right_ref, f32[2,64,768]{2,1,0:T(8,128)S(1)} %shard_map.122.rhs_ref, f32[2,64,768]{2,1,0:T(8,128)} %get-tuple-element.75.held_ref), custom_call_target="tpu_custom_call", output_to_operand_aliasing={{}: (3, {})} | custom-call | flops 19660800 | bytes 393216 | tf_op jit(solution)/shard_map/pallas_call | solution.py:344
  (37 shorter events, 0.4 us)
Async XLA Ops:
  0.6 7.6 %copy-start = (bf16[1,1536,1536]{2,1,0:T(8,128)(2,1)S(1)}, bf16[1,1536,1536]{2,1,0:T(8,128)(2,1)}, u32[]{:S(2)}) copy-start(bf16[1,1536,1536]{2,1,0:T(8,128)(2,1)} %param.11) | copy-start | bytes 14155780
  0.6 7.6 %copy-start.7 = (s32[3]{0:T(128)S(1)}, s32[3]{0:T(128)}, u32[]{:S(2)}) copy-start(s32[3]{0:T(128)} %owner_ref.5) | copy-start | bytes 40
  0.7 7.6 %copy-start.8 = (s32[1,2]{1,0:T(1,128)S(1)}, s32[1,2]{1,0:T(1,128)}, u32[]{:S(2)}) copy-start(s32[1,2]{1,0:T(1,128)} %ranks_ref.4) | copy-start | bytes 28
  3.6 8.5 %collective-permute-start.2 = (bf16[32,1536]{1,0:T(8,128)(2,1)}, bf16[32,1536]{1,0:T(8,128)(2,1)S(1)}, u32[]{:S(2)}, u32[]{:S(2)}) collective-permute-start(bf16[32,1536]{1,0:T(8,128)(2,1)} %get-tuple-element.43), channel_id=1, source_target_pairs={{0,6},{1,25},{2,4},{3,27},{4,2},{5,29},{6,0},{7,31},{8,14},{9,17},... | collective-permute-start | bytes 294920 | tf_op jit(solution)/shard_map/ppermute | solution.py:42
  7.6 4.8 %collective-permute-start.1 = (bf16[32,1536]{1,0:T(8,128)(2,1)}, bf16[32,1536]{1,0:T(8,128)(2,1)S(1)}, u32[]{:S(2)}, u32[]{:S(2)}) collective-permute-start(bf16[32,1536]{1,0:T(8,128)(2,1)} %get-tuple-element.43), channel_id=1, source_target_pairs={{0,4},{1,17},{2,6},{3,19},{4,0},{5,21},{6,2},{7,23},{8,12},{9,25},... | collective-permute-start | bytes 294920 | tf_op jit(solution)/shard_map/ppermute | solution.py:42
  8.1 4.8 %collective-permute-start = (bf16[32,1536]{1,0:T(8,128)(2,1)}, bf16[32,1536]{1,0:T(8,128)(2,1)S(1)}, u32[]{:S(2)}, u32[]{:S(2)}) collective-permute-start(bf16[32,1536]{1,0:T(8,128)(2,1)} %get-tuple-element.43), channel_id=1, source_target_pairs={{0,2},{1,9},{2,0},{3,11},{4,6},{5,13},{6,4},{7,15},{8,10},{9,1},{1... | collective-permute-start | bytes 294920 | tf_op jit(solution)/shard_map/ppermute | solution.py:42
  8.3 1.3 %copy-start.2 = (bf16[1,2,1536,200]{2,3,1,0:T(8,128)(2,1)S(1)}, bf16[1,2,1536,200]{2,3,1,0:T(8,128)(2,1)}, u32[]{:S(2)}) copy-start(bf16[1,2,1536,200]{2,3,1,0:T(8,128)(2,1)} %param.14) | copy-start | bytes 3686404
  9.5 1.3 %copy-start.3 = (bf16[1,2,1536,200]{2,3,1,0:T(8,128)(2,1)S(1)}, bf16[1,2,1536,200]{2,3,1,0:T(8,128)(2,1)}, u32[]{:S(2)}) copy-start(bf16[1,2,1536,200]{2,3,1,0:T(8,128)(2,1)} %param.13) | copy-start | bytes 3686404
  10.8 2.1 %copy-start.1 = (bf16[2,3,200,768]{3,2,1,0:T(8,128)(2,1)S(1)}, bf16[2,3,200,768]{3,2,1,0:T(8,128)(2,1)}, u32[]{:S(2)}) copy-start(bf16[2,3,200,768]{3,2,1,0:T(8,128)(2,1)} %own_ref.5) | copy-start | bytes 5529604
  10.8 2.2 %copy-start.10 = (bf16[32,1536]{1,0:T(8,128)(2,1)S(1)}, bf16[32,1536]{1,0:T(8,128)(2,1)}, u32[]{:S(2)}) copy-start(bf16[32,1536]{1,0:T(8,128)(2,1)} %get-tuple-element.43) | copy-start | bytes 294916
  10.8 11.5 %copy-start.6 = (f32[32,1536]{1,0:T(8,128)S(1)}, f32[32,1536]{1,0:T(8,128)}, u32[]{:S(2)}) copy-start(f32[32,1536]{1,0:T(8,128)} %get-tuple-element.51.raw_ref) | copy-start | bytes 589828
  12.9 14.4 %collective-permute-start.9 = (bf16[2,3,200,768]{3,2,1,0:T(8,128)(2,1)S(1)}, bf16[2,3,200,768]{3,2,1,0:T(8,128)(2,1)S(1)}, u32[]{:S(2)}, u32[]{:S(2)}) collective-permute-start(bf16[2,3,200,768]{3,2,1,0:T(8,128)(2,1)S(1)} %copy-done.1), channel_id=1, source_target_pairs={{0,1},{1,0},{2,3},{3,2},{4,5},{5,4},{6,7},{7,6},{8,9},{9,8},{10,11... | collective-permute-start | bytes 5529608 | tf_op jit(solution)/shard_map/ppermute | solution.py:52
  13.1 6.6 %collective-permute-start.5 = (bf16[32,1536]{1,0:T(8,128)(2,1)S(1)}, bf16[32,1536]{1,0:T(8,128)(2,1)S(1)}, u32[]{:S(2)}, u32[]{:S(2)}) collective-permute-start(bf16[32,1536]{1,0:T(8,128)(2,1)S(1)} %add_add_fusion.5), channel_id=1, source_target_pairs={{0,24},{1,7},{2,26},{3,5},{4,28},{5,3},{6,30},{7,1},{8,16},{9,15},... | collective-permute-start | bytes 294920 | tf_op jit(solution)/shard_map/ppermute | solution.py:42
  16.7 5.7 %collective-permute-start.4 = (bf16[32,1536]{1,0:T(8,128)(2,1)S(1)}, bf16[32,1536]{1,0:T(8,128)(2,1)S(1)}, u32[]{:S(2)}, u32[]{:S(2)}) collective-permute-start(bf16[32,1536]{1,0:T(8,128)(2,1)S(1)} %add_add_fusion.5), channel_id=1, source_target_pairs={{0,16},{1,5},{2,18},{3,7},{4,20},{5,1},{6,22},{7,3},{8,24},{9,13},... | collective-permute-start | bytes 294920 | tf_op jit(solution)/shard_map/ppermute | solution.py:42
  16.7 5.7 %collective-permute-start.3 = (bf16[32,1536]{1,0:T(8,128)(2,1)S(1)}, bf16[32,1536]{1,0:T(8,128)(2,1)S(1)}, u32[]{:S(2)}, u32[]{:S(2)}) collective-permute-start(bf16[32,1536]{1,0:T(8,128)(2,1)S(1)} %add_add_fusion.5), channel_id=1, source_target_pairs={{0,8},{1,3},{2,10},{3,1},{4,12},{5,7},{6,14},{7,5},{8,0},{9,11},{1... | collective-permute-start | bytes 294920 | tf_op jit(solution)/shard_map/ppermute | solution.py:42
  22.9 6.5 %collective-permute-start.8 = (bf16[32,1536]{1,0:T(8,128)(2,1)S(1)}, bf16[32,1536]{1,0:T(8,128)(2,1)S(1)}, u32[]{:S(2)}, u32[]{:S(2)}) collective-permute-start(bf16[32,1536]{1,0:T(8,128)(2,1)S(1)} %get-tuple-element.57), channel_id=1, source_target_pairs={{0,24},{1,7},{2,26},{3,5},{4,28},{5,3},{6,30},{7,1},{8,16},{9,15},... | collective-permute-start | bytes 294920 | tf_op jit(solution)/shard_map/ppermute | solution.py:42
  25.2 6.2 %collective-permute-start.7 = (bf16[32,1536]{1,0:T(8,128)(2,1)S(1)}, bf16[32,1536]{1,0:T(8,128)(2,1)S(1)}, u32[]{:S(2)}, u32[]{:S(2)}) collective-permute-start(bf16[32,1536]{1,0:T(8,128)(2,1)S(1)} %get-tuple-element.57), channel_id=1, source_target_pairs={{0,16},{1,5},{2,18},{3,7},{4,20},{5,1},{6,22},{7,3},{8,24},{9,13},... | collective-permute-start | bytes 294920 | tf_op jit(solution)/shard_map/ppermute | solution.py:42
  25.5 6.0 %collective-permute-start.6 = (bf16[32,1536]{1,0:T(8,128)(2,1)S(1)}, bf16[32,1536]{1,0:T(8,128)(2,1)S(1)}, u32[]{:S(2)}, u32[]{:S(2)}) collective-permute-start(bf16[32,1536]{1,0:T(8,128)(2,1)S(1)} %get-tuple-element.57), channel_id=1, source_target_pairs={{0,8},{1,3},{2,10},{3,1},{4,12},{5,7},{6,14},{7,5},{8,0},{9,11},{1... | collective-permute-start | bytes 294920 | tf_op jit(solution)/shard_map/ppermute | solution.py:42
  27.8 7.3 %copy-start.4 = (bf16[2,3,200,768]{3,2,1,0:T(8,128)(2,1)S(1)}, bf16[2,3,200,768]{3,2,1,0:T(8,128)(2,1)}, u32[]{:S(2)}) copy-start(bf16[2,3,200,768]{3,2,1,0:T(8,128)(2,1)} %right_ref.1) | copy-start | bytes 5529604
  27.9 7.2 %copy-start.9 = (s32[2,3]{1,0:T(2,128)S(1)}, s32[2,3]{1,0:T(2,128)}, u32[]{:S(2)}) copy-start(s32[2,3]{1,0:T(2,128)} %ranks_ref.5) | copy-start | bytes 76
  27.9 3.6 %collective-permute-start.10 = (bf16[2,32,200]{2,1,0:T(8,128)(2,1)S(1)}, bf16[2,32,200]{2,1,0:T(8,128)(2,1)S(1)}, u32[]{:S(2)}, u32[]{:S(2)}) collective-permute-start(bf16[2,32,200]{2,1,0:T(8,128)(2,1)S(1)} %shard_map.116.own_ref), channel_id=1, source_target_pairs={{0,1},{1,0},{2,3},{3,2},{4,5},{5,4},{6,7},{7,6},{8,9},{9,8},{10,11... | collective-permute-start | bytes 76808 | tf_op jit(solution)/shard_map/ppermute | solution.py:52
  31.5 4.5 %copy-start.5 = (f32[2,64,768]{2,1,0:T(8,128)S(1)}, f32[2,64,768]{2,1,0:T(8,128)}, u32[]{:S(2)}) copy-start(f32[2,64,768]{2,1,0:T(8,128)} %rhs_ref.1) | copy-start | bytes 1179652
  31.5 5.6 %collective-permute-start.13 = (bf16[32,1536]{1,0:T(8,128)(2,1)S(1)}, bf16[32,1536]{1,0:T(8,128)(2,1)S(1)}, u32[]{:S(2)}, u32[]{:S(2)}) collective-permute-start(bf16[32,1536]{1,0:T(8,128)(2,1)S(1)} %add_add_fusion.3), channel_id=1, source_target_pairs={{0,6},{1,25},{2,4},{3,27},{4,2},{5,29},{6,0},{7,31},{8,14},{9,17},... | collective-permute-start | bytes 294920 | tf_op jit(solution)/shard_map/ppermute | solution.py:42
  33.8 4.6 %collective-permute-start.12 = (bf16[32,1536]{1,0:T(8,128)(2,1)S(1)}, bf16[32,1536]{1,0:T(8,128)(2,1)S(1)}, u32[]{:S(2)}, u32[]{:S(2)}) collective-permute-start(bf16[32,1536]{1,0:T(8,128)(2,1)S(1)} %add_add_fusion.3), channel_id=1, source_target_pairs={{0,4},{1,17},{2,6},{3,19},{4,0},{5,21},{6,2},{7,23},{8,12},{9,25},... | collective-permute-start | bytes 294920 | tf_op jit(solution)/shard_map/ppermute | solution.py:42
  34.3 4.6 %collective-permute-start.11 = (bf16[32,1536]{1,0:T(8,128)(2,1)S(1)}, bf16[32,1536]{1,0:T(8,128)(2,1)S(1)}, u32[]{:S(2)}, u32[]{:S(2)}) collective-permute-start(bf16[32,1536]{1,0:T(8,128)(2,1)S(1)} %add_add_fusion.3), channel_id=1, source_target_pairs={{0,2},{1,9},{2,0},{3,11},{4,6},{5,13},{6,4},{7,15},{8,10},{9,1},{1... | collective-permute-start | bytes 294920 | tf_op jit(solution)/shard_map/ppermute | solution.py:42
  39.5 5.6 %collective-permute-start.16 = (bf16[32,1536]{1,0:T(8,128)(2,1)S(1)}, bf16[32,1536]{1,0:T(8,128)(2,1)S(1)}, u32[]{:S(2)}, u32[]{:S(2)}) collective-permute-start(bf16[32,1536]{1,0:T(8,128)(2,1)S(1)} %shard_map.120), channel_id=1, source_target_pairs={{0,6},{1,25},{2,4},{3,27},{4,2},{5,29},{6,0},{7,31},{8,14},{9,17},... | collective-permute-start | bytes 294920 | tf_op jit(solution)/shard_map/ppermute | solution.py:42
  41.3 4.9 %collective-permute-start.15 = (bf16[32,1536]{1,0:T(8,128)(2,1)S(1)}, bf16[32,1536]{1,0:T(8,128)(2,1)S(1)}, u32[]{:S(2)}, u32[]{:S(2)}) collective-permute-start(bf16[32,1536]{1,0:T(8,128)(2,1)S(1)} %shard_map.120), channel_id=1, source_target_pairs={{0,4},{1,17},{2,6},{3,19},{4,0},{5,21},{6,2},{7,23},{8,12},{9,25},... | collective-permute-start | bytes 294920 | tf_op jit(solution)/shard_map/ppermute | solution.py:42
  41.8 4.6 %collective-permute-start.14 = (bf16[32,1536]{1,0:T(8,128)(2,1)S(1)}, bf16[32,1536]{1,0:T(8,128)(2,1)S(1)}, u32[]{:S(2)}, u32[]{:S(2)}) collective-permute-start(bf16[32,1536]{1,0:T(8,128)(2,1)S(1)} %shard_map.120), channel_id=1, source_target_pairs={{0,2},{1,9},{2,0},{3,11},{4,6},{5,13},{6,4},{7,15},{8,10},{9,1},{1... | collective-permute-start | bytes 294920 | tf_op jit(solution)/shard_map/ppermute | solution.py:42
  43.5 1.2 %collective-permute-start.17 = (bf16[2,32,200]{2,1,0:T(8,128)(2,1)S(1)}, bf16[2,32,200]{2,1,0:T(8,128)(2,1)S(1)}, u32[]{:S(2)}, u32[]{:S(2)}) collective-permute-start(bf16[2,32,200]{2,1,0:T(8,128)(2,1)S(1)} %shard_map.121.own_ref), channel_id=1, source_target_pairs={{0,1},{1,0},{2,3},{3,2},{4,5},{5,4},{6,7},{7,6},{8,9},{9,8},{10,11... | collective-permute-start | bytes 76808 | tf_op jit(solution)/shard_map/ppermute | solution.py:52
  46.4 6.5 %collective-permute-start.20 = (bf16[32,1536]{1,0:T(8,128)(2,1)S(1)}, bf16[32,1536]{1,0:T(8,128)(2,1)S(1)}, u32[]{:S(2)}, u32[]{:S(2)}) collective-permute-start(bf16[32,1536]{1,0:T(8,128)(2,1)S(1)} %add_add_fusion.1), channel_id=1, source_target_pairs={{0,24},{1,7},{2,26},{3,5},{4,28},{5,3},{6,30},{7,1},{8,16},{9,15},... | collective-permute-start | bytes 294920 | tf_op jit(solution)/shard_map/ppermute | solution.py:42
  48.8 6.2 %collective-permute-start.19 = (bf16[32,1536]{1,0:T(8,128)(2,1)S(1)}, bf16[32,1536]{1,0:T(8,128)(2,1)S(1)}, u32[]{:S(2)}, u32[]{:S(2)}) collective-permute-start(bf16[32,1536]{1,0:T(8,128)(2,1)S(1)} %add_add_fusion.1), channel_id=1, source_target_pairs={{0,16},{1,5},{2,18},{3,7},{4,20},{5,1},{6,22},{7,3},{8,24},{9,13},... | collective-permute-start | bytes 294920 | tf_op jit(solution)/shard_map/ppermute | solution.py:42
  48.8 6.2 %collective-permute-start.18 = (bf16[32,1536]{1,0:T(8,128)(2,1)S(1)}, bf16[32,1536]{1,0:T(8,128)(2,1)S(1)}, u32[]{:S(2)}, u32[]{:S(2)}) collective-permute-start(bf16[32,1536]{1,0:T(8,128)(2,1)S(1)} %add_add_fusion.1), channel_id=1, source_target_pairs={{0,8},{1,3},{2,10},{3,1},{4,12},{5,7},{6,14},{7,5},{8,0},{9,11},{1... | collective-permute-start | bytes 294920 | tf_op jit(solution)/shard_map/ppermute | solution.py:42
  55.5 1.2 %collective-permute-start.21 = (bf16[2,32,200]{2,1,0:T(8,128)(2,1)S(1)}, bf16[2,32,200]{2,1,0:T(8,128)(2,1)S(1)}, u32[]{:S(2)}, u32[]{:S(2)}) collective-permute-start(bf16[2,32,200]{2,1,0:T(8,128)(2,1)S(1)} %shard_map.123.weights_ref), channel_id=1, source_target_pairs={{0,1},{1,0},{2,3},{3,2},{4,5},{5,4},{6,7},{7,6},{8,9},{9,8},{10,11... | collective-permute-start | bytes 76808 | tf_op jit(solution)/shard_map/ppermute | solution.py:52

commit v7 on v5

--- a/solution.py
+++ b/solution.py
@@ -31,9 +31,11 @@
     if slots & (slots - 1):
         for work in beside:
             work()
-        return lax.psum(block, "tc")
+        return [lax.psum(block, "tc")]
+    parts = [block]
     beside = list(beside)
     for flips in exchanges(slots):
+        block = functools.reduce(jnp.add, parts)
         received = []
         for flip in flips:
             pairs = [
@@ -44,11 +46,10 @@
             received.append(lax.ppermute(block, ("tc", "pr"), pairs))
         if beside:
             block, received, _ = lax.optimization_barrier((block, received, beside.pop(0)()))
-        for part in received:
-            block = block + part
+        parts = [block, *received]
     for work in beside:
         work()
-    return block
+    return parts
 
 
 def swap(block, cores):
@@ -123,8 +124,15 @@
             out_ref[row, pivot] = jnp.where(rank_ids < ranks_ref[row, pivot], tile, 0.0).astype(jnp.bfloat16)
 
 
-def step_kernel(solved_ref, ahead_ref, turned_ref, flag_ref, raw_ref, *outs):
-    factor = jnp.dot(solved_ref[...], turned_ref[...], preferred_element_type=jnp.float32).astype(jnp.bfloat16)
+def sum_of(part_refs):
+    return functools.reduce(jnp.add, [ref[...] for ref in part_refs])
+
+
+def step_kernel(count, *refs):
+    ahead_ref, turned_ref, flag_ref, raw_ref, solved_ref, *outs = refs[count:]
+    solved = sum_of(refs[:count])
+    solved_ref[...] = solved
+    factor = jnp.dot(solved, turned_ref[...], preferred_element_type=jnp.float32).astype(jnp.bfloat16)
     raw = raw_ref[...] - jnp.dot(factor, ahead_ref[...], preferred_element_type=jnp.float32)
     outs[0][...] = jnp.where(flag_ref[...] > 0.5, raw, 0.0).astype(jnp.bfloat16)
     if len(outs) > 1:
@@ -141,6 +149,26 @@
         weights_ref[row] = (
             lax.dot_general(own_part, own_ref[row, pivot], dims, preferred_element_type=jnp.float32)
             + lax.dot_general(other_part, other_ref[row, pivot], dims, preferred_element_type=jnp.float32)
+        ).astype(jnp.bfloat16)
+
+
+def turn_kernel(own_ref, other_ref, own_out_ref, other_out_ref):
+    for row in range(own_ref.shape[0]):
+        own_out_ref[row] = own_ref[row, 0].T
+        other_out_ref[row] = other_ref[row, 0].T
+
+
+def last_weights_kernel(count, *refs):
+    own_ref, other_ref, weights_ref, solved_ref = refs[count:]
+    solved_ref[...] = sum_of(refs[:count])
+    core = lax.axis_index("pr")
+    half = own_ref.shape[1]
+    own_part = solved_ref[:, pl.ds(pl.multiple_of(core * half, half), half)]
+    other_part = solved_ref[:, pl.ds(pl.multiple_of((1 - core) * half, half), half)]
+    for row in range(own_ref.shape[0]):
+        weights_ref[row] = (
+            jnp.dot(own_part, own_ref[row], preferred_element_type=jnp.float32)
+            + jnp.dot(other_part, other_ref[row], preferred_element_type=jnp.float32)
         ).astype(jnp.bfloat16)
 
 
@@ -282,6 +310,18 @@
             2 * rows * rank * size,
         )(solved[pivot], future_left, other_left)[0]
 
+    def turn():
+        half = future_left.shape[3]
+        return call(
+            turn_kernel,
+            [jax.ShapeDtypeStruct((rows, half, rank), jnp.bfloat16)] * 2,
+            [VMEM] * 2,
+            (),
+            rows * rank * size,
+            4 * rows * rank * size,
+        )(future_left, other_left)
+
+    turned = []
     solved = [None] * count
     total = future_rhs
     masked = None
@@ -303,6 +343,8 @@
             if before == count:
                 return None
             held["masked"] = mask() if masked is None else masked
+            if not turned:
+                turned.extend(turn())
             held["total"] = call(
                 functools.partial(update_kernel, before),
                 [jax.ShapeDtypeStruct(total.shape, jnp.float32)],
@@ -311,23 +353,32 @@
                 product_flops,
                 rows * rank * size + 2 * 4 * total.size,
             )(held["own"], held["other"], held["masked"], total)[0]
-            return held["total"]
-
-        solved[current] = spread(block, slots, cores, count - 1 - current, [early, late])
+            return held["total"], list(turned)
+
+        parts = spread(block, slots, cores, count - 1 - current, [early, late])
         total, masked = held.get("total", total), held.get("masked", masked)
         if current > 0:
             outs = call(
-                step_kernel,
-                [narrow, wide] if current > 1 else [narrow],
-                [VMEM] * 5,
+                functools.partial(step_kernel, len(parts)),
+                [narrow, narrow, wide] if current > 1 else [narrow, narrow],
+                [VMEM] * (len(parts) + 4),
                 (),
                 4 * probes * rank * size,
                 4 * rank * size,
-            )(solved[current], *held["ready"], raw)
-            block, raw = outs[0], outs[-1]
+            )(*parts, *held["ready"], raw)
+            solved[current], block, raw = outs[0], outs[1], outs[-1]
     if masked is None:
         masked = mask()
-    own = weigh(0)
+    if not turned:
+        turned.extend(turn())
+    own, solved[0] = call(
+        functools.partial(last_weights_kernel, len(parts)),
+        [jax.ShapeDtypeStruct((rows, probes, rank), jnp.bfloat16), narrow],
+        [VMEM] * (len(parts) + 2),
+        (),
+        product_flops,
+        2 * rows * rank * size,
+    )(*parts, *turned)
     other = swap(own, cores)
     half = total.shape[2]
     scratch = [pltpu.VMEM((rows, probes, half), jnp.float32), pltpu.SemaphoreType.DMA((rows,))]

time: 57.9 us -> 57.7 us (level)
  waiting for transfers between devices: 17.4 us -> 16.4 us
    ppermute x18, waiting for transfers between devices: 16 us -> 15 us  [spread(): received.append(lax.ppermute(block, ('tc', 'pr'), pairs))]
    pallas_call x2 -> x4, Pallas kernels: 1.1 us -> 1.92 us  [the longest x2 1.09 us: local(): call(functools.partial(step_kernel, len(parts)), [narrow, narrow, wide] i...]
    pallas_call x3 -> x2, Pallas kernels: 1.41 us -> 0.94 us  [weigh(): call(functools.partial(weights_kernel, pivot), [jax.ShapeDtypeStruct((row...]
  transfers between devices with their start and end apart: 22 -> 22, of which waited for: 16 -> 15; matrix products, arithmetic and copies ran while one was open for 0% -> 0% of each run, Pallas kernels for 11% -> 12%
where the time goes in v7:
time: 57.7 us; the launch traced here: 57.5 us
  starting transfers between devices  25.3 us (44%)
  waiting for transfers between devices  16.4 us (28%)
  Pallas kernels  11.8 us (20%)
  local copies, waits for them, and re-layouts  3.14 us (5%)
  between operations  0.82 us (1%)
    ppermute x18, starting transfers between devices, spread(): received.append(lax.ppermute(block, ('tc', 'pr'), pairs))  24.6 us
    ppermute x18, waiting for transfers between devices, spread(): received.append(lax.ppermute(block, ('tc', 'pr'), pairs))  15 us
    unnamed x22, local copies, waits for them, and re-layouts  3.14 us
    pallas_call x1, Pallas kernels, local(): call(first_kernel, [wide, narrow], [ANY, ANY, ANY], [pltpu.VMEM((size, si...  2.98 us
    pallas_call x2, Pallas kernels, ahead(): call(functools.partial(ahead_kernel, current), [jax.ShapeDtypeStruct((ran...  2.58 us
    ppermute x4, waiting for transfers between devices, swap(): lax.ppermute(block, 'pr', [(core, cores - 1 - core) for core in range(cor...  1.47 us
  transfers between devices with their start and end apart: 22, of which 15 were waited for; matrix products, arithmetic and copies ran while one was open for 0% of the time, Pallas kernels for 12%

profile of v7, /device:TPU:0, one launch (start us, length us, event | category | flops | bytes accessed | tf_op | source)
XLA Modules:
  0.0 57.5 jit_solution(1094324928976008539)
XLA Ops:
  0.7 3.0 %shard_map.113 = (f32[32,1536]{1,0:T(8,128)}, bf16[32,1536]{1,0:T(8,128)(2,1)}) custom-call(s32[3]{0:T(128)} %owner_ref.5, f32[32,1536]{1,0:T(8,128)} %bitcast.18, bf16[1536,1536]{1,0:T(8,128)(2,1)} %bitcast.11), custom_call_target="tpu_custom_call" | custom-call | flops 75497472 | bytes 2359296 | tf_op jit(solution)/shard_map/pallas_call | solution.py:259
  3.6 0.5 collective-permute-start.9
  4.2 3.5 %collective-permute-start.2 = (bf16[32,1536]{1,0:T(8,128)(2,1)}, bf16[32,1536]{1,0:T(8,128)(2,1)S(1)}, u32[]{:S(2)}, u32[]{:S(2)}) collective-permute-start(bf16[32,1536]{1,0:T(8,128)(2,1)} %get-tuple-element.52), channel_id=1, source_target_pairs={{0,6},{1,25},{2,4},{3,27},{4,2},{5,29},{6,0},{7,31},{8,14},{9,17},... | collective-permute-start | bytes 294920 | tf_op jit(solution)/shard_map/ppermute | solution.py:46
  7.7 0.5 collective-permute-start.1
  8.3 1.3 %copy-done.2 = bf16[1,2,1536,200]{2,3,1,0:T(8,128)(2,1)S(1)} copy-done((bf16[1,2,1536,200]{2,3,1,0:T(8,128)(2,1)S(1)}, bf16[1,2,1536,200]{2,3,1,0:T(8,128)(2,1)}, u32[]{:S(2)}) %copy-start.2) | copy-done | bytes 1228824
  9.6 1.3 %copy-done.3 = bf16[1,2,1536,200]{2,3,1,0:T(8,128)(2,1)S(1)} copy-done((bf16[1,2,1536,200]{2,3,1,0:T(8,128)(2,1)S(1)}, bf16[1,2,1536,200]{2,3,1,0:T(8,128)(2,1)}, u32[]{:S(2)}) %copy-start.3) | copy-done | bytes 1228824
  10.9 1.3 %shard_map.114 = (bf16[200,1536]{1,0:T(8,128)(2,1)S(1)}, bf16[1536,200]{1,0:T(8,128)(2,1)S(1)}, f32[1,1536]{1,0:T(1,128)S(1)}) custom-call(s32[3]{0:T(128)S(1)} %copy-done.7, s32[1,2]{1,0:T(1,128)S(1)} %copy-done.8, bf16[2,200,1536]{2,1,0:T(8,128)(2,1)S(1)} %bitcast.14, bf16[2,200,1536]{2,1,0:T(8,128)(2,1)S(1)} %bitcast.16, bf16[1536,1536]{1,0:T(8,128)(2,1)S(1)} %bitcast.12), custom_call_target="tpu_custom_call" | custom-call | flops 471859200 | bytes 3588096 | tf_op jit(solution)/shard_map/pallas_call | solution.py:278
  12.2 0.3 collective-permute-done.1
  12.5 0.5 collective-permute-done
  13.1 3.7 %collective-permute-start.5 = (bf16[32,1536]{1,0:T(8,128)(2,1)S(1)}, bf16[32,1536]{1,0:T(8,128)(2,1)S(1)}, u32[]{:S(2)}, u32[]{:S(2)}) collective-permute-start(bf16[32,1536]{1,0:T(8,128)(2,1)S(1)} %add_add_fusion.2.refs_0_), channel_id=1, source_target_pairs={{0,24},{1,7},{2,26},{3,5},{4,28},{5,3},{6,30},{7,1},{8,16},{9,15},... | collective-permute-start | bytes 294920 | tf_op jit(solution)/shard_map/ppermute | solution.py:46
  16.7 0.8 %collective-permute-start.3 = (bf16[32,1536]{1,0:T(8,128)(2,1)S(1)}, bf16[32,1536]{1,0:T(8,128)(2,1)S(1)}, u32[]{:S(2)}, u32[]{:S(2)}) collective-permute-start(bf16[32,1536]{1,0:T(8,128)(2,1)S(1)} %add_add_fusion.2.refs_0_), channel_id=1, source_target_pairs={{0,8},{1,3},{2,10},{3,1},{4,12},{5,7},{6,14},{7,5},{8,0},{9,11},{1... | collective-permute-start | bytes 294920 | tf_op jit(solution)/shard_map/ppermute | solution.py:46
  17.5 2.1 %collective-permute-done.5.refs_3_ = bf16[32,1536]{1,0:T(8,128)(2,1)S(1)} collective-permute-done((bf16[32,1536]{1,0:T(8,128)(2,1)S(1)}, bf16[32,1536]{1,0:T(8,128)(2,1)S(1)}, u32[]{:S(2)}, u32[]{:S(2)}) %collective-permute-start.5) | collective-permute-done | bytes 98336 | tf_op jit(solution)/shard_map/ppermute | solution.py:46
  19.6 2.7 %collective-permute-done.4.refs_2_ = bf16[32,1536]{1,0:T(8,128)(2,1)S(1)} collective-permute-done((bf16[32,1536]{1,0:T(8,128)(2,1)S(1)}, bf16[32,1536]{1,0:T(8,128)(2,1)S(1)}, u32[]{:S(2)}, u32[]{:S(2)}) %collective-permute-start.4) | collective-permute-done | bytes 98336 | tf_op jit(solution)/shard_map/ppermute | solution.py:46
  22.4 0.5 shard_map.115
  22.9 2.2 %collective-permute-start.8 = (bf16[32,1536]{1,0:T(8,128)(2,1)S(1)}, bf16[32,1536]{1,0:T(8,128)(2,1)S(1)}, u32[]{:S(2)}, u32[]{:S(2)}) collective-permute-start(bf16[32,1536]{1,0:T(8,128)(2,1)S(1)} %get-tuple-element.67), channel_id=1, source_target_pairs={{0,24},{1,7},{2,26},{3,5},{4,28},{5,3},{6,30},{7,1},{8,16},{9,15},... | collective-permute-start | bytes 294920 | tf_op jit(solution)/shard_map/ppermute | solution.py:46
  25.2 0.4 collective-permute-start.7
  25.6 1.8 %collective-permute-start.6 = (bf16[32,1536]{1,0:T(8,128)(2,1)S(1)}, bf16[32,1536]{1,0:T(8,128)(2,1)S(1)}, u32[]{:S(2)}, u32[]{:S(2)}) collective-permute-start(bf16[32,1536]{1,0:T(8,128)(2,1)S(1)} %get-tuple-element.67), channel_id=1, source_target_pairs={{0,8},{1,3},{2,10},{3,1},{4,12},{5,7},{6,14},{7,5},{8,0},{9,11},{1... | collective-permute-start | bytes 294920 | tf_op jit(solution)/shard_map/ppermute | solution.py:46
  27.4 0.5 shard_map.116.own_ref
  28.0 1.3 %shard_map.117 = (bf16[200,1536]{1,0:T(8,128)(2,1)S(1)}, bf16[1536,200]{1,0:T(8,128)(2,1)S(1)}, f32[1,1536]{1,0:T(1,128)S(1)}) custom-call(s32[3]{0:T(128)S(1)} %copy-done.7, s32[1,2]{1,0:T(1,128)S(1)} %copy-done.8, bf16[2,200,1536]{2,1,0:T(8,128)(2,1)S(1)} %bitcast.15, bf16[2,200,1536]{2,1,0:T(8,128)(2,1)S(1)} %bitcast.17, bf16[1536,1536]{1,0:T(8,128)(2,1)S(1)} %bitcast.13), custom_call_target="tpu_custom_call" | custom-call | flops 471859200 | bytes 3588096 | tf_op jit(solution)/shard_map/pallas_call | solution.py:278
  29.3 0.2 collective-permute-done.8
  29.4 2.1 %collective-permute-done.7 = bf16[32,1536]{1,0:T(8,128)(2,1)S(1)} collective-permute-done((bf16[32,1536]{1,0:T(8,128)(2,1)S(1)}, bf16[32,1536]{1,0:T(8,128)(2,1)S(1)}, u32[]{:S(2)}, u32[]{:S(2)}) %collective-permute-start.7) | collective-permute-done | bytes 98336 | tf_op jit(solution)/shard_map/ppermute | solution.py:46
  31.6 2.2 %collective-permute-start.13 = (bf16[32,1536]{1,0:T(8,128)(2,1)S(1)}, bf16[32,1536]{1,0:T(8,128)(2,1)S(1)}, u32[]{:S(2)}, u32[]{:S(2)}) collective-permute-start(bf16[32,1536]{1,0:T(8,128)(2,1)S(1)} %add_add_fusion.1.refs_0_), channel_id=1, source_target_pairs={{0,6},{1,25},{2,4},{3,27},{4,2},{5,29},{6,0},{7,31},{8,14},{9,17},... | collective-permute-start | bytes 294920 | tf_op jit(solution)/shard_map/ppermute | solution.py:46
  33.7 0.5 collective-permute-start.12
  34.2 0.9 %collective-permute-start.11 = (bf16[32,1536]{1,0:T(8,128)(2,1)S(1)}, bf16[32,1536]{1,0:T(8,128)(2,1)S(1)}, u32[]{:S(2)}, u32[]{:S(2)}) collective-permute-start(bf16[32,1536]{1,0:T(8,128)(2,1)S(1)} %add_add_fusion.1.refs_0_), channel_id=1, source_target_pairs={{0,2},{1,9},{2,0},{3,11},{4,6},{5,13},{6,4},{7,15},{8,10},{9,1},{1... | collective-permute-start | bytes 294920 | tf_op jit(solution)/shard_map/ppermute | solution.py:46
  35.1 0.9 %shard_map.118.right_ref = bf16[2,3,200,768]{3,2,1,0:T(8,128)(2,1)S(1)} custom-call(s32[2,3]{1,0:T(2,128)S(1)} %copy-done.9, bf16[2,3,200,768]{3,2,1,0:T(8,128)(2,1)S(1)} %copy-done.4), custom_call_target="tpu_custom_call" | custom-call | flops 921600 | bytes 3686400 | tf_op jit(solution)/shard_map/pallas_call | solution.py:292
  36.0 0.5 shard_map.120
  36.5 0.5 copy-done.5
  37.0 0.3 shard_map.119.rhs_ref
  37.3 1.0 %collective-permute-done.12.refs_2_ = bf16[32,1536]{1,0:T(8,128)(2,1)S(1)} collective-permute-done((bf16[32,1536]{1,0:T(8,128)(2,1)S(1)}, bf16[32,1536]{1,0:T(8,128)(2,1)S(1)}, u32[]{:S(2)}, u32[]{:S(2)}) %collective-permute-start.12) | collective-permute-done | bytes 98336 | tf_op jit(solution)/shard_map/ppermute | solution.py:46
  38.3 0.5 collective-permute-done.11.refs_1_
  38.8 0.5 shard_map.121
  39.4 1.9 %collective-permute-start.16 = (bf16[32,1536]{1,0:T(8,128)(2,1)S(1)}, bf16[32,1536]{1,0:T(8,128)(2,1)S(1)}, u32[]{:S(2)}, u32[]{:S(2)}) collective-permute-start(bf16[32,1536]{1,0:T(8,128)(2,1)S(1)} %get-tuple-element.80), channel_id=1, source_target_pairs={{0,6},{1,25},{2,4},{3,27},{4,2},{5,29},{6,0},{7,31},{8,14},{9,17},... | collective-permute-start | bytes 294920 | tf_op jit(solution)/shard_map/ppermute | solution.py:46
  41.3 0.5 collective-permute-start.15
  41.8 1.1 %collective-permute-start.14 = (bf16[32,1536]{1,0:T(8,128)(2,1)S(1)}, bf16[32,1536]{1,0:T(8,128)(2,1)S(1)}, u32[]{:S(2)}, u32[]{:S(2)}) collective-permute-start(bf16[32,1536]{1,0:T(8,128)(2,1)S(1)} %get-tuple-element.80), channel_id=1, source_target_pairs={{0,2},{1,9},{2,0},{3,11},{4,6},{5,13},{6,4},{7,15},{8,10},{9,1},{1... | collective-permute-start | bytes 294920 | tf_op jit(solution)/shard_map/ppermute | solution.py:46
  42.9 0.5 shard_map.122.own_ref
  43.4 1.2 %collective-permute-done.17.other_ref = bf16[2,32,200]{2,1,0:T(8,128)(2,1)S(1)} collective-permute-done((bf16[2,32,200]{2,1,0:T(8,128)(2,1)S(1)}, bf16[2,32,200]{2,1,0:T(8,128)(2,1)S(1)}, u32[]{:S(2)}, u32[]{:S(2)}) %collective-permute-start.17) | collective-permute-done | bytes 25632 | tf_op jit(solution)/shard_map/ppermute | solution.py:56
  44.6 0.3 collective-permute-done.16
  45.0 1.0 %collective-permute-done.15 = bf16[32,1536]{1,0:T(8,128)(2,1)S(1)} collective-permute-done((bf16[32,1536]{1,0:T(8,128)(2,1)S(1)}, bf16[32,1536]{1,0:T(8,128)(2,1)S(1)}, u32[]{:S(2)}, u32[]{:S(2)}) %collective-permute-start.15) | collective-permute-done | bytes 98336 | tf_op jit(solution)/shard_map/ppermute | solution.py:46
  46.0 0.4 collective-permute-done.14
  46.4 2.2 %collective-permute-start.20 = (bf16[32,1536]{1,0:T(8,128)(2,1)S(1)}, bf16[32,1536]{1,0:T(8,128)(2,1)S(1)}, u32[]{:S(2)}, u32[]{:S(2)}) collective-permute-start(bf16[32,1536]{1,0:T(8,128)(2,1)S(1)} %add_add_fusion.refs_0_), channel_id=1, source_target_pairs={{0,24},{1,7},{2,26},{3,5},{4,28},{5,3},{6,30},{7,1},{8,16},{9,15},... | collective-permute-start | bytes 294920 | tf_op jit(solution)/shard_map/ppermute | solution.py:46
  48.7 2.2 %collective-permute-start.18 = (bf16[32,1536]{1,0:T(8,128)(2,1)S(1)}, bf16[32,1536]{1,0:T(8,128)(2,1)S(1)}, u32[]{:S(2)}, u32[]{:S(2)}) collective-permute-start(bf16[32,1536]{1,0:T(8,128)(2,1)S(1)} %add_add_fusion.refs_0_), channel_id=1, source_target_pairs={{0,8},{1,3},{2,10},{3,1},{4,12},{5,7},{6,14},{7,5},{8,0},{9,11},{1... | collective-permute-start | bytes 294920 | tf_op jit(solution)/shard_map/ppermute | solution.py:46
  50.9 0.3 shard_map.123.rhs_ref
  51.2 1.7 %collective-permute-done.20.refs_3_ = bf16[32,1536]{1,0:T(8,128)(2,1)S(1)} collective-permute-done((bf16[32,1536]{1,0:T(8,128)(2,1)S(1)}, bf16[32,1536]{1,0:T(8,128)(2,1)S(1)}, u32[]{:S(2)}, u32[]{:S(2)}) %collective-permute-start.20) | collective-permute-done | bytes 98336 | tf_op jit(solution)/shard_map/ppermute | solution.py:46
  53.0 2.1 %collective-permute-done.19.refs_2_ = bf16[32,1536]{1,0:T(8,128)(2,1)S(1)} collective-permute-done((bf16[32,1536]{1,0:T(8,128)(2,1)S(1)}, bf16[32,1536]{1,0:T(8,128)(2,1)S(1)}, u32[]{:S(2)}, u32[]{:S(2)}) %collective-permute-start.19) | collective-permute-done | bytes 98336 | tf_op jit(solution)/shard_map/ppermute | solution.py:46
  55.0 0.4 shard_map.124
  55.4 0.9 %shard_map.125 = (f32[2,64,768]{2,1,0:T(8,128)}, bf16[3,32,1536]{2,1,0:T(8,128)(2,1)}) custom-call(bf16[2,32,200]{2,1,0:T(8,128)(2,1)S(1)} %get-tuple-element.88.weights_ref, bf16[2,3,200,768]{3,2,1,0:T(8,128)(2,1)S(1)} %shard_map.118.right_ref, f32[2,64,768]{2,1,0:T(8,128)S(1)} %shard_map.123.rhs_ref, bf16[32,1536]{1,0:T(8,128)(2,1)S(1)} %get-tuple-element.89.refs_0_, ...), custom_call_target="tpu_custom_call" | custom-call | flops 19660800 | bytes 393216 | tf_op jit(solution)/shard_map/pallas_call | solution.py:385
  56.3 0.3 collective-permute-done.21.weights_ref
  56.6 0.9 %shard_map.126 = f32[2,64,768]{2,1,0:T(8,128)} custom-call(bf16[2,32,200]{2,1,0:T(8,128)(2,1)S(1)} %collective-permute-done.21.weights_ref, bf16[2,3,200,768]{3,2,1,0:T(8,128)(2,1)S(1)} %shard_map.118.right_ref, f32[2,64,768]{2,1,0:T(8,128)S(1)} %shard_map.123.rhs_ref, f32[2,64,768]{2,1,0:T(8,128)} %get-tuple-element.91.held_ref), custom_call_target="tpu_custom_call", output_to_operand_aliasing={{}: (3, {})} | custom-call | flops 19660800 | bytes 393216 | tf_op jit(solution)/shard_map/pallas_call | solution.py:397
  (35 shorter events, 0.4 us)
Async XLA Ops:
  0.6 7.7 %copy-start = (bf16[1,1536,1536]{2,1,0:T(8,128)(2,1)S(1)}, bf16[1,1536,1536]{2,1,0:T(8,128)(2,1)}, u32[]{:S(2)}) copy-start(bf16[1,1536,1536]{2,1,0:T(8,128)(2,1)} %param.11) | copy-start | bytes 14155780
  0.6 7.7 %copy-start.7 = (s32[3]{0:T(128)S(1)}, s32[3]{0:T(128)}, u32[]{:S(2)}) copy-start(s32[3]{0:T(128)} %owner_ref.5) | copy-start | bytes 40
  0.7 7.7 %copy-start.8 = (s32[1,2]{1,0:T(1,128)S(1)}, s32[1,2]{1,0:T(1,128)}, u32[]{:S(2)}) copy-start(s32[1,2]{1,0:T(1,128)} %ranks_ref.4) | copy-start | bytes 28
  3.6 23.7 %collective-permute-start.9 = (bf16[2,3,200,768]{3,2,1,0:T(8,128)(2,1)}, bf16[2,3,200,768]{3,2,1,0:T(8,128)(2,1)S(1)}, u32[]{:S(2)}, u32[]{:S(2)}) collective-permute-start(bf16[2,3,200,768]{3,2,1,0:T(8,128)(2,1)} %own_ref.2), channel_id=1, source_target_pairs={{0,1},{1,0},{2,3},{3,2},{4,5},{5,4},{6,7},{7,6},{8,9},{9,8},{10,11... | collective-permute-start | bytes 5529608 | tf_op jit(solution)/shard_map/ppermute | solution.py:56
  4.2 8.1 %collective-permute-start.2 = (bf16[32,1536]{1,0:T(8,128)(2,1)}, bf16[32,1536]{1,0:T(8,128)(2,1)S(1)}, u32[]{:S(2)}, u32[]{:S(2)}) collective-permute-start(bf16[32,1536]{1,0:T(8,128)(2,1)} %get-tuple-element.52), channel_id=1, source_target_pairs={{0,6},{1,25},{2,4},{3,27},{4,2},{5,29},{6,0},{7,31},{8,14},{9,17},... | collective-permute-start | bytes 294920 | tf_op jit(solution)/shard_map/ppermute | solution.py:46
  7.7 4.8 %collective-permute-start.1 = (bf16[32,1536]{1,0:T(8,128)(2,1)}, bf16[32,1536]{1,0:T(8,128)(2,1)S(1)}, u32[]{:S(2)}, u32[]{:S(2)}) collective-permute-start(bf16[32,1536]{1,0:T(8,128)(2,1)} %get-tuple-element.52), channel_id=1, source_target_pairs={{0,4},{1,17},{2,6},{3,19},{4,0},{5,21},{6,2},{7,23},{8,12},{9,25},... | collective-permute-start | bytes 294920 | tf_op jit(solution)/shard_map/ppermute | solution.py:46
  8.2 4.8 %collective-permute-start = (bf16[32,1536]{1,0:T(8,128)(2,1)}, bf16[32,1536]{1,0:T(8,128)(2,1)S(1)}, u32[]{:S(2)}, u32[]{:S(2)}) collective-permute-start(bf16[32,1536]{1,0:T(8,128)(2,1)} %get-tuple-element.52), channel_id=1, source_target_pairs={{0,2},{1,9},{2,0},{3,11},{4,6},{5,13},{6,4},{7,15},{8,10},{9,1},{1... | collective-permute-start | bytes 294920 | tf_op jit(solution)/shard_map/ppermute | solution.py:46
  8.3 1.3 %copy-start.2 = (bf16[1,2,1536,200]{2,3,1,0:T(8,128)(2,1)S(1)}, bf16[1,2,1536,200]{2,3,1,0:T(8,128)(2,1)}, u32[]{:S(2)}) copy-start(bf16[1,2,1536,200]{2,3,1,0:T(8,128)(2,1)} %param.14) | copy-start | bytes 3686404
  9.6 1.3 %copy-start.3 = (bf16[1,2,1536,200]{2,3,1,0:T(8,128)(2,1)S(1)}, bf16[1,2,1536,200]{2,3,1,0:T(8,128)(2,1)}, u32[]{:S(2)}) copy-start(bf16[1,2,1536,200]{2,3,1,0:T(8,128)(2,1)} %param.13) | copy-start | bytes 3686404
  10.9 2.1 %copy-start.10 = (bf16[32,1536]{1,0:T(8,128)(2,1)S(1)}, bf16[32,1536]{1,0:T(8,128)(2,1)}, u32[]{:S(2)}) copy-start(bf16[32,1536]{1,0:T(8,128)(2,1)} %get-tuple-element.52) | copy-start | bytes 294916
  10.9 11.5 %copy-start.6 = (f32[32,1536]{1,0:T(8,128)S(1)}, f32[32,1536]{1,0:T(8,128)}, u32[]{:S(2)}) copy-start(f32[32,1536]{1,0:T(8,128)} %get-tuple-element.60.refs_7_) | copy-start | bytes 589828
  12.2 15.2 %copy-start.1 = (bf16[2,3,200,768]{3,2,1,0:T(8,128)(2,1)S(1)}, bf16[2,3,200,768]{3,2,1,0:T(8,128)(2,1)}, u32[]{:S(2)}) copy-start(bf16[2,3,200,768]{3,2,1,0:T(8,128)(2,1)} %own_ref.2) | copy-start | bytes 5529604
  13.1 6.6 %collective-permute-start.5 = (bf16[32,1536]{1,0:T(8,128)(2,1)S(1)}, bf16[32,1536]{1,0:T(8,128)(2,1)S(1)}, u32[]{:S(2)}, u32[]{:S(2)}) collective-permute-start(bf16[32,1536]{1,0:T(8,128)(2,1)S(1)} %add_add_fusion.2.refs_0_), channel_id=1, source_target_pairs={{0,24},{1,7},{2,26},{3,5},{4,28},{5,3},{6,30},{7,1},{8,16},{9,15},... | collective-permute-start | bytes 294920 | tf_op jit(solution)/shard_map/ppermute | solution.py:46
  16.7 5.7 %collective-permute-start.4 = (bf16[32,1536]{1,0:T(8,128)(2,1)S(1)}, bf16[32,1536]{1,0:T(8,128)(2,1)S(1)}, u32[]{:S(2)}, u32[]{:S(2)}) collective-permute-start(bf16[32,1536]{1,0:T(8,128)(2,1)S(1)} %add_add_fusion.2.refs_0_), channel_id=1, source_target_pairs={{0,16},{1,5},{2,18},{3,7},{4,20},{5,1},{6,22},{7,3},{8,24},{9,13},... | collective-permute-start | bytes 294920 | tf_op jit(solution)/shard_map/ppermute | solution.py:46
  16.7 5.7 %collective-permute-start.3 = (bf16[32,1536]{1,0:T(8,128)(2,1)S(1)}, bf16[32,1536]{1,0:T(8,128)(2,1)S(1)}, u32[]{:S(2)}, u32[]{:S(2)}) collective-permute-start(bf16[32,1536]{1,0:T(8,128)(2,1)S(1)} %add_add_fusion.2.refs_0_), channel_id=1, source_target_pairs={{0,8},{1,3},{2,10},{3,1},{4,12},{5,7},{6,14},{7,5},{8,0},{9,11},{1... | collective-permute-start | bytes 294920 | tf_op jit(solution)/shard_map/ppermute | solution.py:46
  22.9 6.5 %collective-permute-start.8 = (bf16[32,1536]{1,0:T(8,128)(2,1)S(1)}, bf16[32,1536]{1,0:T(8,128)(2,1)S(1)}, u32[]{:S(2)}, u32[]{:S(2)}) collective-permute-start(bf16[32,1536]{1,0:T(8,128)(2,1)S(1)} %get-tuple-element.67), channel_id=1, source_target_pairs={{0,24},{1,7},{2,26},{3,5},{4,28},{5,3},{6,30},{7,1},{8,16},{9,15},... | collective-permute-start | bytes 294920 | tf_op jit(solution)/shard_map/ppermute | solution.py:46
  25.2 6.3 %collective-permute-start.7 = (bf16[32,1536]{1,0:T(8,128)(2,1)S(1)}, bf16[32,1536]{1,0:T(8,128)(2,1)S(1)}, u32[]{:S(2)}, u32[]{:S(2)}) collective-permute-start(bf16[32,1536]{1,0:T(8,128)(2,1)S(1)} %get-tuple-element.67), channel_id=1, source_target_pairs={{0,16},{1,5},{2,18},{3,7},{4,20},{5,1},{6,22},{7,3},{8,24},{9,13},... | collective-permute-start | bytes 294920 | tf_op jit(solution)/shard_map/ppermute | solution.py:46
  25.6 6.0 %collective-permute-start.6 = (bf16[32,1536]{1,0:T(8,128)(2,1)S(1)}, bf16[32,1536]{1,0:T(8,128)(2,1)S(1)}, u32[]{:S(2)}, u32[]{:S(2)}) collective-permute-start(bf16[32,1536]{1,0:T(8,128)(2,1)S(1)} %get-tuple-element.67), channel_id=1, source_target_pairs={{0,8},{1,3},{2,10},{3,1},{4,12},{5,7},{6,14},{7,5},{8,0},{9,11},{1... | collective-permute-start | bytes 294920 | tf_op jit(solution)/shard_map/ppermute | solution.py:46
  27.9 7.2 %copy-start.4 = (bf16[2,3,200,768]{3,2,1,0:T(8,128)(2,1)S(1)}, bf16[2,3,200,768]{3,2,1,0:T(8,128)(2,1)}, u32[]{:S(2)}) copy-start(bf16[2,3,200,768]{3,2,1,0:T(8,128)(2,1)} %right_ref.1) | copy-start | bytes 5529604
  27.9 7.2 %copy-start.9 = (s32[2,3]{1,0:T(2,128)S(1)}, s32[2,3]{1,0:T(2,128)}, u32[]{:S(2)}) copy-start(s32[2,3]{1,0:T(2,128)} %ranks_ref.5) | copy-start | bytes 76
  27.9 3.6 %collective-permute-start.10 = (bf16[2,32,200]{2,1,0:T(8,128)(2,1)S(1)}, bf16[2,32,200]{2,1,0:T(8,128)(2,1)S(1)}, u32[]{:S(2)}, u32[]{:S(2)}) collective-permute-start(bf16[2,32,200]{2,1,0:T(8,128)(2,1)S(1)} %shard_map.116.own_ref), channel_id=1, source_target_pairs={{0,1},{1,0},{2,3},{3,2},{4,5},{5,4},{6,7},{7,6},{8,9},{9,8},{10,11... | collective-permute-start | bytes 76808 | tf_op jit(solution)/shard_map/ppermute | solution.py:56
  31.6 5.8 %collective-permute-start.13 = (bf16[32,1536]{1,0:T(8,128)(2,1)S(1)}, bf16[32,1536]{1,0:T(8,128)(2,1)S(1)}, u32[]{:S(2)}, u32[]{:S(2)}) collective-permute-start(bf16[32,1536]{1,0:T(8,128)(2,1)S(1)} %add_add_fusion.1.refs_0_), channel_id=1, source_target_pairs={{0,6},{1,25},{2,4},{3,27},{4,2},{5,29},{6,0},{7,31},{8,14},{9,17},... | collective-permute-start | bytes 294920 | tf_op jit(solution)/shard_map/ppermute | solution.py:46
  33.7 4.6 %collective-permute-start.12 = (bf16[32,1536]{1,0:T(8,128)(2,1)S(1)}, bf16[32,1536]{1,0:T(8,128)(2,1)S(1)}, u32[]{:S(2)}, u32[]{:S(2)}) collective-permute-start(bf16[32,1536]{1,0:T(8,128)(2,1)S(1)} %add_add_fusion.1.refs_0_), channel_id=1, source_target_pairs={{0,4},{1,17},{2,6},{3,19},{4,0},{5,21},{6,2},{7,23},{8,12},{9,25},... | collective-permute-start | bytes 294920 | tf_op jit(solution)/shard_map/ppermute | solution.py:46
  34.2 4.6 %collective-permute-start.11 = (bf16[32,1536]{1,0:T(8,128)(2,1)S(1)}, bf16[32,1536]{1,0:T(8,128)(2,1)S(1)}, u32[]{:S(2)}, u32[]{:S(2)}) collective-permute-start(bf16[32,1536]{1,0:T(8,128)(2,1)S(1)} %add_add_fusion.1.refs_0_), channel_id=1, source_target_pairs={{0,2},{1,9},{2,0},{3,11},{4,6},{5,13},{6,4},{7,15},{8,10},{9,1},{1... | collective-permute-start | bytes 294920 | tf_op jit(solution)/shard_map/ppermute | solution.py:46
  36.0 1.0 %copy-start.5 = (f32[2,64,768]{2,1,0:T(8,128)S(1)}, f32[2,64,768]{2,1,0:T(8,128)}, u32[]{:S(2)}) copy-start(f32[2,64,768]{2,1,0:T(8,128)} %rhs_ref.1) | copy-start | bytes 1179652
  39.4 5.6 %collective-permute-start.16 = (bf16[32,1536]{1,0:T(8,128)(2,1)S(1)}, bf16[32,1536]{1,0:T(8,128)(2,1)S(1)}, u32[]{:S(2)}, u32[]{:S(2)}) collective-permute-start(bf16[32,1536]{1,0:T(8,128)(2,1)S(1)} %get-tuple-element.80), channel_id=1, source_target_pairs={{0,6},{1,25},{2,4},{3,27},{4,2},{5,29},{6,0},{7,31},{8,14},{9,17},... | collective-permute-start | bytes 294920 | tf_op jit(solution)/shard_map/ppermute | solution.py:46
  41.3 4.7 %collective-permute-start.15 = (bf16[32,1536]{1,0:T(8,128)(2,1)S(1)}, bf16[32,1536]{1,0:T(8,128)(2,1)S(1)}, u32[]{:S(2)}, u32[]{:S(2)}) collective-permute-start(bf16[32,1536]{1,0:T(8,128)(2,1)S(1)} %get-tuple-element.80), channel_id=1, source_target_pairs={{0,4},{1,17},{2,6},{3,19},{4,0},{5,21},{6,2},{7,23},{8,12},{9,25},... | collective-permute-start | bytes 294920 | tf_op jit(solution)/shard_map/ppermute | solution.py:46
  41.8 4.6 %collective-permute-start.14 = (bf16[32,1536]{1,0:T(8,128)(2,1)S(1)}, bf16[32,1536]{1,0:T(8,128)(2,1)S(1)}, u32[]{:S(2)}, u32[]{:S(2)}) collective-permute-start(bf16[32,1536]{1,0:T(8,128)(2,1)S(1)} %get-tuple-element.80), channel_id=1, source_target_pairs={{0,2},{1,9},{2,0},{3,11},{4,6},{5,13},{6,4},{7,15},{8,10},{9,1},{1... | collective-permute-start | bytes 294920 | tf_op jit(solution)/shard_map/ppermute | solution.py:46
  43.4 1.2 %collective-permute-start.17 = (bf16[2,32,200]{2,1,0:T(8,128)(2,1)S(1)}, bf16[2,32,200]{2,1,0:T(8,128)(2,1)S(1)}, u32[]{:S(2)}, u32[]{:S(2)}) collective-permute-start(bf16[2,32,200]{2,1,0:T(8,128)(2,1)S(1)} %shard_map.122.own_ref), channel_id=1, source_target_pairs={{0,1},{1,0},{2,3},{3,2},{4,5},{5,4},{6,7},{7,6},{8,9},{9,8},{10,11... | collective-permute-start | bytes 76808 | tf_op jit(solution)/shard_map/ppermute | solution.py:56
  46.4 6.5 %collective-permute-start.20 = (bf16[32,1536]{1,0:T(8,128)(2,1)S(1)}, bf16[32,1536]{1,0:T(8,128)(2,1)S(1)}, u32[]{:S(2)}, u32[]{:S(2)}) collective-permute-start(bf16[32,1536]{1,0:T(8,128)(2,1)S(1)} %add_add_fusion.refs_0_), channel_id=1, source_target_pairs={{0,24},{1,7},{2,26},{3,5},{4,28},{5,3},{6,30},{7,1},{8,16},{9,15},... | collective-permute-start | bytes 294920 | tf_op jit(solution)/shard_map/ppermute | solution.py:46
  48.7 6.3 %collective-permute-start.19 = (bf16[32,1536]{1,0:T(8,128)(2,1)S(1)}, bf16[32,1536]{1,0:T(8,128)(2,1)S(1)}, u32[]{:S(2)}, u32[]{:S(2)}) collective-permute-start(bf16[32,1536]{1,0:T(8,128)(2,1)S(1)} %add_add_fusion.refs_0_), channel_id=1, source_target_pairs={{0,16},{1,5},{2,18},{3,7},{4,20},{5,1},{6,22},{7,3},{8,24},{9,13},... | collective-permute-start | bytes 294920 | tf_op jit(solution)/shard_map/ppermute | solution.py:46
  48.7 6.3 %collective-permute-start.18 = (bf16[32,1536]{1,0:T(8,128)(2,1)S(1)}, bf16[32,1536]{1,0:T(8,128)(2,1)S(1)}, u32[]{:S(2)}, u32[]{:S(2)}) collective-permute-start(bf16[32,1536]{1,0:T(8,128)(2,1)S(1)} %add_add_fusion.refs_0_), channel_id=1, source_target_pairs={{0,8},{1,3},{2,10},{3,1},{4,12},{5,7},{6,14},{7,5},{8,0},{9,11},{1... | collective-permute-start | bytes 294920 | tf_op jit(solution)/shard_map/ppermute | solution.py:46
  55.4 1.2 %collective-permute-start.21 = (bf16[2,32,200]{2,1,0:T(8,128)(2,1)S(1)}, bf16[2,32,200]{2,1,0:T(8,128)(2,1)S(1)}, u32[]{:S(2)}, u32[]{:S(2)}) collective-permute-start(bf16[2,32,200]{2,1,0:T(8,128)(2,1)S(1)} %get-tuple-element.88.weights_ref), channel_id=1, source_target_pairs={{0,1},{1,0},{2,3},{3,2},{4,5},{5,4},{6,7},{7,6},{8,9},{9,8},{10,11... | collective-permute-start | bytes 76808 | tf_op jit(solution)/shard_map/ppermute | solution.py:56

commit v8 on v7

--- a/solution.py
+++ b/solution.py
@@ -188,13 +188,17 @@
 
 def part_update(slot, weights_ref, right_ref, rhs_ref, out_ref, part, sems):
     copies = []
-    rows = probe_rows(slot, weights_ref.shape[1])
+    probes = weights_ref.shape[1]
+    rows = probe_rows(slot, probes)
+    width = rhs_ref.shape[2] // 2
     for row in range(rhs_ref.shape[0]):
-        part[row] = rhs_ref[row, rows, :] - jnp.dot(
-            weights_ref[row], right_ref[row, 0], preferred_element_type=jnp.float32
-        )
-        copies.append(pltpu.make_async_copy(part.at[row], out_ref.at[row, rows, :], sems.at[row]))
-        copies[-1].start()
+        for half in range(2):
+            cols = pl.ds(half * width, width)
+            part[row, :, cols] = rhs_ref[row, rows, cols] - jnp.dot(
+                weights_ref[row], right_ref[row, 0, :, cols], preferred_element_type=jnp.float32
+            )
+            copies.append(pltpu.make_async_copy(part.at[row, :, cols], out_ref.at[row, rows, cols], sems.at[2 * row + half]))
+            copies[-1].start()
     return copies
 
 
@@ -381,7 +385,7 @@
     )(*parts, *turned)
     other = swap(own, cores)
     half = total.shape[2]
-    scratch = [pltpu.VMEM((rows, probes, half), jnp.float32), pltpu.SemaphoreType.DMA((rows,))]
+    scratch = [pltpu.VMEM((rows, probes, half), jnp.float32), pltpu.SemaphoreType.DMA((2 * rows,))]
     partial, stacked = call(
         functools.partial(own_kernel, count),
         [

time: 57.7 us -> 57.7 us (level)
  no operation moved by 1% of the time
where the time goes in v8:
time: 57.7 us; the launch traced here: 57.5 us
  starting transfers between devices  25.3 us (44%)
  waiting for transfers between devices  16.4 us (28%)
  Pallas kernels  11.8 us (20%)
  local copies, waits for them, and re-layouts  3.14 us (5%)
  between operations  0.82 us (1%)
    ppermute x18, starting transfers between devices, spread(): received.append(lax.ppermute(block, ('tc', 'pr'), pairs))  24.6 us
    ppermute x18, waiting for transfers between devices, spread(): received.append(lax.ppermute(block, ('tc', 'pr'), pairs))  15 us
    unnamed x22, local copies, waits for them, and re-layouts  3.14 us
    pallas_call x1, Pallas kernels, local(): call(first_kernel, [wide, narrow], [ANY, ANY, ANY], [pltpu.VMEM((size, si...  2.98 us
    pallas_call x2, Pallas kernels, ahead(): call(functools.partial(ahead_kernel, current), [jax.ShapeDtypeStruct((ran...  2.58 us
    ppermute x4, waiting for transfers between devices, swap(): lax.ppermute(block, 'pr', [(core, cores - 1 - core) for core in range(cor...  1.43 us
  transfers between devices with their start and end apart: 22, of which 15 were waited for; matrix products, arithmetic and copies ran while one was open for 0% of the time, Pallas kernels for 12%

profile of v8, /device:TPU:0, one launch (start us, length us, event | category | flops | bytes accessed | tf_op | source)
XLA Modules:
  0.0 57.5 jit_solution(12679211231273541892)
XLA Ops:
  0.7 3.0 %shard_map.113 = (f32[32,1536]{1,0:T(8,128)}, bf16[32,1536]{1,0:T(8,128)(2,1)}) custom-call(s32[3]{0:T(128)} %owner_ref.5, f32[32,1536]{1,0:T(8,128)} %bitcast.18, bf16[1536,1536]{1,0:T(8,128)(2,1)} %bitcast.11), custom_call_target="tpu_custom_call" | custom-call | flops 75497472 | bytes 2359296 | tf_op jit(solution)/shard_map/pallas_call | solution.py:263
  3.6 0.5 collective-permute-start.9
  4.2 3.5 %collective-permute-start.2 = (bf16[32,1536]{1,0:T(8,128)(2,1)}, bf16[32,1536]{1,0:T(8,128)(2,1)S(1)}, u32[]{:S(2)}, u32[]{:S(2)}) collective-permute-start(bf16[32,1536]{1,0:T(8,128)(2,1)} %get-tuple-element.52), channel_id=1, source_target_pairs={{0,6},{1,25},{2,4},{3,27},{4,2},{5,29},{6,0},{7,31},{8,14},{9,17},... | collective-permute-start | bytes 294920 | tf_op jit(solution)/shard_map/ppermute | solution.py:46
  7.7 0.5 collective-permute-start.1
  8.3 1.3 %copy-done.2 = bf16[1,2,1536,200]{2,3,1,0:T(8,128)(2,1)S(1)} copy-done((bf16[1,2,1536,200]{2,3,1,0:T(8,128)(2,1)S(1)}, bf16[1,2,1536,200]{2,3,1,0:T(8,128)(2,1)}, u32[]{:S(2)}) %copy-start.2) | copy-done | bytes 1228824
  9.6 1.3 %copy-done.3 = bf16[1,2,1536,200]{2,3,1,0:T(8,128)(2,1)S(1)} copy-done((bf16[1,2,1536,200]{2,3,1,0:T(8,128)(2,1)S(1)}, bf16[1,2,1536,200]{2,3,1,0:T(8,128)(2,1)}, u32[]{:S(2)}) %copy-start.3) | copy-done | bytes 1228824
  10.9 1.3 %shard_map.114 = (bf16[200,1536]{1,0:T(8,128)(2,1)S(1)}, bf16[1536,200]{1,0:T(8,128)(2,1)S(1)}, f32[1,1536]{1,0:T(1,128)S(1)}) custom-call(s32[3]{0:T(128)S(1)} %copy-done.7, s32[1,2]{1,0:T(1,128)S(1)} %copy-done.8, bf16[2,200,1536]{2,1,0:T(8,128)(2,1)S(1)} %bitcast.14, bf16[2,200,1536]{2,1,0:T(8,128)(2,1)S(1)} %bitcast.16, bf16[1536,1536]{1,0:T(8,128)(2,1)S(1)} %bitcast.12), custom_call_target="tpu_custom_call" | custom-call | flops 471859200 | bytes 3588096 | tf_op jit(solution)/shard_map/pallas_call | solution.py:282
  12.2 0.3 collective-permute-done.1
  12.5 0.5 collective-permute-done
  13.1 3.7 %collective-permute-start.5 = (bf16[32,1536]{1,0:T(8,128)(2,1)S(1)}, bf16[32,1536]{1,0:T(8,128)(2,1)S(1)}, u32[]{:S(2)}, u32[]{:S(2)}) collective-permute-start(bf16[32,1536]{1,0:T(8,128)(2,1)S(1)} %add_add_fusion.2.refs_0_), channel_id=1, source_target_pairs={{0,24},{1,7},{2,26},{3,5},{4,28},{5,3},{6,30},{7,1},{8,16},{9,15},... | collective-permute-start | bytes 294920 | tf_op jit(solution)/shard_map/ppermute | solution.py:46
  16.7 0.8 %collective-permute-start.3 = (bf16[32,1536]{1,0:T(8,128)(2,1)S(1)}, bf16[32,1536]{1,0:T(8,128)(2,1)S(1)}, u32[]{:S(2)}, u32[]{:S(2)}) collective-permute-start(bf16[32,1536]{1,0:T(8,128)(2,1)S(1)} %add_add_fusion.2.refs_0_), channel_id=1, source_target_pairs={{0,8},{1,3},{2,10},{3,1},{4,12},{5,7},{6,14},{7,5},{8,0},{9,11},{1... | collective-permute-start | bytes 294920 | tf_op jit(solution)/shard_map/ppermute | solution.py:46
  17.5 2.1 %collective-permute-done.5.refs_3_ = bf16[32,1536]{1,0:T(8,128)(2,1)S(1)} collective-permute-done((bf16[32,1536]{1,0:T(8,128)(2,1)S(1)}, bf16[32,1536]{1,0:T(8,128)(2,1)S(1)}, u32[]{:S(2)}, u32[]{:S(2)}) %collective-permute-start.5) | collective-permute-done | bytes 98336 | tf_op jit(solution)/shard_map/ppermute | solution.py:46
  19.6 2.7 %collective-permute-done.4.refs_2_ = bf16[32,1536]{1,0:T(8,128)(2,1)S(1)} collective-permute-done((bf16[32,1536]{1,0:T(8,128)(2,1)S(1)}, bf16[32,1536]{1,0:T(8,128)(2,1)S(1)}, u32[]{:S(2)}, u32[]{:S(2)}) %collective-permute-start.4) | collective-permute-done | bytes 98336 | tf_op jit(solution)/shard_map/ppermute | solution.py:46
  22.4 0.5 shard_map.115
  22.9 2.2 %collective-permute-start.8 = (bf16[32,1536]{1,0:T(8,128)(2,1)S(1)}, bf16[32,1536]{1,0:T(8,128)(2,1)S(1)}, u32[]{:S(2)}, u32[]{:S(2)}) collective-permute-start(bf16[32,1536]{1,0:T(8,128)(2,1)S(1)} %get-tuple-element.67), channel_id=1, source_target_pairs={{0,24},{1,7},{2,26},{3,5},{4,28},{5,3},{6,30},{7,1},{8,16},{9,15},... | collective-permute-start | bytes 294920 | tf_op jit(solution)/shard_map/ppermute | solution.py:46
  25.2 0.4 collective-permute-start.7
  25.6 1.8 %collective-permute-start.6 = (bf16[32,1536]{1,0:T(8,128)(2,1)S(1)}, bf16[32,1536]{1,0:T(8,128)(2,1)S(1)}, u32[]{:S(2)}, u32[]{:S(2)}) collective-permute-start(bf16[32,1536]{1,0:T(8,128)(2,1)S(1)} %get-tuple-element.67), channel_id=1, source_target_pairs={{0,8},{1,3},{2,10},{3,1},{4,12},{5,7},{6,14},{7,5},{8,0},{9,11},{1... | collective-permute-start | bytes 294920 | tf_op jit(solution)/shard_map/ppermute | solution.py:46
  27.4 0.5 shard_map.116.own_ref
  28.0 1.3 %shard_map.117 = (bf16[200,1536]{1,0:T(8,128)(2,1)S(1)}, bf16[1536,200]{1,0:T(8,128)(2,1)S(1)}, f32[1,1536]{1,0:T(1,128)S(1)}) custom-call(s32[3]{0:T(128)S(1)} %copy-done.7, s32[1,2]{1,0:T(1,128)S(1)} %copy-done.8, bf16[2,200,1536]{2,1,0:T(8,128)(2,1)S(1)} %bitcast.15, bf16[2,200,1536]{2,1,0:T(8,128)(2,1)S(1)} %bitcast.17, bf16[1536,1536]{1,0:T(8,128)(2,1)S(1)} %bitcast.13), custom_call_target="tpu_custom_call" | custom-call | flops 471859200 | bytes 3588096 | tf_op jit(solution)/shard_map/pallas_call | solution.py:282
  29.3 0.2 collective-permute-done.8
  29.4 2.1 %collective-permute-done.7 = bf16[32,1536]{1,0:T(8,128)(2,1)S(1)} collective-permute-done((bf16[32,1536]{1,0:T(8,128)(2,1)S(1)}, bf16[32,1536]{1,0:T(8,128)(2,1)S(1)}, u32[]{:S(2)}, u32[]{:S(2)}) %collective-permute-start.7) | collective-permute-done | bytes 98336 | tf_op jit(solution)/shard_map/ppermute | solution.py:46
  31.6 2.2 %collective-permute-start.13 = (bf16[32,1536]{1,0:T(8,128)(2,1)S(1)}, bf16[32,1536]{1,0:T(8,128)(2,1)S(1)}, u32[]{:S(2)}, u32[]{:S(2)}) collective-permute-start(bf16[32,1536]{1,0:T(8,128)(2,1)S(1)} %add_add_fusion.1.refs_0_), channel_id=1, source_target_pairs={{0,6},{1,25},{2,4},{3,27},{4,2},{5,29},{6,0},{7,31},{8,14},{9,17},... | collective-permute-start | bytes 294920 | tf_op jit(solution)/shard_map/ppermute | solution.py:46
  33.7 0.5 collective-permute-start.12
  34.2 0.9 %collective-permute-start.11 = (bf16[32,1536]{1,0:T(8,128)(2,1)S(1)}, bf16[32,1536]{1,0:T(8,128)(2,1)S(1)}, u32[]{:S(2)}, u32[]{:S(2)}) collective-permute-start(bf16[32,1536]{1,0:T(8,128)(2,1)S(1)} %add_add_fusion.1.refs_0_), channel_id=1, source_target_pairs={{0,2},{1,9},{2,0},{3,11},{4,6},{5,13},{6,4},{7,15},{8,10},{9,1},{1... | collective-permute-start | bytes 294920 | tf_op jit(solution)/shard_map/ppermute | solution.py:46
  35.1 0.9 %shard_map.118.right_ref = bf16[2,3,200,768]{3,2,1,0:T(8,128)(2,1)S(1)} custom-call(s32[2,3]{1,0:T(2,128)S(1)} %copy-done.9, bf16[2,3,200,768]{3,2,1,0:T(8,128)(2,1)S(1)} %copy-done.4), custom_call_target="tpu_custom_call" | custom-call | flops 921600 | bytes 3686400 | tf_op jit(solution)/shard_map/pallas_call | solution.py:296
  36.0 0.5 shard_map.120
  36.5 0.5 copy-done.5
  37.0 0.3 shard_map.119.rhs_ref
  37.3 1.0 %collective-permute-done.12.refs_2_ = bf16[32,1536]{1,0:T(8,128)(2,1)S(1)} collective-permute-done((bf16[32,1536]{1,0:T(8,128)(2,1)S(1)}, bf16[32,1536]{1,0:T(8,128)(2,1)S(1)}, u32[]{:S(2)}, u32[]{:S(2)}) %collective-permute-start.12) | collective-permute-done | bytes 98336 | tf_op jit(solution)/shard_map/ppermute | solution.py:46
  38.3 0.5 collective-permute-done.11.refs_1_
  38.8 0.5 shard_map.121
  39.4 1.9 %collective-permute-start.16 = (bf16[32,1536]{1,0:T(8,128)(2,1)S(1)}, bf16[32,1536]{1,0:T(8,128)(2,1)S(1)}, u32[]{:S(2)}, u32[]{:S(2)}) collective-permute-start(bf16[32,1536]{1,0:T(8,128)(2,1)S(1)} %get-tuple-element.80), channel_id=1, source_target_pairs={{0,6},{1,25},{2,4},{3,27},{4,2},{5,29},{6,0},{7,31},{8,14},{9,17},... | collective-permute-start | bytes 294920 | tf_op jit(solution)/shard_map/ppermute | solution.py:46
  41.3 0.5 collective-permute-start.15
  41.8 1.1 %collective-permute-start.14 = (bf16[32,1536]{1,0:T(8,128)(2,1)S(1)}, bf16[32,1536]{1,0:T(8,128)(2,1)S(1)}, u32[]{:S(2)}, u32[]{:S(2)}) collective-permute-start(bf16[32,1536]{1,0:T(8,128)(2,1)S(1)} %get-tuple-element.80), channel_id=1, source_target_pairs={{0,2},{1,9},{2,0},{3,11},{4,6},{5,13},{6,4},{7,15},{8,10},{9,1},{1... | collective-permute-start | bytes 294920 | tf_op jit(solution)/shard_map/ppermute | solution.py:46
  42.9 0.5 shard_map.122.own_ref
  43.4 1.2 %collective-permute-done.17.other_ref = bf16[2,32,200]{2,1,0:T(8,128)(2,1)S(1)} collective-permute-done((bf16[2,32,200]{2,1,0:T(8,128)(2,1)S(1)}, bf16[2,32,200]{2,1,0:T(8,128)(2,1)S(1)}, u32[]{:S(2)}, u32[]{:S(2)}) %collective-permute-start.17) | collective-permute-done | bytes 25632 | tf_op jit(solution)/shard_map/ppermute | solution.py:56
  44.6 0.3 collective-permute-done.16
  45.0 1.0 %collective-permute-done.15 = bf16[32,1536]{1,0:T(8,128)(2,1)S(1)} collective-permute-done((bf16[32,1536]{1,0:T(8,128)(2,1)S(1)}, bf16[32,1536]{1,0:T(8,128)(2,1)S(1)}, u32[]{:S(2)}, u32[]{:S(2)}) %collective-permute-start.15) | collective-permute-done | bytes 98336 | tf_op jit(solution)/shard_map/ppermute | solution.py:46
  46.0 0.4 collective-permute-done.14
  46.4 2.2 %collective-permute-start.20 = (bf16[32,1536]{1,0:T(8,128)(2,1)S(1)}, bf16[32,1536]{1,0:T(8,128)(2,1)S(1)}, u32[]{:S(2)}, u32[]{:S(2)}) collective-permute-start(bf16[32,1536]{1,0:T(8,128)(2,1)S(1)} %add_add_fusion.refs_0_), channel_id=1, source_target_pairs={{0,24},{1,7},{2,26},{3,5},{4,28},{5,3},{6,30},{7,1},{8,16},{9,15},... | collective-permute-start | bytes 294920 | tf_op jit(solution)/shard_map/ppermute | solution.py:46
  48.7 2.2 %collective-permute-start.18 = (bf16[32,1536]{1,0:T(8,128)(2,1)S(1)}, bf16[32,1536]{1,0:T(8,128)(2,1)S(1)}, u32[]{:S(2)}, u32[]{:S(2)}) collective-permute-start(bf16[32,1536]{1,0:T(8,128)(2,1)S(1)} %add_add_fusion.refs_0_), channel_id=1, source_target_pairs={{0,8},{1,3},{2,10},{3,1},{4,12},{5,7},{6,14},{7,5},{8,0},{9,11},{1... | collective-permute-start | bytes 294920 | tf_op jit(solution)/shard_map/ppermute | solution.py:46
  50.9 0.3 shard_map.123.rhs_ref
  51.2 1.7 %collective-permute-done.20.refs_3_ = bf16[32,1536]{1,0:T(8,128)(2,1)S(1)} collective-permute-done((bf16[32,1536]{1,0:T(8,128)(2,1)S(1)}, bf16[32,1536]{1,0:T(8,128)(2,1)S(1)}, u32[]{:S(2)}, u32[]{:S(2)}) %collective-permute-start.20) | collective-permute-done | bytes 98336 | tf_op jit(solution)/shard_map/ppermute | solution.py:46
  53.0 2.1 %collective-permute-done.19.refs_2_ = bf16[32,1536]{1,0:T(8,128)(2,1)S(1)} collective-permute-done((bf16[32,1536]{1,0:T(8,128)(2,1)S(1)}, bf16[32,1536]{1,0:T(8,128)(2,1)S(1)}, u32[]{:S(2)}, u32[]{:S(2)}) %collective-permute-start.19) | collective-permute-done | bytes 98336 | tf_op jit(solution)/shard_map/ppermute | solution.py:46
  55.0 0.4 shard_map.124
  55.4 1.0 %shard_map.125 = (f32[2,64,768]{2,1,0:T(8,128)}, bf16[3,32,1536]{2,1,0:T(8,128)(2,1)}) custom-call(bf16[2,32,200]{2,1,0:T(8,128)(2,1)S(1)} %get-tuple-element.88.weights_ref, bf16[2,3,200,768]{3,2,1,0:T(8,128)(2,1)S(1)} %shard_map.118.right_ref, f32[2,64,768]{2,1,0:T(8,128)S(1)} %shard_map.123.rhs_ref, bf16[32,1536]{1,0:T(8,128)(2,1)S(1)} %get-tuple-element.89.refs_0_, ...), custom_call_target="tpu_custom_call" | custom-call | flops 19660800 | bytes 393216 | tf_op jit(solution)/shard_map/pallas_call | solution.py:389
  56.4 0.2 collective-permute-done.21.weights_ref
  56.6 0.9 %shard_map.126 = f32[2,64,768]{2,1,0:T(8,128)} custom-call(bf16[2,32,200]{2,1,0:T(8,128)(2,1)S(1)} %collective-permute-done.21.weights_ref, bf16[2,3,200,768]{3,2,1,0:T(8,128)(2,1)S(1)} %shard_map.118.right_ref, f32[2,64,768]{2,1,0:T(8,128)S(1)} %shard_map.123.rhs_ref, f32[2,64,768]{2,1,0:T(8,128)} %get-tuple-element.91.held_ref), custom_call_target="tpu_custom_call", output_to_operand_aliasing={{}: (3, {})} | custom-call | flops 19660800 | bytes 393216 | tf_op jit(solution)/shard_map/pallas_call | solution.py:401
  (35 shorter events, 0.4 us)
Async XLA Ops:
  0.6 7.7 %copy-start = (bf16[1,1536,1536]{2,1,0:T(8,128)(2,1)S(1)}, bf16[1,1536,1536]{2,1,0:T(8,128)(2,1)}, u32[]{:S(2)}) copy-start(bf16[1,1536,1536]{2,1,0:T(8,128)(2,1)} %param.11) | copy-start | bytes 14155780
  0.6 7.7 %copy-start.7 = (s32[3]{0:T(128)S(1)}, s32[3]{0:T(128)}, u32[]{:S(2)}) copy-start(s32[3]{0:T(128)} %owner_ref.5) | copy-start | bytes 40
  0.7 7.7 %copy-start.8 = (s32[1,2]{1,0:T(1,128)S(1)}, s32[1,2]{1,0:T(1,128)}, u32[]{:S(2)}) copy-start(s32[1,2]{1,0:T(1,128)} %ranks_ref.4) | copy-start | bytes 28
  3.6 23.7 %collective-permute-start.9 = (bf16[2,3,200,768]{3,2,1,0:T(8,128)(2,1)}, bf16[2,3,200,768]{3,2,1,0:T(8,128)(2,1)S(1)}, u32[]{:S(2)}, u32[]{:S(2)}) collective-permute-start(bf16[2,3,200,768]{3,2,1,0:T(8,128)(2,1)} %own_ref.2), channel_id=1, source_target_pairs={{0,1},{1,0},{2,3},{3,2},{4,5},{5,4},{6,7},{7,6},{8,9},{9,8},{10,11... | collective-permute-start | bytes 5529608 | tf_op jit(solution)/shard_map/ppermute | solution.py:56
  4.2 8.1 %collective-permute-start.2 = (bf16[32,1536]{1,0:T(8,128)(2,1)}, bf16[32,1536]{1,0:T(8,128)(2,1)S(1)}, u32[]{:S(2)}, u32[]{:S(2)}) collective-permute-start(bf16[32,1536]{1,0:T(8,128)(2,1)} %get-tuple-element.52), channel_id=1, source_target_pairs={{0,6},{1,25},{2,4},{3,27},{4,2},{5,29},{6,0},{7,31},{8,14},{9,17},... | collective-permute-start | bytes 294920 | tf_op jit(solution)/shard_map/ppermute | solution.py:46
  7.7 4.8 %collective-permute-start.1 = (bf16[32,1536]{1,0:T(8,128)(2,1)}, bf16[32,1536]{1,0:T(8,128)(2,1)S(1)}, u32[]{:S(2)}, u32[]{:S(2)}) collective-permute-start(bf16[32,1536]{1,0:T(8,128)(2,1)} %get-tuple-element.52), channel_id=1, source_target_pairs={{0,4},{1,17},{2,6},{3,19},{4,0},{5,21},{6,2},{7,23},{8,12},{9,25},... | collective-permute-start | bytes 294920 | tf_op jit(solution)/shard_map/ppermute | solution.py:46
  8.2 4.8 %collective-permute-start = (bf16[32,1536]{1,0:T(8,128)(2,1)}, bf16[32,1536]{1,0:T(8,128)(2,1)S(1)}, u32[]{:S(2)}, u32[]{:S(2)}) collective-permute-start(bf16[32,1536]{1,0:T(8,128)(2,1)} %get-tuple-element.52), channel_id=1, source_target_pairs={{0,2},{1,9},{2,0},{3,11},{4,6},{5,13},{6,4},{7,15},{8,10},{9,1},{1... | collective-permute-start | bytes 294920 | tf_op jit(solution)/shard_map/ppermute | solution.py:46
  8.3 1.3 %copy-start.2 = (bf16[1,2,1536,200]{2,3,1,0:T(8,128)(2,1)S(1)}, bf16[1,2,1536,200]{2,3,1,0:T(8,128)(2,1)}, u32[]{:S(2)}) copy-start(bf16[1,2,1536,200]{2,3,1,0:T(8,128)(2,1)} %param.14) | copy-start | bytes 3686404
  9.6 1.3 %copy-start.3 = (bf16[1,2,1536,200]{2,3,1,0:T(8,128)(2,1)S(1)}, bf16[1,2,1536,200]{2,3,1,0:T(8,128)(2,1)}, u32[]{:S(2)}) copy-start(bf16[1,2,1536,200]{2,3,1,0:T(8,128)(2,1)} %param.13) | copy-start | bytes 3686404
  10.9 2.1 %copy-start.10 = (bf16[32,1536]{1,0:T(8,128)(2,1)S(1)}, bf16[32,1536]{1,0:T(8,128)(2,1)}, u32[]{:S(2)}) copy-start(bf16[32,1536]{1,0:T(8,128)(2,1)} %get-tuple-element.52) | copy-start | bytes 294916
  10.9 11.5 %copy-start.6 = (f32[32,1536]{1,0:T(8,128)S(1)}, f32[32,1536]{1,0:T(8,128)}, u32[]{:S(2)}) copy-start(f32[32,1536]{1,0:T(8,128)} %get-tuple-element.60.refs_7_) | copy-start | bytes 589828
  12.2 15.2 %copy-start.1 = (bf16[2,3,200,768]{3,2,1,0:T(8,128)(2,1)S(1)}, bf16[2,3,200,768]{3,2,1,0:T(8,128)(2,1)}, u32[]{:S(2)}) copy-start(bf16[2,3,200,768]{3,2,1,0:T(8,128)(2,1)} %own_ref.2) | copy-start | bytes 5529604
  13.1 6.6 %collective-permute-start.5 = (bf16[32,1536]{1,0:T(8,128)(2,1)S(1)}, bf16[32,1536]{1,0:T(8,128)(2,1)S(1)}, u32[]{:S(2)}, u32[]{:S(2)}) collective-permute-start(bf16[32,1536]{1,0:T(8,128)(2,1)S(1)} %add_add_fusion.2.refs_0_), channel_id=1, source_target_pairs={{0,24},{1,7},{2,26},{3,5},{4,28},{5,3},{6,30},{7,1},{8,16},{9,15},... | collective-permute-start | bytes 294920 | tf_op jit(solution)/shard_map/ppermute | solution.py:46
  16.7 5.7 %collective-permute-start.4 = (bf16[32,1536]{1,0:T(8,128)(2,1)S(1)}, bf16[32,1536]{1,0:T(8,128)(2,1)S(1)}, u32[]{:S(2)}, u32[]{:S(2)}) collective-permute-start(bf16[32,1536]{1,0:T(8,128)(2,1)S(1)} %add_add_fusion.2.refs_0_), channel_id=1, source_target_pairs={{0,16},{1,5},{2,18},{3,7},{4,20},{5,1},{6,22},{7,3},{8,24},{9,13},... | collective-permute-start | bytes 294920 | tf_op jit(solution)/shard_map/ppermute | solution.py:46
  16.7 5.7 %collective-permute-start.3 = (bf16[32,1536]{1,0:T(8,128)(2,1)S(1)}, bf16[32,1536]{1,0:T(8,128)(2,1)S(1)}, u32[]{:S(2)}, u32[]{:S(2)}) collective-permute-start(bf16[32,1536]{1,0:T(8,128)(2,1)S(1)} %add_add_fusion.2.refs_0_), channel_id=1, source_target_pairs={{0,8},{1,3},{2,10},{3,1},{4,12},{5,7},{6,14},{7,5},{8,0},{9,11},{1... | collective-permute-start | bytes 294920 | tf_op jit(solution)/shard_map/ppermute | solution.py:46
  22.9 6.5 %collective-permute-start.8 = (bf16[32,1536]{1,0:T(8,128)(2,1)S(1)}, bf16[32,1536]{1,0:T(8,128)(2,1)S(1)}, u32[]{:S(2)}, u32[]{:S(2)}) collective-permute-start(bf16[32,1536]{1,0:T(8,128)(2,1)S(1)} %get-tuple-element.67), channel_id=1, source_target_pairs={{0,24},{1,7},{2,26},{3,5},{4,28},{5,3},{6,30},{7,1},{8,16},{9,15},... | collective-permute-start | bytes 294920 | tf_op jit(solution)/shard_map/ppermute | solution.py:46
  25.2 6.3 %collective-permute-start.7 = (bf16[32,1536]{1,0:T(8,128)(2,1)S(1)}, bf16[32,1536]{1,0:T(8,128)(2,1)S(1)}, u32[]{:S(2)}, u32[]{:S(2)}) collective-permute-start(bf16[32,1536]{1,0:T(8,128)(2,1)S(1)} %get-tuple-element.67), channel_id=1, source_target_pairs={{0,16},{1,5},{2,18},{3,7},{4,20},{5,1},{6,22},{7,3},{8,24},{9,13},... | collective-permute-start | bytes 294920 | tf_op jit(solution)/shard_map/ppermute | solution.py:46
  25.6 6.0 %collective-permute-start.6 = (bf16[32,1536]{1,0:T(8,128)(2,1)S(1)}, bf16[32,1536]{1,0:T(8,128)(2,1)S(1)}, u32[]{:S(2)}, u32[]{:S(2)}) collective-permute-start(bf16[32,1536]{1,0:T(8,128)(2,1)S(1)} %get-tuple-element.67), channel_id=1, source_target_pairs={{0,8},{1,3},{2,10},{3,1},{4,12},{5,7},{6,14},{7,5},{8,0},{9,11},{1... | collective-permute-start | bytes 294920 | tf_op jit(solution)/shard_map/ppermute | solution.py:46
  27.9 7.2 %copy-start.4 = (bf16[2,3,200,768]{3,2,1,0:T(8,128)(2,1)S(1)}, bf16[2,3,200,768]{3,2,1,0:T(8,128)(2,1)}, u32[]{:S(2)}) copy-start(bf16[2,3,200,768]{3,2,1,0:T(8,128)(2,1)} %right_ref.1) | copy-start | bytes 5529604
  27.9 7.2 %copy-start.9 = (s32[2,3]{1,0:T(2,128)S(1)}, s32[2,3]{1,0:T(2,128)}, u32[]{:S(2)}) copy-start(s32[2,3]{1,0:T(2,128)} %ranks_ref.5) | copy-start | bytes 76
  27.9 3.6 %collective-permute-start.10 = (bf16[2,32,200]{2,1,0:T(8,128)(2,1)S(1)}, bf16[2,32,200]{2,1,0:T(8,128)(2,1)S(1)}, u32[]{:S(2)}, u32[]{:S(2)}) collective-permute-start(bf16[2,32,200]{2,1,0:T(8,128)(2,1)S(1)} %shard_map.116.own_ref), channel_id=1, source_target_pairs={{0,1},{1,0},{2,3},{3,2},{4,5},{5,4},{6,7},{7,6},{8,9},{9,8},{10,11... | collective-permute-start | bytes 76808 | tf_op jit(solution)/shard_map/ppermute | solution.py:56
  31.6 5.8 %collective-permute-start.13 = (bf16[32,1536]{1,0:T(8,128)(2,1)S(1)}, bf16[32,1536]{1,0:T(8,128)(2,1)S(1)}, u32[]{:S(2)}, u32[]{:S(2)}) collective-permute-start(bf16[32,1536]{1,0:T(8,128)(2,1)S(1)} %add_add_fusion.1.refs_0_), channel_id=1, source_target_pairs={{0,6},{1,25},{2,4},{3,27},{4,2},{5,29},{6,0},{7,31},{8,14},{9,17},... | collective-permute-start | bytes 294920 | tf_op jit(solution)/shard_map/ppermute | solution.py:46
  33.7 4.6 %collective-permute-start.12 = (bf16[32,1536]{1,0:T(8,128)(2,1)S(1)}, bf16[32,1536]{1,0:T(8,128)(2,1)S(1)}, u32[]{:S(2)}, u32[]{:S(2)}) collective-permute-start(bf16[32,1536]{1,0:T(8,128)(2,1)S(1)} %add_add_fusion.1.refs_0_), channel_id=1, source_target_pairs={{0,4},{1,17},{2,6},{3,19},{4,0},{5,21},{6,2},{7,23},{8,12},{9,25},... | collective-permute-start | bytes 294920 | tf_op jit(solution)/shard_map/ppermute | solution.py:46
  34.2 4.6 %collective-permute-start.11 = (bf16[32,1536]{1,0:T(8,128)(2,1)S(1)}, bf16[32,1536]{1,0:T(8,128)(2,1)S(1)}, u32[]{:S(2)}, u32[]{:S(2)}) collective-permute-start(bf16[32,1536]{1,0:T(8,128)(2,1)S(1)} %add_add_fusion.1.refs_0_), channel_id=1, source_target_pairs={{0,2},{1,9},{2,0},{3,11},{4,6},{5,13},{6,4},{7,15},{8,10},{9,1},{1... | collective-permute-start | bytes 294920 | tf_op jit(solution)/shard_map/ppermute | solution.py:46
  36.0 1.0 %copy-start.5 = (f32[2,64,768]{2,1,0:T(8,128)S(1)}, f32[2,64,768]{2,1,0:T(8,128)}, u32[]{:S(2)}) copy-start(f32[2,64,768]{2,1,0:T(8,128)} %rhs_ref.1) | copy-start | bytes 1179652
  39.4 5.6 %collective-permute-start.16 = (bf16[32,1536]{1,0:T(8,128)(2,1)S(1)}, bf16[32,1536]{1,0:T(8,128)(2,1)S(1)}, u32[]{:S(2)}, u32[]{:S(2)}) collective-permute-start(bf16[32,1536]{1,0:T(8,128)(2,1)S(1)} %get-tuple-element.80), channel_id=1, source_target_pairs={{0,6},{1,25},{2,4},{3,27},{4,2},{5,29},{6,0},{7,31},{8,14},{9,17},... | collective-permute-start | bytes 294920 | tf_op jit(solution)/shard_map/ppermute | solution.py:46
  41.3 4.7 %collective-permute-start.15 = (bf16[32,1536]{1,0:T(8,128)(2,1)S(1)}, bf16[32,1536]{1,0:T(8,128)(2,1)S(1)}, u32[]{:S(2)}, u32[]{:S(2)}) collective-permute-start(bf16[32,1536]{1,0:T(8,128)(2,1)S(1)} %get-tuple-element.80), channel_id=1, source_target_pairs={{0,4},{1,17},{2,6},{3,19},{4,0},{5,21},{6,2},{7,23},{8,12},{9,25},... | collective-permute-start | bytes 294920 | tf_op jit(solution)/shard_map/ppermute | solution.py:46
  41.8 4.6 %collective-permute-start.14 = (bf16[32,1536]{1,0:T(8,128)(2,1)S(1)}, bf16[32,1536]{1,0:T(8,128)(2,1)S(1)}, u32[]{:S(2)}, u32[]{:S(2)}) collective-permute-start(bf16[32,1536]{1,0:T(8,128)(2,1)S(1)} %get-tuple-element.80), channel_id=1, source_target_pairs={{0,2},{1,9},{2,0},{3,11},{4,6},{5,13},{6,4},{7,15},{8,10},{9,1},{1... | collective-permute-start | bytes 294920 | tf_op jit(solution)/shard_map/ppermute | solution.py:46
  43.4 1.2 %collective-permute-start.17 = (bf16[2,32,200]{2,1,0:T(8,128)(2,1)S(1)}, bf16[2,32,200]{2,1,0:T(8,128)(2,1)S(1)}, u32[]{:S(2)}, u32[]{:S(2)}) collective-permute-start(bf16[2,32,200]{2,1,0:T(8,128)(2,1)S(1)} %shard_map.122.own_ref), channel_id=1, source_target_pairs={{0,1},{1,0},{2,3},{3,2},{4,5},{5,4},{6,7},{7,6},{8,9},{9,8},{10,11... | collective-permute-start | bytes 76808 | tf_op jit(solution)/shard_map/ppermute | solution.py:56
  46.4 6.5 %collective-permute-start.20 = (bf16[32,1536]{1,0:T(8,128)(2,1)S(1)}, bf16[32,1536]{1,0:T(8,128)(2,1)S(1)}, u32[]{:S(2)}, u32[]{:S(2)}) collective-permute-start(bf16[32,1536]{1,0:T(8,128)(2,1)S(1)} %add_add_fusion.refs_0_), channel_id=1, source_target_pairs={{0,24},{1,7},{2,26},{3,5},{4,28},{5,3},{6,30},{7,1},{8,16},{9,15},... | collective-permute-start | bytes 294920 | tf_op jit(solution)/shard_map/ppermute | solution.py:46
  48.7 6.3 %collective-permute-start.19 = (bf16[32,1536]{1,0:T(8,128)(2,1)S(1)}, bf16[32,1536]{1,0:T(8,128)(2,1)S(1)}, u32[]{:S(2)}, u32[]{:S(2)}) collective-permute-start(bf16[32,1536]{1,0:T(8,128)(2,1)S(1)} %add_add_fusion.refs_0_), channel_id=1, source_target_pairs={{0,16},{1,5},{2,18},{3,7},{4,20},{5,1},{6,22},{7,3},{8,24},{9,13},... | collective-permute-start | bytes 294920 | tf_op jit(solution)/shard_map/ppermute | solution.py:46
  48.7 6.3 %collective-permute-start.18 = (bf16[32,1536]{1,0:T(8,128)(2,1)S(1)}, bf16[32,1536]{1,0:T(8,128)(2,1)S(1)}, u32[]{:S(2)}, u32[]{:S(2)}) collective-permute-start(bf16[32,1536]{1,0:T(8,128)(2,1)S(1)} %add_add_fusion.refs_0_), channel_id=1, source_target_pairs={{0,8},{1,3},{2,10},{3,1},{4,12},{5,7},{6,14},{7,5},{8,0},{9,11},{1... | collective-permute-start | bytes 294920 | tf_op jit(solution)/shard_map/ppermute | solution.py:46
  55.4 1.2 %collective-permute-start.21 = (bf16[2,32,200]{2,1,0:T(8,128)(2,1)S(1)}, bf16[2,32,200]{2,1,0:T(8,128)(2,1)S(1)}, u32[]{:S(2)}, u32[]{:S(2)}) collective-permute-start(bf16[2,32,200]{2,1,0:T(8,128)(2,1)S(1)} %get-tuple-element.88.weights_ref), channel_id=1, source_target_pairs={{0,1},{1,0},{2,3},{3,2},{4,5},{5,4},{6,7},{7,6},{8,9},{9,8},{10,11... | collective-permute-start | bytes 76808 | tf_op jit(solution)/shard_map/ppermute | solution.py:56
